TPU v7x, 32 devices: a whole 2x2x4 slice. The times are simulated.
32 devices in a mesh: head: 2 (over y), batch: 16 (over z, x, core).
Axes of the slice: x: 2, y: 2, z: 4, core: 2. Of those that a mesh axis runs over, the one named last changes fastest.
Arguments:
- short_rows: bfloat16 [32, 512, 1024], P('batch', 'head'), may hold values from -6 to 6
- medium_rows: bfloat16 [16, 1024, 1024], P('batch', 'head'), may hold values from -6 to 6
- long_rows: bfloat16 [16, 2048, 1024], P('batch', 'head'), may hold values from -6 to 6
- short_len: int32 [32], P('batch'), may hold values from 256 to 512, as said below
- medium_len: int32 [16], P('batch'), may hold values from 512 to 1024, as said below
- long_len: int32 [16], P('batch'), may hold values from 1024 to 2048, as said below
- short_cotangent: bfloat16 [32, 512, 1024], P('batch', 'head'), may hold values from -6 to 6
- medium_cotangent: bfloat16 [16, 1024, 1024], P('batch', 'head'), may hold values from -6 to 6
- long_cotangent: bfloat16 [16, 2048, 1024], P('batch', 'head'), may hold values from -6 to 6
- norm_gains: float32 [3, 1024], replicated, may hold values from 0.1 to 1.9
- norm_shifts: float32 [5, 1024], replicated, may hold values from -3 to 3
- head_weights: bfloat16 [3, 1024, 1024], P(None, None, 'head'), may hold values from -0.1875 to 0.1875
- head_biases: float32 [2, 1024], P(None, 'head'), may hold values from -3 to 3
- head_scale: float32 [16], P('head'), may hold values from 0.1 to 1.9
- out_weight: bfloat16 [1024, 1024], P('head'), may hold values from -0.75 to 0.75
- up_weight: bfloat16 [4096, 1024], P(('head', 'batch')), may hold values from -0.1875 to 0.1875
- mid_gain: float32 [4096], replicated, may hold values from 0.1 to 1.9
- mid_shifts: float32 [2, 4096], replicated, may hold values from -3 to 3
- down_weight: bfloat16 [4096, 1024], P(('head', 'batch')), may hold values from -0.09375 to 0.09375
Outputs:
- short_out: bfloat16 [32, 512, 1024], P('batch', 'head')
- medium_out: bfloat16 [16, 1024, 1024], P('batch', 'head')
- long_out: bfloat16 [16, 2048, 1024], P('batch', 'head')
- short_grad: bfloat16 [32, 512, 1024], P('batch', 'head')
- medium_grad: bfloat16 [16, 1024, 1024], P('batch', 'head')
- long_grad: bfloat16 [16, 2048, 1024], P('batch', 'head')
- grad_norm_gains: float32 [3, 1024], replicated
- grad_norm_shifts: float32 [5, 1024], replicated
- grad_head_weights: float32 [3, 1024, 1024], P(None, None, 'head')
- grad_head_biases: float32 [2, 1024], P(None, 'head')
- grad_head_scale: float32 [16], P('head')
- grad_out_weight: float32 [1024, 1024], P('head')
- grad_up_weight: float32 [4096, 1024], P(('head', 'batch'))
- grad_mid_gain: float32 [4096], replicated
- grad_mid_shifts: float32 [2, 4096], replicated
- grad_down_weight: float32 [4096, 1024], P(('head', 'batch'))
Inputs may be any that keep to these rules, and one draw needn't show every extreme that they name: `short_len`: lengths of the rows of the first tensor; in each of the 16 groups of rows of one index of batch, at least one row of the three tensors together is used to its full length. `medium_len`: lengths of the rows of the second tensor, drawn as the first. `long_len`: lengths of the rows of the third tensor, drawn as the first.
All inputs are finite; a program needn't handle non-finite values.
Results may differ from a plain program's by a relative error of at most 0.02.
Values may be sent and summed in bfloat16 or wider, within the bound.
A program may use at most 384 MiB of HBM per device.

v0:
```python
import jax
import jax.numpy as jnp
from jax import lax
from jax.sharding import PartitionSpec as P

EPSILON = 1e-05
ROW_PAIRS = (((0,), (0,)), ((), ()))
COLUMN_PAIRS = (((1,), (1,)), ((), ()))


def normalize(value, gain, shift):
    centred = value - jnp.mean(value, axis=-1, keepdims=True)
    inverse = lax.rsqrt(jnp.mean(centred * centred, axis=-1, keepdims=True) + EPSILON)
    unit = centred * inverse
    return (unit * gain + shift, unit, inverse)


def normalize_back(grad, unit, inverse, gain):
    scaled = grad * gain
    inner = (
        scaled
        - jnp.mean(scaled, axis=-1, keepdims=True)
        - unit * jnp.mean(scaled * unit, axis=-1, keepdims=True)
    )
    return (inner * inverse, jnp.sum(grad * unit, axis=0), jnp.sum(grad, axis=0))


def split_rows(merged, shapes):
    pieces = []
    offset = 0
    for shape in shapes:
        number = shape[0] * shape[1]
        pieces.append(merged[offset : offset + number].reshape(shape))
        offset += number
    return tuple(pieces)


def join_rows(arrays, width):
    return jnp.concatenate([item.reshape(-1, width) for item in arrays], 0)


def block_scores(query_block, key_row, start, length):
    block, heads, width = query_block.shape
    span = key_row.shape[0]
    scores = jnp.einsum(
        "qhd,khd->hqk", query_block, key_row, preferred_element_type=jnp.float32
    ) * width ** (-0.5)
    query_place = start + lax.broadcasted_iota(jnp.int32, (block, span), 0)
    key_place = lax.broadcasted_iota(jnp.int32, (block, span), 1)
    allowed = (key_place <= query_place) & (key_place < length)
    return jnp.where(allowed[None], scores, -1e30)


def attend_forward(query, keys, values, lengths):
    rows, span, heads, width = query.shape
    block = min(512, span)
    count = span // block
    blocks = query.reshape(rows * count, block, heads, width)

    def attend_one_block(item):
        query_block, index = item
        row = index // count
        scores = block_scores(query_block, keys[row], index % count * block, lengths[row])
        top = jnp.max(scores, axis=-1, keepdims=True)
        weights = jnp.exp(scores - top)
        total = jnp.sum(weights, axis=-1, keepdims=True)
        shares = (weights / total).astype(jnp.bfloat16)
        mixed = jnp.einsum("hqk,khd->qhd", shares, values[row], preferred_element_type=jnp.float32)
        return (mixed, (top + jnp.log(total))[..., 0])

    mixed, log_total = lax.map(
        attend_one_block, (blocks, jnp.arange(rows * count, dtype=jnp.int32))
    )
    return (mixed.reshape(rows, span, heads, width), log_total.reshape(rows, count, heads, block))


def attend_backward(query, keys, values, lengths, log_total, mixed_grad):
    rows, span, heads, width = query.shape
    count = log_total.shape[1]
    block = span // count
    scale = width ** (-0.5)

    def one_row(item):
        query_row, key_row, value_row, grad_row, total_row, length = item

        def one_one_block(carry, index):
            key_grad, value_grad = carry
            start = index * block
            query_block = lax.dynamic_slice_in_dim(query_row, start, block, 0)
            grad_block = lax.dynamic_slice_in_dim(grad_row, start, block, 0)
            scores = block_scores(query_block, key_row, start, length)
            shares = jnp.exp(scores - total_row[index][..., None])
            value_grad = value_grad + jnp.einsum(
                "hqk,qhd->khd",
                shares.astype(jnp.bfloat16),
                grad_block,
                preferred_element_type=jnp.float32,
            )
            share_grad = jnp.einsum(
                "qhd,khd->hqk", grad_block, value_row, preferred_element_type=jnp.float32
            )
            inner = jnp.sum(shares * share_grad, axis=-1, keepdims=True)
            score_grad = (shares * (share_grad - inner)).astype(jnp.bfloat16)
            query_grad = (
                jnp.einsum("hqk,khd->qhd", score_grad, key_row, preferred_element_type=jnp.float32)
                * scale
            )
            key_grad = (
                key_grad
                + jnp.einsum(
                    "hqk,qhd->khd", score_grad, query_block, preferred_element_type=jnp.float32
                )
                * scale
            )
            return ((key_grad, value_grad), query_grad.astype(jnp.bfloat16))

        empty = jnp.zeros((span, heads, width), jnp.float32)
        (key_grad, value_grad), query_grad = lax.scan(
            one_one_block, (empty, empty), jnp.arange(count, dtype=jnp.int32)
        )
        return (
            query_grad.reshape(span, heads, width),
            key_grad.astype(jnp.bfloat16),
            value_grad.astype(jnp.bfloat16),
        )

    return lax.map(one_row, (query, keys, values, mixed_grad, log_total, lengths))


def project_forward(gathered, lengths, head_weights, head_biases, head_scale):
    rows, span, width = gathered.shape
    flat_rows = gathered.reshape(rows * span, width)
    part = head_weights.shape[2]
    heads = head_scale.shape[0]
    shape = (rows, span, heads, part // heads)
    query = (
        (jnp.dot(flat_rows, head_weights[0], preferred_element_type=jnp.float32) + head_biases[0])
        .astype(jnp.bfloat16)
        .reshape(shape)
    )
    keys = (
        jnp.dot(flat_rows, head_weights[1], preferred_element_type=jnp.float32)
        .astype(jnp.bfloat16)
        .reshape(shape)
    )
    values = (
        (jnp.dot(flat_rows, head_weights[2], preferred_element_type=jnp.float32) + head_biases[1])
        .astype(jnp.bfloat16)
        .reshape(shape)
    )
    mixed, log_total = attend_forward(query, keys, values, lengths)
    scaled = (mixed * head_scale[:, None]).astype(jnp.bfloat16).reshape(rows * span, part)
    return (query, keys, values, mixed, log_total, scaled)


def project_backward(gathered, lengths, stored, grad_rows, head_weights, head_scale, out_weight):
    query, keys, values, mixed, log_total, scaled = stored
    rows, span, width = gathered.shape
    part = head_weights.shape[2]
    flat_grad = grad_rows.reshape(rows * span, width)
    out_grad = lax.dot_general(scaled, flat_grad, ROW_PAIRS, preferred_element_type=jnp.float32)
    scaled_grad = lax.dot_general(
        flat_grad, out_weight, COLUMN_PAIRS, preferred_element_type=jnp.float32
    ).reshape(mixed.shape)
    scale_grad = jnp.sum(scaled_grad * mixed, axis=(0, 1, 3))
    mixed_grad = (scaled_grad * head_scale[:, None]).astype(jnp.bfloat16)
    query_grad, key_grad, value_grad = attend_backward(
        query, keys, values, lengths, log_total, mixed_grad
    )
    pieces = [item.reshape(rows * span, part) for item in (query_grad, key_grad, value_grad)]
    flat_rows = gathered.reshape(rows * span, width)
    weight_grad = jnp.stack(
        [
            lax.dot_general(flat_rows, item, ROW_PAIRS, preferred_element_type=jnp.float32)
            for item in pieces
        ]
    )
    bias_grad = jnp.stack(
        [
            jnp.sum(pieces[0].astype(jnp.float32), axis=0),
            jnp.sum(pieces[2].astype(jnp.float32), axis=0),
        ]
    )
    normed_grad = lax.dot_general(
        pieces[0], head_weights[0], COLUMN_PAIRS, preferred_element_type=jnp.float32
    )
    normed_grad = normed_grad + lax.dot_general(
        pieces[1], head_weights[1], COLUMN_PAIRS, preferred_element_type=jnp.float32
    )
    normed_grad = normed_grad + lax.dot_general(
        pieces[2], head_weights[2], COLUMN_PAIRS, preferred_element_type=jnp.float32
    )
    return (weight_grad, bias_grad, scale_grad, out_grad, normed_grad.reshape(rows, span, width))


def shards(
    short_rows,
    medium_rows,
    long_rows,
    short_len,
    medium_len,
    long_len,
    short_cotangent,
    medium_cotangent,
    long_cotangent,
    norm_gains,
    norm_shifts,
    head_weights,
    head_biases,
    head_scale,
    out_weight,
    up_weight,
    mid_gain,
    mid_shifts,
    down_weight,
):
    inputs = (short_rows, medium_rows, long_rows)
    lengths = (short_len, medium_len, long_len)
    shapes = tuple((item.shape for item in inputs))
    width = short_rows.shape[2]
    merged = join_rows(inputs, width).astype(jnp.float32)
    normed, first_unit, first_inverse = normalize(merged, norm_gains[0], norm_shifts[0])
    normed_low = split_rows(normed.astype(jnp.bfloat16), shapes)
    gathered = (
        lax.all_gather(normed_low[0], "head", axis=1, tiled=True),
        lax.all_gather(normed_low[1], "head", axis=1, tiled=True),
        lax.all_gather(normed_low[2], "head", axis=1, tiled=True),
    )
    saved = [
        project_forward(rows_all, length, head_weights, head_biases, head_scale)
        for rows_all, length in zip(gathered, lengths)
    ]
    partials = [
        jnp.dot(stored[5], out_weight, preferred_element_type=jnp.float32)
        .astype(jnp.bfloat16)
        .astype(jnp.float32)
        .reshape(rows_all.shape)
        for stored, rows_all in zip(saved, gathered)
    ]
    summed = (
        lax.psum_scatter(
            partials[0].astype(jnp.bfloat16), "head", scatter_dimension=1, tiled=True
        ).astype(jnp.float32),
        lax.psum_scatter(
            partials[1].astype(jnp.bfloat16), "head", scatter_dimension=1, tiled=True
        ).astype(jnp.float32),
        lax.psum_scatter(
            partials[2].astype(jnp.bfloat16), "head", scatter_dimension=1, tiled=True
        ).astype(jnp.float32),
    )
    attended = join_rows(summed, width) + norm_shifts[3]
    post, post_unit, post_inverse = normalize(attended, norm_gains[1], norm_shifts[1])
    residual = merged + post
    dense_pre, dense_unit, dense_inverse = normalize(residual, norm_gains[2], norm_shifts[2])
    dense_in = dense_pre.astype(jnp.bfloat16)
    cotangent = join_rows((short_cotangent, medium_cotangent, long_cotangent), width)
    cot_wide = cotangent.astype(jnp.float32)
    whole_up, whole_down = (
        lax.all_gather(up_weight, ("head", "batch"), axis=0, tiled=True),
        lax.all_gather(down_weight, ("head", "batch"), axis=0, tiled=True),
    )
    hidden = (
        lax.dot_general(dense_in, whole_up, COLUMN_PAIRS, preferred_element_type=jnp.float32)
        + mid_shifts[0]
    )
    activated, gelu_back = jax.vjp(jax.nn.gelu, hidden)
    middle, mid_unit, mid_inverse = normalize(activated, mid_gain, mid_shifts[1])
    middle_low = middle.astype(jnp.bfloat16)
    branch = jnp.dot(middle_low, whole_down, preferred_element_type=jnp.float32)
    middle_grad = lax.dot_general(
        cotangent, whole_down, COLUMN_PAIRS, preferred_element_type=jnp.float32
    )
    active_grad, mid_gain_grad, mid_shift_grad = normalize_back(
        middle_grad, mid_unit, mid_inverse, mid_gain
    )
    hidden_grad = gelu_back(active_grad)[0].astype(jnp.bfloat16)
    dense_grad = jnp.dot(hidden_grad, whole_up, preferred_element_type=jnp.float32)
    down_piece = lax.dot_general(
        middle_low, cotangent, ROW_PAIRS, preferred_element_type=jnp.float32
    )
    up_piece = lax.dot_general(hidden_grad, dense_in, ROW_PAIRS, preferred_element_type=jnp.float32)
    both_grads = lax.psum_scatter(
        jnp.concatenate([down_piece, up_piece], 1),
        ("head", "batch"),
        scatter_dimension=0,
        tiled=True,
    )
    mid_terms = jnp.stack([jnp.sum(hidden_grad.astype(jnp.float32), axis=0), mid_shift_grad])
    outputs = split_rows((residual + branch + norm_shifts[4]).astype(jnp.bfloat16), shapes)
    grad_down_weight = both_grads[:, :width]
    grad_up_weight = both_grads[:, width:]
    residual_part, third_gain, third_shift = normalize_back(
        dense_grad, dense_unit, dense_inverse, norm_gains[2]
    )
    residual_grad = cot_wide + residual_part
    attended_grad, second_gain, second_shift = normalize_back(
        residual_grad, post_unit, post_inverse, norm_gains[1]
    )
    out_bias_grad = jnp.sum(attended_grad, axis=0)
    grad_low = split_rows(attended_grad.astype(jnp.bfloat16), shapes)
    grad_rows = (
        lax.all_gather(grad_low[0], "head", axis=1, tiled=True),
        lax.all_gather(grad_low[1], "head", axis=1, tiled=True),
        lax.all_gather(grad_low[2], "head", axis=1, tiled=True),
    )
    results = [
        project_backward(rows_all, length, stored, grad_all, head_weights, head_scale, out_weight)
        for rows_all, length, stored, grad_all in zip(gathered, lengths, saved, grad_rows)
    ]
    weight_grad = results[0][0] + results[1][0] + results[2][0]
    bias_grad = results[0][1] + results[1][1] + results[2][1]
    scale_grad = results[0][2] + results[1][2] + results[2][2]
    out_grad = results[0][3] + results[1][3] + results[2][3]
    normed_terms = [item[4].astype(jnp.bfloat16).astype(jnp.float32) for item in results]
    normed_grad = (
        lax.psum_scatter(
            normed_terms[0].astype(jnp.bfloat16), "head", scatter_dimension=1, tiled=True
        ).astype(jnp.float32),
        lax.psum_scatter(
            normed_terms[1].astype(jnp.bfloat16), "head", scatter_dimension=1, tiled=True
        ).astype(jnp.float32),
        lax.psum_scatter(
            normed_terms[2].astype(jnp.bfloat16), "head", scatter_dimension=1, tiled=True
        ).astype(jnp.float32),
    )
    first_grad = join_rows(normed_grad, width)
    input_part, first_gain, first_shift = normalize_back(
        first_grad, first_unit, first_inverse, norm_gains[0]
    )
    input_grads = split_rows((residual_grad + input_part).astype(jnp.bfloat16), shapes)
    grad_head_weights, grad_head_biases, grad_head_scale, grad_out_weight = (
        lax.psum(weight_grad.astype(jnp.bfloat16), "batch").astype(jnp.float32),
        lax.psum(bias_grad.astype(jnp.bfloat16), "batch").astype(jnp.float32),
        lax.psum(scale_grad.astype(jnp.bfloat16), "batch").astype(jnp.float32),
        lax.psum(out_grad.astype(jnp.bfloat16), "batch").astype(jnp.float32),
    )
    gain_terms = jnp.stack([first_gain, second_gain, third_gain])
    shift_terms = jnp.stack(
        [first_shift, second_shift, third_shift, out_bias_grad, jnp.sum(cot_wide, axis=0)]
    )
    grad_norm_gains, grad_norm_shifts, grad_mid_gain, grad_mid_shifts = lax.psum(
        (gain_terms, shift_terms, mid_gain_grad, mid_terms), ("head", "batch")
    )
    return (
        outputs[0],
        outputs[1],
        outputs[2],
        input_grads[0],
        input_grads[1],
        input_grads[2],
        grad_norm_gains,
        grad_norm_shifts,
        grad_head_weights,
        grad_head_biases,
        grad_head_scale,
        grad_out_weight,
        grad_up_weight,
        grad_mid_gain,
        grad_mid_shifts,
        grad_down_weight,
    )


def solution(mesh):
    in_specs = (
        P("batch", "head", None),
        P("batch", "head", None),
        P("batch", "head", None),
        P("batch"),
        P("batch"),
        P("batch"),
        P("batch", "head", None),
        P("batch", "head", None),
        P("batch", "head", None),
        P(),
        P(),
        P(None, None, "head"),
        P(None, "head"),
        P("head"),
        P("head", None),
        P(("head", "batch"), None),
        P(),
        P(),
        P(("head", "batch"), None),
    )
    out_specs = (
        P("batch", "head", None),
        P("batch", "head", None),
        P("batch", "head", None),
        P("batch", "head", None),
        P("batch", "head", None),
        P("batch", "head", None),
        P(),
        P(),
        P(None, None, "head"),
        P(None, "head"),
        P("head"),
        P("head", None),
        P(("head", "batch"), None),
        P(),
        P(),
        P(("head", "batch"), None),
    )
    return jax.shard_map(shards, mesh=mesh, in_specs=in_specs, out_specs=out_specs, check_vma=False)
```

profile of v0, /device:TPU:0, one launch (start us, length us, event | category | flops | bytes accessed | tf_op | source)
XLA Modules:
  0.0 1964.4 jit_solution(17341221387767504130)
XLA Ops:
  28.2 31.0 %all-gather.21.cloned.1.call-done = bf16[1024,1024]{1,0:T(8,128)(2,1)} async-done(((bf16[512,1024]{1,0:T(8,128)(2,1)}), bf16[1024,1024]{1,0:T(8,128)(2,1)}) %all-gather.21.cloned.1.call-update) | async-done | bytes 2097168 | tf_op jit(solution)/shard_map/all_gather | solution.py:226
  78.4 35.5 %while.118 = (s32[]{:T(128)}, f32[2,512,8,64]{1,3,2,0:T(8,128)}, f32[2,8,512]{2,1,0:T(8,128)S(1)}, s32[2]{0:T(128)S(1)}, s32[1]{0:T(128)}, /*index=5*/bf16[2,512...) while((s32[]{:T(128)}, f32[2,512,8,64]{1,3,2,0:T(8,128)}, ...), condition=%wide.region_10.11_spmd, body=%wide.region_7.10_spmd.sunk | while | flops 1125119488 | bytes 56236808 | solution.py:71
  201.4 202.3 %while.119 = (s32[]{:T(128)}, f32[4,512,8,64]{1,3,2,0:T(8,128)}, f32[4,8,512]{2,1,0:T(8,128)}, s32[4]{0:T(128)S(1)}, s32[1]{0:T(128)}, /*index=5*/bf16[4,512,8,6...) while((s32[]{:T(128)}, f32[4,512,8,64]{1,3,2,0:T(8,128)}, ...), condition=%wide.region_15.16_spmd, body=%wide.region_12.15_spmd.sunk | while | flops 2250242560 | bytes 110765832 | solution.py:71
  418.3 55.4 %reduce-scatter.12.cloned.1.call-done = bf16[1,1024,1024]{2,1,0:T(8,128)(2,1)} async-done(((bf16[1,2048,1024]{2,1,0:T(8,128)(2,1)}), bf16[1,1024,1024]{2,1,0:T(8,128)(2,1)}) %reduce-scatter.12.cloned.1.call-update) | async-done | bytes 2097168 | tf_op jit(solution)/shard_map/reduce_scatter | solution.py:247
  493.5 25.6 %all-gather.15.cloned.1.call-done = bf16[4096,1024]{1,0:T(8,128)(2,1)} async-done(((bf16[128,1024]{1,0:T(8,128)(2,1)}), bf16[4096,1024]{1,0:T(8,128)(2,1)}) %all-gather.15.cloned.1.call-update) | async-done | bytes 8388624 | tf_op jit(solution)/shard_map/all_gather | solution.py:259
  519.1 34.1 %fusion.207 = (f32[2048]{0:T(1024)S(1)}, f32[2048,4096]{1,0:T(8,128)}) fusion(f32[4096]{0:T(1024)S(1)} %bitcast.627, bf16[4096,1024]{1,0:T(8,128)(2,1)} %all-gather.15.cloned.1.call-done, f32[2048,1024]{1,0:T(8,128)} %copy-done.13, f32[1024]{0:T(1024)S(1)} %bitcast.658, f32[1024]{0:T(1024)S(1)} %bitcast.648, f32[2048]{0:T(1024)S(1)} %add_rsqrt_fusion.1, ...), kind=kOutput, calls=%fused_computation.347 | convolution fusion | flops 17274238976 | bytes 50380800 | tf_op jit(solution)/shard_map/dot_general | solution.py:263
  572.9 25.1 %all-gather.17.cloned.1.call-done = bf16[4096,1024]{1,0:T(8,128)(2,1)} async-done(((bf16[128,1024]{1,0:T(8,128)(2,1)}), bf16[4096,1024]{1,0:T(8,128)(2,1)}) %all-gather.17.cloned.1.call-update) | async-done | bytes 8388624 | tf_op jit(solution)/shard_map/all_gather | solution.py:260
  598.0 44.3 %multiply_reduce_fusion.3 = (f32[4096]{0:T(1024)}, f32[2048]{0:T(1024)S(1)}, f32[2048]{0:T(1024)S(1)}, f32[4096]{0:T(1024)}, f32[2048,4096]{1,0:T(8,128)}) fusion(f32[2048]{0:T(1024)S(1)} %add_rsqrt_fusion, f32[2048]{0:T(1024)S(1)} %broadcast_multiply_fusion.2, f32[2048,4096]{1,0:T(8,128)} %get-tuple-element.1120, f32[4096]{0:T(1024)S(1)} %bitcast.629, ...), kind=kOutput, calls=%fused_computation.170 | convolution fusion | flops 17343434752 | bytes 79790080 | tf_op jit(solution)/shard_map/dot_general | solution.py:270
  642.3 45.4 %convert_reduce_fusion = (f32[4096]{0:T(1024)}, bf16[2048,4096]{1,0:T(8,128)(2,1)}, bf16[2048,4096]{1,0:T(8,128)(2,1)}) fusion(f32[2048]{0:T(1024)S(1)} %get-tuple-element.1127, f32[2048]{0:T(1024)S(1)} %add_rsqrt_fusion, f32[2048]{0:T(1024)S(1)} %broadcast_multiply_fusion.2, f32[2048,4096]{1,0:T(8,128)} %get-tuple-element.1120, f32[4096]{0:T(1024)S(1)} %bitcast.630, ...), kind=kLoop, calls=%fused_computation.169 | loop fusion | flops 285208576 | bytes 100761600 | tf_op jit(solution)/shard_map/reduce_sum | solution.py:288
  687.8 27.2 %multiply_reduce_fusion.7 = (f32[1024]{0:T(1024)}, f32[2048]{0:T(1024)S(1)}, f32[2048]{0:T(1024)S(1)}, f32[1024]{0:T(1024)}, f32[2048,1024]{1,0:T(8,128)}) fusion(f32[2048,1024]{1,0:T(8,128)} %copy-done.13, f32[2048]{0:T(1024)S(1)} %add_rsqrt_fusion.1, f32[2048]{0:T(1024)S(1)} %broadcast_multiply_fusion.9, f32[1024]{0:T(1024)S(1)} %bitcast.649, ...), kind=kOutput, calls=%fused_computation.198 | convolution fusion | flops 17198739456 | bytes 41988096 | tf_op jit(solution)/shard_map/dot_general | solution.py:277
  778.4 123.7 %while.121 = (s32[]{:T(128)}, f32[1024,8,64]{0,2,1:T(8,128)}, f32[1024,8,64]{0,2,1:T(8,128)}, bf16[2,512,8,64]{1,3,2,0:T(8,128)(2,1)}, s32[2]{0:T(128)S(1)}, /*i...) while((s32[]{:T(128)}, f32[1024,8,64]{0,2,1:T(8,128)}, ...), condition=%wide.region_35.36_spmd.clone, body=%wide.region_33.35_spmd.clone.sunk | while | flops 2726295040 | bytes 262757296 | solution.py:118
  911.7 29.9 %while.120 = (s32[]{:T(128)}, bf16[2,512,8,64]{1,3,2,0:T(8,128)(2,1)}, bf16[2,512,8,64]{1,3,2,0:T(8,128)(2,1)}, bf16[2,512,8,64]{1,3,2,0:T(8,128)(2,1)}, bf16[2,...) while((s32[]{:T(128)}, ...), condition=%wide.region_31.32_spmd, body=%wide.region_29.31_spmd.sunk | while | flops 1375465984 | bytes 94492968 | solution.py:127
  982.2 449.4 %while.122 = (s32[]{:T(128)}, f32[2048,8,64]{0,2,1:T(8,128)}, f32[2048,8,64]{0,2,1:T(8,128)}, bf16[4,512,8,64]{1,3,2,0:T(8,128)(2,1)}, s32[4]{0:T(128)S(1)}, /*i...) while((s32[]{:T(128)}, f32[2048,8,64]{0,2,1:T(8,128)}, ...), condition=%wide.region_39.40_spmd.clone, body=%wide.region_37.39_spmd.clone.sunk | while | flops 5452069376 | bytes 355033920 | solution.py:118
  1004.9 24.7 %multiply_reduce_fusion.24 = (f32[8,512]{1,0:T(8,128)S(1)}, f32[8,512,2048]{2,1,0:T(8,128)}) fusion(f32[8,512,2048]{2,1,0:T(8,128)} %fusion.392, f32[8,512]{1,0:T(8,128)S(1)} %dynamic-slice_bitcast_fusion.8, bf16[2048,8,64]{0,2,1:T(8,128)(2,1)S(1)} %get-tuple-element.1644, bf16[2048,8,64]{0,2,1:T(8,128)(2,1)} %get-tuple-element.1642, ...), kind=kOutput, calls=%fused_computation.135.clone.1 | convolution fusion | flops 1115680768 | bytes 70811648 | tf_op jit(solution)/shard_map/while/body/eval_jaxpr/while/body/eval_jaxpr/qhd,khd->hqk/dot_general | solution.py:45
  1029.6 27.4 %multiply_convert_fusion.18 = bf16[8,512,2048]{2,1,0:T(8,128)(2,1)} fusion(f32[8,512,2048]{2,1,0:T(8,128)} %get-tuple-element.1495, f32[8,512,2048]{2,1,0:T(8,128)} %fusion.392, f32[8,512]{1,0:T(8,128)S(1)} %get-tuple-element.1496), kind=kLoop, calls=%fused_computation.134.clone.1 | loop fusion | flops 25165824 | bytes 83902464 | tf_op jit(solution)/shard_map/while/body/eval_jaxpr/while/body/eval_jaxpr/convert_element_type | solution.py:103
  1115.3 24.7 %multiply_reduce_fusion.24 = (f32[8,512]{1,0:T(8,128)S(1)}, f32[8,512,2048]{2,1,0:T(8,128)}) fusion(f32[8,512,2048]{2,1,0:T(8,128)} %fusion.392, f32[8,512]{1,0:T(8,128)S(1)} %dynamic-slice_bitcast_fusion.8, bf16[2048,8,64]{0,2,1:T(8,128)(2,1)S(1)} %get-tuple-element.1644, bf16[2048,8,64]{0,2,1:T(8,128)(2,1)} %get-tuple-element.1642, ...), kind=kOutput, calls=%fused_computation.135.clone.1 | convolution fusion | flops 1115680768 | bytes 70811648 | tf_op jit(solution)/shard_map/while/body/eval_jaxpr/while/body/eval_jaxpr/qhd,khd->hqk/dot_general | solution.py:45
  1140.1 27.4 %multiply_convert_fusion.18 = bf16[8,512,2048]{2,1,0:T(8,128)(2,1)} fusion(f32[8,512,2048]{2,1,0:T(8,128)} %get-tuple-element.1495, f32[8,512,2048]{2,1,0:T(8,128)} %fusion.392, f32[8,512]{1,0:T(8,128)S(1)} %get-tuple-element.1496), kind=kLoop, calls=%fused_computation.134.clone.1 | loop fusion | flops 25165824 | bytes 83902464 | tf_op jit(solution)/shard_map/while/body/eval_jaxpr/while/body/eval_jaxpr/convert_element_type | solution.py:103
  1228.2 24.7 %multiply_reduce_fusion.24 = (f32[8,512]{1,0:T(8,128)S(1)}, f32[8,512,2048]{2,1,0:T(8,128)}) fusion(f32[8,512,2048]{2,1,0:T(8,128)} %fusion.392, f32[8,512]{1,0:T(8,128)S(1)} %dynamic-slice_bitcast_fusion.8, bf16[2048,8,64]{0,2,1:T(8,128)(2,1)S(1)} %get-tuple-element.1644, bf16[2048,8,64]{0,2,1:T(8,128)(2,1)} %get-tuple-element.1642, ...), kind=kOutput, calls=%fused_computation.135.clone.1 | convolution fusion | flops 1115680768 | bytes 70811648 | tf_op jit(solution)/shard_map/while/body/eval_jaxpr/while/body/eval_jaxpr/qhd,khd->hqk/dot_general | solution.py:45
  1252.9 27.4 %multiply_convert_fusion.18 = bf16[8,512,2048]{2,1,0:T(8,128)(2,1)} fusion(f32[8,512,2048]{2,1,0:T(8,128)} %get-tuple-element.1495, f32[8,512,2048]{2,1,0:T(8,128)} %fusion.392, f32[8,512]{1,0:T(8,128)S(1)} %get-tuple-element.1496), kind=kLoop, calls=%fused_computation.134.clone.1 | loop fusion | flops 25165824 | bytes 83902464 | tf_op jit(solution)/shard_map/while/body/eval_jaxpr/while/body/eval_jaxpr/convert_element_type | solution.py:103
  1341.1 24.7 %multiply_reduce_fusion.24 = (f32[8,512]{1,0:T(8,128)S(1)}, f32[8,512,2048]{2,1,0:T(8,128)}) fusion(f32[8,512,2048]{2,1,0:T(8,128)} %fusion.392, f32[8,512]{1,0:T(8,128)S(1)} %dynamic-slice_bitcast_fusion.8, bf16[2048,8,64]{0,2,1:T(8,128)(2,1)S(1)} %get-tuple-element.1644, bf16[2048,8,64]{0,2,1:T(8,128)(2,1)} %get-tuple-element.1642, ...), kind=kOutput, calls=%fused_computation.135.clone.1 | convolution fusion | flops 1115680768 | bytes 70811648 | tf_op jit(solution)/shard_map/while/body/eval_jaxpr/while/body/eval_jaxpr/qhd,khd->hqk/dot_general | solution.py:45
  1365.8 27.4 %multiply_convert_fusion.18 = bf16[8,512,2048]{2,1,0:T(8,128)(2,1)} fusion(f32[8,512,2048]{2,1,0:T(8,128)} %get-tuple-element.1495, f32[8,512,2048]{2,1,0:T(8,128)} %fusion.392, f32[8,512]{1,0:T(8,128)S(1)} %get-tuple-element.1496), kind=kLoop, calls=%fused_computation.134.clone.1 | loop fusion | flops 25165824 | bytes 83902464 | tf_op jit(solution)/shard_map/while/body/eval_jaxpr/while/body/eval_jaxpr/convert_element_type | solution.py:103
  1510.6 26.2 %fusion.205 = f32[4096,1024]{0,1:T(8,128)} fusion(bf16[2048,4096]{1,0:T(8,128)(2,1)} %get-tuple-element.1075, f32[2048,1024]{1,0:T(8,128)} %copy-done.13, f32[1024]{0:T(1024)S(1)} %bitcast.659, f32[1024]{0:T(1024)S(1)} %bitcast.651, f32[2048]{0:T(1024)S(1)} %copy-done.110, f32[2048]{0:T(1024)S(1)} %copy-done.102), kind=kOutput, calls=%fused_computation.345 | convolution fusion | flops 17190354944 | bytes 41967616 | tf_op jit(solution)/shard_map/dot_general | solution.py:281
  1591.5 38.2 %all-reduce.1 = (bf16[2,512]{1,0:T(2,128)(2,1)S(1)}, bf16[8]{0:T(256)(128)(2,1)S(1)}) all-reduce(bf16[2,512]{1,0:T(2,128)(2,1)S(1)} %fusion.202, bf16[8]{0:T(256)(128)(2,1)S(1)} %add_convert_fusion.13), channel_id=1, replica_groups=mesh['head'=2,'batch'=16] {'batch'}, use_global_device_ids=true, to_apply=%region_62.63 | all-reduce | flops 1032 | bytes 4128 | tf_op jit(solution)/shard_map/psum | solution.py:333
  1680.6 267.6 %reduce-scatter.20.cloned.1.call-done = f32[128,2048]{0,1:T(8,128)} async-done(((f32[4096,2048]{0,1:T(8,128)}), f32[128,2048]{0,1:T(8,128)}) %reduce-scatter.20.cloned.1.call-update) | async-done | bytes 1048592 | tf_op jit(solution)/shard_map/reduce_scatter | solution.py:282
  (708 shorter events, 1105.2 us)
Async XLA Ops:
  8.0 135.3 %copy-start = (bf16[512,1024]{1,0:T(8,128)(2,1)S(1)}, bf16[512,1024]{1,0:T(8,128)(2,1)}, u32[]{:S(2)}) copy-start(bf16[512,1024]{1,0:T(8,128)(2,1)} %param.45) | copy-start | bytes 3145732
  8.1 51.2 %all-gather.21.cloned.1.call-start = ((), (), s32[]{:S(2)}) async-start(), calls=%async_computation.18 | async-start | bytes 3145728 | tf_op jit(solution)/shard_map/all_gather | solution.py:226
  23.3 96.1 %all-gather.13.cloned.1.call-start = ((), (), s32[]{:S(2)}) async-start(), calls=%async_computation.7 | async-start | bytes 3145728 | tf_op jit(solution)/shard_map/all_gather | solution.py:225
  24.0 154.6 %all-gather.23.cloned.1.call-start = ((), (), s32[]{:S(2)}) async-start(), calls=%async_computation.19 | async-start | bytes 6291456 | tf_op jit(solution)/shard_map/all_gather | solution.py:227
  27.2 391.1 %reduce-scatter.10.cloned.1.call-start = ((), (), s32[]{:S(2)}) async-start(), calls=%async_computation.9 | async-start | bytes 3145728 | tf_op jit(solution)/shard_map/reduce_scatter | solution.py:244
  147.6 270.7 %reduce-scatter.8.cloned.1.call-start = ((), (), s32[]{:S(2)}) async-start(), calls=%async_computation.8 | async-start | bytes 3145728 | tf_op jit(solution)/shard_map/reduce_scatter | solution.py:241
  178.5 295.2 %reduce-scatter.12.cloned.1.call-start = ((), (), s32[]{:S(2)}) async-start(), calls=%async_computation.10 | async-start | bytes 6291456 | tf_op jit(solution)/shard_map/reduce_scatter | solution.py:247
  417.0 63.2 %copy-start.16 = (bf16[1,1024,1024]{2,1,0:T(8,128)(2,1)S(1)}, bf16[1,1024,1024]{2,1,0:T(8,128)(2,1)}, u32[]{:S(2)}) copy-start(bf16[1,1024,1024]{2,1,0:T(8,128)(2,1)} %param.33) | copy-start | bytes 6291460
  417.0 63.2 %copy-start.103 = (f32[1,1024]{1,0:T(1,128)S(1)}, f32[1,1024]{1,0:T(1,128)}, u32[]{:S(2)}) copy-start(f32[1,1024]{1,0:T(1,128)} %get-tuple-element.1115) | copy-start | bytes 12292
  417.0 63.2 %copy-start.113 = (f32[1,1024]{1,0:T(1,128)S(1)}, f32[1,1024]{1,0:T(1,128)}, u32[]{:S(2)}) copy-start(f32[1,1024]{1,0:T(1,128)} %get-tuple-element.1107) | copy-start | bytes 12292
  417.0 102.1 %all-gather.15.cloned.1.call-start = ((), (), s32[]{:S(2)}) async-start(), calls=%async_computation.11 | async-start | bytes 8650752 | tf_op jit(solution)/shard_map/all_gather | solution.py:259
  417.6 180.4 %all-gather.17.cloned.1.call-start = ((), (), s32[]{:S(2)}) async-start(), calls=%async_computation.12 | async-start | bytes 8650752 | tf_op jit(solution)/shard_map/all_gather | solution.py:260
  418.2 354.4 %all-gather.25.cloned.1.call-start = ((), (), s32[]{:S(2)}) async-start(), calls=%async_computation.20 | async-start | bytes 3145728 | tf_op jit(solution)/shard_map/all_gather | solution.py:303
  488.4 226.6 %copy-start.101 = (f32[2048]{0:T(1024)}, f32[2048]{0:T(1024)S(1)}, u32[]{:S(2)}) copy-start(f32[2048]{0:T(1024)S(1)} %broadcast_multiply_fusion.9) | copy-start | bytes 24580
  493.5 221.6 %copy-start.109 = (f32[2048]{0:T(1024)}, f32[2048]{0:T(1024)S(1)}, u32[]{:S(2)}) copy-start(f32[2048]{0:T(1024)S(1)} %add_rsqrt_fusion.1) | copy-start | bytes 24580
  740.7 161.4 %all-gather.19.cloned.1.call-start = ((), (), s32[]{:S(2)}) async-start(), calls=%async_computation.13 | async-start | bytes 3145728 | tf_op jit(solution)/shard_map/all_gather | solution.py:302
  741.4 232.2 %all-gather.27.cloned.1.call-start = ((), (), s32[]{:S(2)}) async-start(), calls=%async_computation.21 | async-start | bytes 6291456 | tf_op jit(solution)/shard_map/all_gather | solution.py:304
  751.0 879.7 %all-reduce.8.cloned.1.call-start = ((), (), s32[]{:S(2)}) async-start(), calls=%async_computation.23 | async-start | bytes 8388608 | tf_op jit(solution)/shard_map/psum | solution.py:332
  778.4 123.7 %copy-start.94 = (f32[8]{0:T(128)S(1)}, f32[8]{0:T(128)}, u32[]{:S(2)}) copy-start(f32[8]{0:T(128)} %param.44) | copy-start | bytes 100
  1458.3 179.6 %reduce-scatter.14.cloned.1.call-start = ((), (), s32[]{:S(2)}) async-start(), calls=%async_computation.14 | async-start | bytes 3145728 | tf_op jit(solution)/shard_map/reduce_scatter | solution.py:316
  1465.4 176.9 %reduce-scatter.16.cloned.1.call-start = ((), (), s32[]{:S(2)}) async-start(), calls=%async_computation.15 | async-start | bytes 3145728 | tf_op jit(solution)/shard_map/reduce_scatter | solution.py:319
  1472.5 174.1 %reduce-scatter.18.cloned.1.call-start = ((), (), s32[]{:S(2)}) async-start(), calls=%async_computation.16 | async-start | bytes 6291456 | tf_op jit(solution)/shard_map/reduce_scatter | solution.py:322
  1487.1 461.1 %reduce-scatter.20.cloned.1.call-start = ((), (), s32[]{:S(2)}) async-start(), calls=%async_computation.17 | async-start | bytes 34603008 | tf_op jit(solution)/shard_map/reduce_scatter | solution.py:282
  1555.8 395.6 %all-reduce.6.cloned.1.call-start = ((), (), s32[]{:S(2)}) async-start(), calls=%async_computation.22 | async-start | bytes 196608 | tf_op jit(solution)/shard_map/psum | solution.py:341
  (162 other events, 1779.1 us)
Sparse Core Ops, SparseCore 0:
  23.4 35.8 all-gather.20
  61.4 33.1 all-gather.12
  96.6 56.7 all-gather.22
  155.5 31.8 reduce-scatter.9
  189.6 31.8 reduce-scatter.7
  417.1 56.5 reduce-scatter.11
  740.8 31.7 all-gather.24
  774.2 33.1 all-gather.18
  809.5 56.7 all-gather.26
  1465.5 32.2 reduce-scatter.13
  1500.1 31.8 reduce-scatter.15
  1534.3 54.3 reduce-scatter.17
  1591.1 357.1 reduce-scatter.19
Sparse Core Ops, SparseCore 1:
  420.7 98.3 all-gather.14
  522.2 75.8 all-gather.16
  1458.4 111.9 all-reduce.7
  1680.7 183.8 all-reduce.5
where the time goes:
time: 1970 us; the launch traced here: 1960 us
  matrix products  879 us (45%)
  waiting for transfers between devices  429 us (22%)
  other arithmetic  427 us (22%)
  local copies, waits for them, and re-layouts  138 us (7%)
  blocking collectives  38.2 us (2%)
  loops' own time  34.3 us (2%)
    reduce_scatter x1, waiting for transfers between devices, shards(): lax.psum_scatter(jnp.concatenate([down_piece, up_piece], 1), ('head', 'ba...  268 us
    dot_general x16, matrix products, block_scores(): jnp.einsum('qhd,khd->hqk', query_block, key_row, preferred_element_type=j...  203 us
    convert_element_type x8, other arithmetic, one_one_block(): score_grad = (shares * (share_grad - inner)).astype(jnp.bfloat16)  134 us
    dot_general x8, matrix products, one_one_block(): jnp.einsum('qhd,khd->hqk', grad_block, value_row, preferred_element_type=...  94.5 us
    dot_general x8, matrix products, attend_one_block(): jnp.einsum('hqk,khd->qhd', shares, values[row], preferred_element_type=jn...  82.7 us
    dot_general x8, matrix products, one_one_block(): jnp.einsum('hqk,qhd->khd', shares.astype(jnp.bfloat16), grad_block, prefe...  82.3 us
    reduce_sum x8, other arithmetic, attend_one_block(): total = jnp.sum(weights, axis=-1, keepdims=True)  71.9 us
    dot_general x8, matrix products, one_one_block(): jnp.einsum('hqk,qhd->khd', score_grad, query_block, preferred_element_typ...  65 us
  transfers between devices with their start and end apart: 17, of which 6 were waited for; matrix products, arithmetic and copies ran while one was open for 40% of the time, Pallas kernels for 0%

commit v1 on v0

v1 whole, which is shorter than its diff:
```python
import functools

import jax
import jax.numpy as jnp
from jax import lax
from jax.experimental import pallas as pl
from jax.experimental.pallas import tpu as pltpu
from jax.sharding import PartitionSpec as P

EPSILON = 1e-05
ROW_PAIRS = (((0,), (0,)), ((), ()))
COLUMN_PAIRS = (((1,), (1,)), ((), ()))
LANES = 128
HEAD = 64
LOG2E = 1.4426950408889634
EXPONENT_SCALE = HEAD ** (-0.5) * LOG2E
MASKED = -1e30
GELU_SCALE = 0.7978845608028654
GELU_CUBE = 0.044715
BF = jnp.bfloat16
F32 = jnp.float32


def dot(a, b, dims=(((1,), (0,)), ((), ()))):
    return lax.dot_general(a, b, dims, preferred_element_type=F32)


def normalize(value, gain, shift):
    centred = value - jnp.mean(value, axis=-1, keepdims=True)
    inverse = lax.rsqrt(jnp.mean(centred * centred, axis=-1, keepdims=True) + EPSILON)
    unit = centred * inverse
    return (unit * gain + shift, unit, inverse)


def normalize_back(grad, unit, inverse, gain):
    scaled = grad * gain
    inner = (
        scaled
        - jnp.mean(scaled, axis=-1, keepdims=True)
        - unit * jnp.mean(scaled * unit, axis=-1, keepdims=True)
    )
    return (inner * inverse, jnp.sum(grad * unit, axis=0), jnp.sum(grad, axis=0))


def place(me, slot, slots, part):
    return pl.multiple_of(lax.rem(me + slot, slots) * part, part)


def attend_forward_kernel(slots, span, block, kept, me_ref, len_ref, *refs):
    qkv = refs[:slots]
    scale_ref = refs[slots]
    refs = refs[kept:]
    outs = refs[slots + 1 : 2 * slots + 1]
    total_ref = refs[2 * slots + 1]
    query, keys, values, mixed = refs[2 * slots + 2 :]
    part = span // slots
    me = me_ref[0]
    length = len_ref[pl.program_id(0)]
    for slot in range(slots):
        at = pl.ds(place(me, slot, slots, part), part)
        query[at, :] = qkv[slot][:, :LANES]
        keys[at, :] = qkv[slot][:, LANES : 2 * LANES]
        values[at, :] = qkv[slot][:, 2 * LANES :]
    first = lax.broadcasted_iota(jnp.int32, (1, LANES), 1) < HEAD
    for i in range(span // block):
        rows = slice(i * block, (i + 1) * block)
        query_block = query[rows, :]
        halves = []
        for head in range(2):
            mine = first if head == 0 else jnp.logical_not(first)
            query_head = jnp.where(mine, query_block, jnp.zeros_like(query_block))
            scores = []
            for j in range(i + 1):
                key_block = keys[j * block : (j + 1) * block, :]
                score = dot(query_head, key_block, COLUMN_PAIRS)
                key_place = lax.broadcasted_iota(jnp.int32, (block, block), 1)
                allowed = None
                if i == j:
                    allowed = key_place <= lax.broadcasted_iota(jnp.int32, (block, block), 0)
                if (j + 1) * block > span // 2:
                    short = key_place < length - j * block
                    allowed = short if allowed is None else allowed & short
                if allowed is not None:
                    score = jnp.where(allowed, score, MASKED)
                scores.append(score)
            top = functools.reduce(jnp.maximum, scores)
            top = jnp.max(top, axis=-1, keepdims=True) * EXPONENT_SCALE
            weights = [jnp.exp2(score * EXPONENT_SCALE - top) for score in scores]
            total = jnp.sum(functools.reduce(jnp.add, weights), axis=-1, keepdims=True)
            result = None
            for j in range(i + 1):
                term = dot(weights[j].astype(BF), values[j * block : (j + 1) * block, :])
                result = term if result is None else result + term
            halves.append(result / total)
            log_total = jnp.broadcast_to(top + jnp.log2(total), (block, LANES))
            total_ref[0, 0, head : head + 1, rows] = jnp.transpose(log_total)[:1, :]
        mixed[rows, :] = (jnp.where(first, halves[0], halves[1]) * scale_ref[...]).astype(BF)
    for slot in range(slots):
        outs[slot][...] = mixed[pl.ds(place(me, slot, slots, part), part), :]


def attend_backward_kernel(slots, span, block, kept, me_ref, len_ref, *refs):
    qkv = refs[:slots]
    out = refs[slots : 2 * slots]
    grads = refs[2 * slots : 3 * slots]
    scale_ref, total_ref = refs[3 * slots : 3 * slots + 2]
    refs = refs[kept:]
    results = refs[3 * slots + 2 : 4 * slots + 2]
    sums_ref = refs[4 * slots + 2]
    query, keys, values, mixed_grad, product, query_grad, key_grad, value_grad = refs[4 * slots + 3 :]
    part = span // slots
    me = me_ref[0]
    length = len_ref[pl.program_id(0)]
    for slot in range(slots):
        at = pl.ds(place(me, slot, slots, part), part)
        query[at, :] = qkv[slot][:, :LANES]
        keys[at, :] = qkv[slot][:, LANES : 2 * LANES]
        values[at, :] = qkv[slot][:, 2 * LANES :]
        grad = grads[slot][...].astype(F32)
        mixed_grad[at, :] = (grad * scale_ref[...]).astype(BF)
        product[at, :] = grad * out[slot][...].astype(F32)
    first = lax.broadcasted_iota(jnp.int32, (1, LANES), 1) < HEAD
    which = lax.broadcasted_iota(jnp.int32, (8, LANES), 0)
    lane_head = lax.broadcasted_iota(jnp.int32, (8, LANES), 1) // HEAD
    picks = jnp.where(which == lane_head, 1.0, 0.0).astype(BF)
    inner = product[...]
    inner_high = inner.astype(BF)
    inner_low = (inner - inner_high.astype(F32)).astype(BF)
    inner_sum = dot(picks, inner_high, COLUMN_PAIRS) + dot(picks, inner_low, COLUMN_PAIRS)
    scale_sum = jnp.sum(inner, axis=0, keepdims=True) / scale_ref[...]
    count = span // block
    for j in range(count):
        cols = slice(j * block, (j + 1) * block)
        key_block, value_block = keys[cols, :], values[cols, :]
        key_parts, value_parts = [], []
        for head in range(2):
            mine = first if head == 0 else jnp.logical_not(first)
            key_head = jnp.where(mine, key_block, jnp.zeros_like(key_block))
            value_head = jnp.where(mine, value_block, jnp.zeros_like(value_block))
            key_sum = value_sum = None
            for i in range(j, count):
                rows = slice(i * block, (i + 1) * block)
                query_block, grad_block = query[rows, :], mixed_grad[rows, :]
                score = dot(key_head, query_block, COLUMN_PAIRS)
                shares = jnp.exp2(score * EXPONENT_SCALE - total_ref[0, 0, head : head + 1, rows])
                key_place = lax.broadcasted_iota(jnp.int32, (block, block), 0)
                allowed = None
                if i == j:
                    allowed = key_place <= lax.broadcasted_iota(jnp.int32, (block, block), 1)
                if (j + 1) * block > span // 2:
                    short = key_place < length - j * block
                    allowed = short if allowed is None else allowed & short
                if allowed is not None:
                    shares = jnp.where(allowed, shares, 0.0)
                share_grad = dot(value_head, grad_block, COLUMN_PAIRS)
                score_grad = shares * (share_grad - inner_sum[head : head + 1, rows])
                score_grad = score_grad.astype(BF)
                term = dot(shares.astype(BF), grad_block)
                value_sum = term if value_sum is None else value_sum + term
                term = dot(score_grad, query_block)
                key_sum = term if key_sum is None else key_sum + term
                term = dot(score_grad, key_head, ROW_PAIRS)
                if j == 0 and head == 0:
                    query_grad[rows, :] = term
                else:
                    query_grad[rows, :] += term
            key_parts.append(key_sum)
            value_parts.append(value_sum)
        key_grad[cols, :] = (jnp.where(first, *key_parts) * HEAD ** (-0.5)).astype(BF)
        value_grad[cols, :] = jnp.where(first, *value_parts).astype(BF)
    query_sum = value_sum = jnp.zeros((1, LANES), F32)
    for slot in range(slots):
        at = pl.ds(place(me, slot, slots, part), part)
        piece = (query_grad[at, :] * HEAD ** (-0.5)).astype(BF)
        results[slot][:, :LANES] = piece
        results[slot][:, LANES : 2 * LANES] = key_grad[at, :]
        results[slot][:, 2 * LANES :] = value_grad[at, :]
        query_sum += jnp.sum(piece.astype(F32), axis=0, keepdims=True)
        value_sum += jnp.sum(value_grad[at, :].astype(F32), axis=0, keepdims=True)
    sums_ref[0, 0, 0:1, :] = query_sum
    sums_ref[0, 0, 1:2, :] = value_sum
    sums_ref[0, 0, 2:3, :] = scale_sum
    sums_ref[0, 0, 3:, :] = jnp.zeros((5, LANES), F32)


def sum_everywhere(value, axes):
    for name, size in axes:
        if size & (size - 1):
            value = lax.psum(value, name)
            continue
        step = 1
        while step < size:
            pairs = [(d, d ^ step) for d in range(size)]
            value = value + lax.ppermute(value, name, pairs)
            step *= 2
    return value


def attention_specs(slots, span, first_block, width):
    part = span // slots
    return pl.BlockSpec((part, width), lambda r, p, *_: (first_block + r, p))


def attend_forward(me, lengths, qkv, scale_lanes, kept, rows, span, first_block):
    slots = len(qkv)
    tokens = qkv[0].shape[0]
    pairs = qkv[0].shape[1] // (3 * LANES)
    block = min(512, span)
    call = pl.pallas_call(
        functools.partial(attend_forward_kernel, slots, span, block, len(kept)),
        grid_spec=pltpu.PrefetchScalarGridSpec(
            num_scalar_prefetch=2,
            grid=(rows, pairs),
            in_specs=[attention_specs(slots, span, first_block, 3 * LANES)] * slots
            + [pl.BlockSpec((1, LANES), lambda r, p, *_: (0, p))]
            + [pl.BlockSpec(memory_space=pl.ANY)] * len(kept),
            out_specs=[attention_specs(slots, span, first_block, LANES)] * slots
            + [pl.BlockSpec((1, 1, 2, span), lambda r, p, *_: (p, r, 0, 0))],
            scratch_shapes=[pltpu.VMEM((span, LANES), BF)] * 4,
        ),
        out_shape=[jax.ShapeDtypeStruct((tokens, pairs * LANES), BF)] * slots
        + [jax.ShapeDtypeStruct((pairs, rows, 2, span), F32)],
        input_output_aliases={3 + slots + k: k for k in range(len(kept))},
        compiler_params=pltpu.CompilerParams(vmem_limit_bytes=56 * 2**20),
        name="attend_forward",
    )
    *outs, log_total = call(me, lengths, *qkv, scale_lanes, *kept)
    return outs, log_total


def attend_backward(
    me, lengths, qkv, outs, grads, scale_lanes, log_total, kept, rows, span, first_block
):
    slots = len(qkv)
    tokens = qkv[0].shape[0]
    pairs = qkv[0].shape[1] // (3 * LANES)
    block = min(512, span)
    call = pl.pallas_call(
        functools.partial(attend_backward_kernel, slots, span, block, len(kept)),
        grid_spec=pltpu.PrefetchScalarGridSpec(
            num_scalar_prefetch=2,
            grid=(rows, pairs),
            in_specs=[attention_specs(slots, span, first_block, 3 * LANES)] * slots
            + [attention_specs(slots, span, first_block, LANES)] * (2 * slots)
            + [
                pl.BlockSpec((1, LANES), lambda r, p, *_: (0, p)),
                pl.BlockSpec((1, 1, 2, span), lambda r, p, *_: (p, r, 0, 0)),
            ]
            + [pl.BlockSpec(memory_space=pl.ANY)] * len(kept),
            out_specs=[attention_specs(slots, span, first_block, 3 * LANES)] * slots
            + [pl.BlockSpec((1, 1, 8, LANES), lambda r, p, *_: (r, p, 0, 0))],
            scratch_shapes=[pltpu.VMEM((span, LANES), BF)] * 4
            + [pltpu.VMEM((span, LANES), F32)] * 2
            + [pltpu.VMEM((span, LANES), BF)] * 2,
        ),
        out_shape=[jax.ShapeDtypeStruct((tokens, pairs * 3 * LANES), BF)] * slots
        + [jax.ShapeDtypeStruct((rows, pairs, 8, LANES), F32)],
        input_output_aliases={4 + 3 * slots + k: k for k in range(len(kept))},
        compiler_params=pltpu.CompilerParams(vmem_limit_bytes=56 * 2**20),
        name="attend_backward",
    )
    *results, sums = call(me, lengths, *qkv, *outs, *grads, scale_lanes, log_total, *kept)
    return results, sums


def fold(value):
    return functools.reduce(
        jnp.add, [value[:, k : k + LANES] for k in range(0, value.shape[1], LANES)]
    )


def row_sum(value):
    return jnp.sum(value, axis=-1, keepdims=True)


def column_sum(value):
    return jnp.sum(value, axis=0, keepdims=True)


def middle_kernel(slots, chunk, *refs):
    rows_ref, cot_ref = refs[:2]
    scaled = refs[2 : 2 + slots]
    out_weights = refs[2 + slots : 2 + 2 * slots]
    feed_ref, gains, shifts, mid_gain, mid_shifts = refs[2 + 2 * slots : 7 + 2 * slots]
    results = refs[7 + 2 * slots :]
    out_ref, residual_grad_ref, dense_ref, attended_grad_ref = results[:4]
    middle_ref, hidden_grad_ref, sums_ref, mid_sums_ref = results[4:8]
    scaled_grads = results[8 : 8 + slots]
    gelu_ref, slope_ref, grad_ref = results[8 + slots :]

    @pl.when(pl.program_id(0) == 0)
    def _():
        sums_ref[...] = jnp.zeros_like(sums_ref)
        mid_sums_ref[...] = jnp.zeros_like(mid_sums_ref)

    attended = shifts[3:4, :]
    for rows, matrix in zip(scaled, out_weights):
        attended = attended + dot(rows[...], matrix[...]).astype(BF).astype(F32)
    post, post_unit, post_inverse = normalize(attended, gains[1:2, :], shifts[1:2, :])
    residual = rows_ref[...].astype(F32) + post
    dense, dense_unit, dense_inverse = normalize(residual, gains[2:3, :], shifts[2:3, :])
    dense = dense.astype(BF)
    dense_ref[...] = dense
    cotangent = cot_ref[...]
    total = mid_gain.shape[1]

    def up(start):
        return feed_ref[2 * start : 2 * start + chunk, :]

    def down(start):
        return feed_ref[2 * start + chunk : 2 * start + 2 * chunk, :]

    base = first = second = third = fourth = None
    for start in range(0, total, chunk):
        cols = slice(start, start + chunk)
        hidden = dot(dense, up(start), COLUMN_PAIRS) + mid_shifts[0:1, cols]
        square = hidden * hidden
        bent = jnp.tanh(hidden * (GELU_SCALE + GELU_SCALE * GELU_CUBE * square))
        half = 0.5 * hidden
        active = half + half * bent
        slope = (0.5 + 0.5 * bent) + (half * (1.0 - bent * bent)) * (
            GELU_SCALE + 3.0 * GELU_SCALE * GELU_CUBE * square
        )
        grad = dot(cotangent, down(start), COLUMN_PAIRS)
        gelu_ref[:, cols] = active
        slope_ref[:, cols] = slope
        grad_ref[:, cols] = grad
        if base is None:
            base = row_sum(fold(active)) / chunk
        away = active - base
        weighted = grad * mid_gain[:, cols]
        terms = [fold(away), fold(away * away), fold(weighted), fold(weighted * away)]
        if first is None:
            first, second, third, fourth = terms
        else:
            first, second, third, fourth = [
                a + b for a, b in zip((first, second, third, fourth), terms)
            ]
    offset = row_sum(first) / total
    mean = base + offset
    inverse = lax.rsqrt(jnp.maximum(row_sum(second) / total - offset * offset, 0.0) + EPSILON)
    grad_mean = row_sum(third) / total
    grad_unit = inverse * (row_sum(fourth) / total - offset * grad_mean)
    branch = dense_grad = None
    for start in range(0, total, chunk):
        cols = slice(start, start + chunk)
        unit = (gelu_ref[:, cols] - mean) * inverse
        gain = mid_gain[:, cols]
        middle = (unit * gain + mid_shifts[1:2, cols]).astype(BF)
        middle_ref[:, cols] = middle
        term = dot(middle, down(start))
        branch = term if branch is None else branch + term
        grad = grad_ref[:, cols]
        inner = inverse * (grad * gain - grad_mean - unit * grad_unit)
        hidden_grad = (inner * slope_ref[:, cols]).astype(BF)
        hidden_grad_ref[:, cols] = hidden_grad
        mid_sums_ref[0:1, cols] += column_sum(grad * unit)
        mid_sums_ref[1:2, cols] += column_sum(grad)
        mid_sums_ref[2:3, cols] += column_sum(hidden_grad.astype(F32))
        term = dot(hidden_grad, up(start))
        dense_grad = term if dense_grad is None else dense_grad + term
    out_ref[...] = (residual + branch + shifts[4:5, :]).astype(BF)
    cot_wide = cotangent.astype(F32)

    def back(grad, unit, inverse, row):
        scaled = grad * gains[row : row + 1, :]
        inner = (
            scaled
            - jnp.mean(scaled, axis=-1, keepdims=True)
            - unit * jnp.mean(scaled * unit, axis=-1, keepdims=True)
        )
        sums_ref[row : row + 1, :] += column_sum(grad * unit)
        sums_ref[row + 2 : row + 3, :] += column_sum(grad)
        return inner * inverse

    residual_grad = cot_wide + back(dense_grad, dense_unit, dense_inverse, 2)
    residual_grad_ref[...] = residual_grad
    attended_grad = back(residual_grad, post_unit, post_inverse, 1)
    sums_ref[5:6, :] += column_sum(attended_grad)
    sums_ref[6:7, :] += column_sum(cot_wide)
    attended_grad = attended_grad.astype(BF)
    attended_grad_ref[...] = attended_grad
    for result, matrix in zip(scaled_grads, out_weights):
        result[...] = dot(attended_grad, matrix[...], COLUMN_PAIRS).astype(BF)


def middle_pass(
    chunk, rows, cotangent, scaled, out_weights, feed, gains, shifts, mid_gain, mid_shifts
):
    slots = len(scaled)
    tokens, width = rows.shape
    part = scaled[0].shape[1]
    hidden = mid_gain.shape[1]
    block = min(256, tokens)

    def tiles(columns):
        return pl.BlockSpec((block, columns), lambda i: (i, 0))

    def whole(array):
        return pl.BlockSpec(array.shape, lambda i: (0, 0), pipeline_mode=pl.Buffered(1))

    call = pl.pallas_call(
        functools.partial(middle_kernel, slots, chunk),
        grid=(tokens // block,),
        in_specs=[tiles(width), tiles(width)]
        + [tiles(part)] * slots
        + [whole(item) for item in (*out_weights, feed, gains, shifts, mid_gain, mid_shifts)],
        out_specs=[tiles(width)] * 4
        + [tiles(hidden)] * 2
        + [pl.BlockSpec((8, width), lambda i: (0, 0)), pl.BlockSpec((8, hidden), lambda i: (0, 0))]
        + [tiles(part)] * slots,
        out_shape=[
            jax.ShapeDtypeStruct((tokens, width), BF),
            jax.ShapeDtypeStruct((tokens, width), F32),
            jax.ShapeDtypeStruct((tokens, width), BF),
            jax.ShapeDtypeStruct((tokens, width), BF),
            jax.ShapeDtypeStruct((tokens, hidden), BF),
            jax.ShapeDtypeStruct((tokens, hidden), BF),
            jax.ShapeDtypeStruct((8, width), F32),
            jax.ShapeDtypeStruct((8, hidden), F32),
        ]
        + [jax.ShapeDtypeStruct((tokens, part), BF)] * slots,
        scratch_shapes=[pltpu.VMEM((block, hidden), F32)] * 3,
        compiler_params=pltpu.CompilerParams(vmem_limit_bytes=60 * 2**20),
        name="middle_pass",
    )
    return call(rows, cotangent, *scaled, *out_weights, feed, gains, shifts, mid_gain, mid_shifts)


def feed_grads_kernel(groups, *refs):
    middles, hidden_grads = refs[:groups], refs[groups : 2 * groups]
    cots, denses = refs[2 * groups : 3 * groups], refs[3 * groups : 4 * groups]
    result = refs[4 * groups]
    width = cots[0].shape[1]
    for at, lefts, rights in ((0, middles, cots), (width, hidden_grads, denses)):
        total = functools.reduce(
            jnp.add, [dot(a[...], b[...], ROW_PAIRS) for a, b in zip(lefts, rights)]
        )
        result[:, at : at + width] = total.astype(BF)


def feed_grads(middles, hidden_grads, cots, denses):
    groups = len(middles)
    hidden, width = middles[0].shape[1], cots[0].shape[1]
    block = min(256, hidden)

    def columns(array):
        return pl.BlockSpec((array.shape[0], block), lambda i: (0, i))

    def whole(array):
        return pl.BlockSpec(array.shape, lambda i: (0, 0), pipeline_mode=pl.Buffered(1))

    return pl.pallas_call(
        functools.partial(feed_grads_kernel, groups),
        grid=(hidden // block,),
        in_specs=[columns(item) for item in (*middles, *hidden_grads)]
        + [whole(item) for item in (*cots, *denses)],
        out_specs=pl.BlockSpec((block, 2 * width), lambda i: (i, 0)),
        out_shape=jax.ShapeDtypeStruct((hidden, 2 * width), BF),
        compiler_params=pltpu.CompilerParams(vmem_limit_bytes=56 * 2**20),
        name="feed_grads",
    )(*middles, *hidden_grads, *cots, *denses)


def shards(
    slots,
    short_rows,
    medium_rows,
    long_rows,
    short_len,
    medium_len,
    long_len,
    short_cotangent,
    medium_cotangent,
    long_cotangent,
    norm_gains,
    norm_shifts,
    head_weights,
    head_biases,
    head_scale,
    out_weight,
    up_weight,
    mid_gain,
    mid_shifts,
    down_weight,
):
    shapes = tuple((item.shape for item in (short_rows, medium_rows, long_rows)))
    width = short_rows.shape[2]
    part = head_weights.shape[2]
    pairs = part // LANES
    me = lax.axis_index("head").astype(jnp.int32).reshape(1)

    def fetch(value, slot):
        return lax.ppermute(value, "head", [((d + slot) % slots, d) for d in range(slots)])

    def deliver(value, slot):
        return lax.ppermute(value, "head", [(d, (d + slot) % slots) for d in range(slots)])

    def spread(own, move):
        return [own[slot] if slot == 0 else move(own[slot], slot) for slot in range(slots)]

    def grouped(short, medium, long):
        return [
            long.reshape(-1, width),
            jnp.concatenate([short.reshape(-1, width), medium.reshape(-1, width)], 0),
        ]

    inputs = grouped(short_rows, medium_rows, long_rows)
    cots = grouped(short_cotangent, medium_cotangent, long_cotangent)
    short_tokens = shapes[0][0] * shapes[0][1]
    spans = tuple(shape[1] * slots for shape in shapes)
    counts = tuple(shape[0] for shape in shapes)
    long_job = (long_len, counts[2], spans[2], 0)
    short_job = (short_len, counts[0], spans[0], 0)
    medium_job = (medium_len, counts[1], spans[1], short_tokens // shapes[1][1])
    jobs = ([long_job], [short_job, medium_job])

    weights = (
        head_weights.reshape(3, width, pairs, LANES).transpose(1, 2, 0, 3).reshape(width, 3 * part)
    )
    biases = (
        jnp.stack([head_biases[0], jnp.zeros_like(head_biases[0]), head_biases[1]])
        .reshape(3, pairs, LANES)
        .transpose(1, 0, 2)
        .reshape(3 * part)
    )
    scale_lanes = jnp.repeat(head_scale, HEAD).reshape(1, part)

    share = up_weight.shape[0]
    batches = mid_gain.shape[0] // (slots * share)
    own_feed = jnp.stack([up_weight, down_weight])
    feed_slots = [own_feed] + [fetch(own_feed, slot) for slot in range(1, slots)]
    feed = lax.all_gather(
        jnp.stack(feed_slots, 1).reshape(2 * slots * share, width), "batch", axis=0, tiled=True
    )

    def turn(values, places):
        return jnp.roll(values, places, axis=1)

    mid_rows = jnp.concatenate([mid_gain[None], mid_shifts], 0).reshape(3, slots, batches, share)
    mid_rows = turn(mid_rows, -me[0]).transpose(0, 2, 1, 3).reshape(3, -1)

    units, inverses, normed_slots = [], [], []
    for rows in inputs:
        value, unit, inverse = normalize(rows.astype(F32), norm_gains[0], norm_shifts[0])
        low = value.astype(BF)
        if normed_slots:
            low, normed_slots[-1] = lax.optimization_barrier((low, normed_slots[-1]))
        normed_slots.append([low] + [fetch(low, slot) for slot in range(1, slots)])
        units.append(unit)
        inverses.append(inverse)
    out_weights, _ = lax.optimization_barrier((out_weight, normed_slots[-1]))
    out_weights = [out_weight] + [deliver(out_weights, slot) for slot in range(1, slots)]

    qkv, saved, scaled = [], [], []
    for group in range(2):
        projected = [(dot(rows, weights) + biases).astype(BF) for rows in normed_slots[group]]
        qkv.append(projected)
        outs, totals = [], []
        for job in jobs[group]:
            outs, log_total = attend_forward(me, job[0], projected, scale_lanes, outs, *job[1:])
            totals.append(log_total)
        saved.append((outs, totals))
        scaled.append(spread(outs, deliver))

    outputs, residual_grads, grad_slots, sums, mid_sums, out_grads = [], [], [], [], [], []
    middles, hidden_grads, denses = [], [], []
    for group in range(2):
        results = middle_pass(
            slots * share,
            inputs[group],
            cots[group],
            scaled[group],
            out_weights,
            feed,
            norm_gains,
            norm_shifts,
            mid_rows[:1],
            mid_rows[1:],
        )
        outputs.append(results[0])
        residual_grads.append(results[1])
        denses.append(results[2])
        middles.append(results[4])
        hidden_grads.append(results[5])
        sums.append(results[6])
        mid_sums.append(results[7])
        grad_slots.append(spread(results[8:], fetch))
        terms = [dot(rows, results[3], ROW_PAIRS) for rows in scaled[group]]
        out_grads = terms if not out_grads else [a + b for a, b in zip(out_grads, terms)]
    both = feed_grads(middles, hidden_grads, cots, denses)
    out_grad = out_grads[0]
    for slot in range(1, slots):
        out_grad = out_grad + fetch(out_grads[slot].astype(BF), slot).astype(F32)
    grad_slots, both = lax.optimization_barrier((grad_slots, both))
    both = lax.psum_scatter(both, "batch", scatter_dimension=0, tiled=True)

    weight_grad = jnp.zeros((width, 3 * part), F32)
    bias_sums = jnp.zeros((8, part), F32)
    normed_grads = []
    for group in range(2):
        qkv_grad = []
        outs, totals = saved[group]
        for job, log_total in zip(jobs[group], totals):
            qkv_grad, back_sums = attend_backward(
                me,
                job[0],
                qkv[group],
                outs,
                grad_slots[group],
                scale_lanes,
                log_total,
                qkv_grad,
                *job[1:],
            )
            bias_sums = bias_sums + jnp.sum(back_sums, axis=0).transpose(1, 0, 2).reshape(8, part)
        terms = [dot(piece, weights, COLUMN_PAIRS).astype(BF) for piece in qkv_grad]
        terms = spread(terms, deliver)
        normed_grad = terms[0].astype(F32)
        for term in terms[1:]:
            normed_grad = normed_grad + term.astype(F32)
        normed_grads.append(normed_grad)
        for rows, piece in zip(normed_slots[group], qkv_grad):
            weight_grad = weight_grad + dot(rows, piece, ROW_PAIRS)

    weight_grad, out_grad = weight_grad.astype(BF), out_grad.astype(BF)
    weight_grad, out_grad, both = lax.optimization_barrier((weight_grad, out_grad, both))
    summed_weight, summed_out = lax.psum((weight_grad, out_grad), "batch")
    both = both.reshape(slots, share, 2 * width)
    both_grads = both[0].astype(F32)
    for slot in range(1, slots):
        both_grads = both_grads + deliver(both[slot], slot).astype(F32)
    grad_head_weights = (
        summed_weight.reshape(width, pairs, 3, LANES)
        .transpose(2, 0, 1, 3)
        .reshape(3, width, part)
        .astype(F32)
    )

    grads = []
    first_gain = first_shift = jnp.zeros((1, width), F32)
    for group in range(2):
        inner, gain_term, shift_term = normalize_back(
            normed_grads[group], units[group], inverses[group], norm_gains[0]
        )
        first_gain = first_gain + gain_term
        first_shift = first_shift + shift_term
        grads.append((residual_grads[group] + inner).astype(BF))
    sums = sums[0] + sums[1]
    mid_terms = (mid_sums[0] + mid_sums[1])[:3].reshape(3, batches, slots, share)
    mid_terms = turn(mid_terms.transpose(0, 2, 1, 3), me[0])
    shared = jnp.concatenate(
        [
            first_gain.reshape(-1),
            sums[1:3].reshape(-1),
            first_shift.reshape(-1),
            sums[3:7].reshape(-1),
            mid_terms.reshape(-1),
        ]
    )
    shared_size = shared.shape[0]
    own_sums = lax.dynamic_update_slice(
        jnp.zeros((slots, 3 * part), F32), bias_sums[:3].reshape(1, -1), (me[0], jnp.int32(0))
    )
    summed = sum_everywhere(
        jnp.concatenate([shared, own_sums.reshape(-1)]), (("head", slots), ("batch", batches))
    )
    norm_sums = summed[: 8 * width].reshape(8, width)
    mid_terms = summed[8 * width : shared_size].reshape(3, -1)
    own_sums = lax.dynamic_slice(
        summed[shared_size:].reshape(slots, 3 * part), (me[0], jnp.int32(0)), (1, 3 * part)
    ).reshape(3, part)
    return (
        outputs[1][:short_tokens].reshape(shapes[0]),
        outputs[1][short_tokens:].reshape(shapes[1]),
        outputs[0].reshape(shapes[2]),
        grads[1][:short_tokens].reshape(shapes[0]),
        grads[1][short_tokens:].reshape(shapes[1]),
        grads[0].reshape(shapes[2]),
        norm_sums[:3],
        norm_sums[3:],
        grad_head_weights,
        own_sums[:2],
        jnp.sum(own_sums[2].reshape(-1, HEAD), axis=1),
        summed_out.astype(F32),
        both_grads[:, width:],
        mid_terms[0],
        jnp.stack([mid_terms[2], mid_terms[1]]),
        both_grads[:, :width],
    )


def solution(mesh):
    in_specs = (
        P("batch", "head", None),
        P("batch", "head", None),
        P("batch", "head", None),
        P("batch"),
        P("batch"),
        P("batch"),
        P("batch", "head", None),
        P("batch", "head", None),
        P("batch", "head", None),
        P(),
        P(),
        P(None, None, "head"),
        P(None, "head"),
        P("head"),
        P("head", None),
        P(("head", "batch"), None),
        P(),
        P(),
        P(("head", "batch"), None),
    )
    out_specs = (
        P("batch", "head", None),
        P("batch", "head", None),
        P("batch", "head", None),
        P("batch", "head", None),
        P("batch", "head", None),
        P("batch", "head", None),
        P(),
        P(),
        P(None, None, "head"),
        P(None, "head"),
        P("head"),
        P("head", None),
        P(("head", "batch"), None),
        P(),
        P(),
        P(("head", "batch"), None),
    )
    return jax.shard_map(
        functools.partial(shards, mesh.shape["head"]),
        mesh=mesh,
        in_specs=in_specs,
        out_specs=out_specs,
        check_vma=False,
    )
```

time: 1970 us -> 722 us (0.37)
  matrix products: 879 us -> 91.5 us
  other arithmetic: 427 us -> 28.5 us
  Pallas kernels: 0 us -> 365 us
  waiting for transfers between devices: 429 us -> 162 us
  local copies, waits for them, and re-layouts: 138 us -> 36.1 us
  blocking collectives: 38.2 us -> 0 us
  loops' own time: 34.3 us -> 0 us
    dot_general x98 -> x16, matrix products: 879 us -> 91.5 us  [dot(): return lax.dot_general(a, b, dims, preferred_element_type=F32)]
    pallas_call x0 -> x9, Pallas kernels: none -> 365 us  [the longest x2 151 us: middle_pass(): call(rows, cotangent, *scaled, *out_weights, feed, gains, shifts, mid_gai...]
    reduce_scatter x7 -> x1, waiting for transfers between devices: 323 us -> 0.01 us  [shards(): both = lax.psum_scatter(both, 'batch', scatter_dimension=0, tiled=True)]
    convert_element_type x23 -> x4, other arithmetic: 171 us -> 11.8 us  [the longest x1 4.89 us: shards(): grads.append((residual_grads[group] + inner).astype(BF))]
    reduce_sum x23 -> x2, other arithmetic: 139 us -> 0.64 us  [the longest x1 0.63 us: shards(): jnp.sum(own_sums[2].reshape(-1, HEAD), axis=1)]
    all_gather x8 -> x1, waiting for transfers between devices: 103 us -> 0.01 us  [shards(): lax.all_gather(jnp.stack(feed_slots, 1).reshape(2 * slots * share, width)...]
    psum x2 -> x1, waiting for transfers between devices: 0.01 us -> 84.6 us  [shards(): summed_weight, summed_out = lax.psum((weight_grad, out_grad), 'batch')]
    ppermute x0 -> x17, waiting for transfers between devices: none -> 77.4 us  [the longest x6 46.5 us: fetch(): lax.ppermute(value, 'head', [((d + slot) % slots, d) for d in range(slots)])]
  transfers between devices with their start and end apart: 17 -> 20, of which waited for: 6 -> 10; matrix products, arithmetic and copies ran while one was open for 40% -> 20% of each run, Pallas kernels for 0% -> 51%
where the time goes in v1:
time: 722 us; the launch traced here: 720 us
  Pallas kernels  365 us (51%)
  waiting for transfers between devices  162 us (22%)
  matrix products  91.5 us (13%)
  local copies, waits for them, and re-layouts  36.1 us (5%)
  other arithmetic  28.5 us (4%)
  starting transfers between devices  21 us (3%)
  between operations  16 us (2%)
    pallas_call x2, Pallas kernels, middle_pass(): call(rows, cotangent, *scaled, *out_weights, feed, gains, shifts, mid_gai...  151 us
    pallas_call x3, Pallas kernels, attend_backward(): call(me, lengths, *qkv, *outs, *grads, scale_lanes, log_total, *kept)  108 us
    dot_general x16, matrix products, dot(): return lax.dot_general(a, b, dims, preferred_element_type=F32)  91.5 us
    psum x1, waiting for transfers between devices, shards(): summed_weight, summed_out = lax.psum((weight_grad, out_grad), 'batch')  84.6 us
    pallas_call x3, Pallas kernels, attend_forward(): *outs, log_total = call(me, lengths, *qkv, scale_lanes, *kept)  62.5 us
    ppermute x6, waiting for transfers between devices, fetch(): lax.ppermute(value, 'head', [((d + slot) % slots, d) for d in range(slots)])  46.5 us
    pallas_call x1, Pallas kernels, feed_grads(): pl.pallas_call(functools.partial(feed_grads_kernel, groups), grid=(hidden...  43.6 us
    ppermute x6, waiting for transfers between devices, deliver(): lax.ppermute(value, 'head', [(d, (d + slot) % slots) for d in range(slots)])  18.6 us
  transfers between devices with their start and end apart: 20, of which 10 were waited for; matrix products, arithmetic and copies ran while one was open for 20% of the time, Pallas kernels for 51%

profile of v1, /device:TPU:0, one launch (start us, length us, event | category | flops | bytes accessed | tf_op | source)
XLA Modules:
  0.0 720.3 jit_solution(14314177497288390655)
XLA Ops:
  11.5 11.9 %collective-permute-done.4 = bf16[2,128,1024]{2,1,0:T(8,128)(2,1)S(1)} collective-permute-done((bf16[2,128,1024]{2,1,0:T(8,128)(2,1)S(1)}, bf16[2,128,1024]{2,1,0:T(8,128)(2,1)S(1)}, u32[]{:S(2)}, u32[]{:S(2)}) %collective-permute-start.4) | collective-permute-done | bytes 524320 | tf_op jit(solution)/shard_map/ppermute | solution.py:494
  45.0 34.6 %collective-permute-done = bf16[1024,1024]{1,0:T(8,128)(2,1)S(1)} collective-permute-done((bf16[1024,1024]{1,0:T(8,128)(2,1)}, bf16[1024,1024]{1,0:T(8,128)(2,1)S(1)}, u32[]{:S(2)}, u32[]{:S(2)}) %collective-permute-start) | collective-permute-done | bytes 2097184 | tf_op jit(solution)/shard_map/ppermute | solution.py:494
  81.0 7.8 %add_convert_fusion.2.refs_0_ = bf16[1024,1536]{1,0:T(8,128)(2,1)} fusion(bf16[1024,1024]{1,0:T(8,128)(2,1)} %get-tuple-element.74, bf16[1024,1536]{0,1:T(8,128)(2,1)} %bitcast.126, f32[1536]{0:T(1024)S(1)} %add.162), kind=kOutput, calls=%fused_computation.2 | convolution fusion | flops 3224371200 | bytes 8394752 | tf_op jit(solution)/shard_map/dot_general | solution.py:25
  93.6 36.1 %attend_forward.5 = (bf16[1024,512]{1,0:T(8,128)(2,1)}, bf16[1024,512]{1,0:T(8,128)(2,1)}, f32[4,1,2,2048]{3,2,1,0:T(2,128)}) custom-call(s32[1]{0:T(128)} %bitcast.4.me_ref, s32[1]{0:T(128)S(6)} %copy.80.len_ref, bf16[1024,1536]{1,0:T(8,128)(2,1)} %add_convert_fusion.2.refs_0_, bf16[1024,1536]{1,0:T(8,128)(2,1)} %add_convert_fusion.1.refs_1_, ...), custom_call_target="tpu_custom_call" | custom-call | tf_op jit(solution)/shard_map/attend_forward/pallas_call | solution.py:227
  130.7 6.4 add_convert_fusion.4.refs_0_
  138.2 6.4 add_convert_fusion.3.refs_1_
  144.7 12.5 %attend_forward.3 = (bf16[1024,512]{1,0:T(8,128)(2,1)}, bf16[1024,512]{1,0:T(8,128)(2,1)}, f32[4,2,2,512]{3,2,1,0:T(2,128)}) custom-call(s32[1]{0:T(128)} %bitcast.4.me_ref, s32[2]{0:T(128)} %len_ref.7, bf16[1024,1536]{1,0:T(8,128)(2,1)} %add_convert_fusion.4.refs_0_, bf16[1024,1536]{1,0:T(8,128)(2,1)} %add_convert_fusion.3.refs_1_, ...), custom_call_target="tpu_custom_call" | custom-call | tf_op jit(solution)/shard_map/attend_forward/pallas_call | solution.py:227
  157.2 13.8 %attend_forward.4 = (bf16[1024,512]{1,0:T(8,128)(2,1)}, bf16[1024,512]{1,0:T(8,128)(2,1)}, f32[4,1,2,1024]{3,2,1,0:T(2,128)}) custom-call(s32[1]{0:T(128)} %bitcast.4.me_ref, s32[1]{0:T(128)S(6)} %copy.79.len_ref, bf16[1024,1536]{1,0:T(8,128)(2,1)} %add_convert_fusion.4.refs_0_, ...), custom_call_target="tpu_custom_call", output_to_operand_aliasing={{0}: (5, {}), {1}: (6, {})} | custom-call | tf_op jit(solution)/shard_map/attend_forward/pallas_call | solution.py:227
  178.7 80.5 %middle_pass.3 = (bf16[1024,1024]{1,0:T(8,128)(2,1)}, f32[1024,1024]{1,0:T(8,128)}, bf16[1024,1024]{1,0:T(8,128)(2,1)}, bf16[1024,1024]{1,0:T(8,128)(2,1)}, bf16...) custom-call(bf16[1024,1024]{1,0:T(8,128)(2,1)} %bitcast.107, ...), custom_call_target="tpu_custom_call" | custom-call | tf_op jit(solution)/shard_map/middle_pass/pallas_call | solution.py:427
  260.2 70.5 %middle_pass.2 = (bf16[1024,1024]{1,0:T(8,128)(2,1)}, f32[1024,1024]{1,0:T(8,128)}, bf16[1024,1024]{1,0:T(8,128)(2,1)}, bf16[1024,1024]{1,0:T(8,128)(2,1)}, bf16...) custom-call(bf16[1024,1024]{1,0:T(8,128)(2,1)} %pad_maximum_fusion.r, ...), custom_call_target="tpu_custom_call" | custom-call | tf_op jit(solution)/shard_map/middle_pass/pallas_call | solution.py:427
  331.9 43.6 %feed_grads.1 = bf16[4096,2048]{1,0:T(8,128)(2,1)} custom-call(bf16[1024,4096]{1,0:T(8,128)(2,1)} %get-tuple-element.84.refs_0_, bf16[1024,4096]{1,0:T(8,128)(2,1)} %get-tuple-element.85.refs_1_, bf16[1024,4096]{1,0:T(8,128)(2,1)} %get-tuple-element.86.refs_2_, bf16[1024,4096]{1,0:T(8,128)(2,1)} %get-tuple-element.87.refs_3_, bf16[1024,1024]{1,0:T(8,128)(2,1)} %bitcast.124, ...), custom_call_target="tpu_custom_call" | custom-call | tf_op jit(solution)/shard_map/feed_grads/pallas_call | solution.py:453
  392.0 17.9 %attend_backward.3 = (bf16[1024,1536]{1,0:T(8,128)(2,1)}, bf16[1024,1536]{1,0:T(8,128)(2,1)}, f32[2,4,8,128]{3,2,1,0:T(8,128)}) custom-call(s32[1]{0:T(128)} %bitcast.4.me_ref, s32[2]{0:T(128)} %len_ref.7, bf16[1024,1536]{1,0:T(8,128)(2,1)} %add_convert_fusion.4.refs_0_, bf16[1024,1536]{1,0:T(8,128)(2,1)} %add_convert_fusion.3.refs_1_, ...), custom_call_target="tpu_custom_call" | custom-call | tf_op jit(solution)/shard_map/attend_backward/pallas_call | solution.py:262
  409.9 23.5 %attend_backward.4 = (bf16[1024,1536]{1,0:T(8,128)(2,1)}, bf16[1024,1536]{1,0:T(8,128)(2,1)}, f32[1,4,8,128]{3,2,1,0:T(8,128)}) custom-call(s32[1]{0:T(128)} %bitcast.4.me_ref, s32[1]{0:T(128)S(6)} %copy.79.len_ref, bf16[1024,1536]{1,0:T(8,128)(2,1)} %add_convert_fusion.4.refs_0_, ...), custom_call_target="tpu_custom_call", output_to_operand_aliasing={{0}: (10, {}), {1}: (11, {})} | custom-call | tf_op jit(solution)/shard_map/attend_backward/pallas_call | solution.py:262
  433.4 6.6 convolution_convert_fusion.2
  441.2 66.7 %attend_backward.5 = (bf16[1024,1536]{1,0:T(8,128)(2,1)}, bf16[1024,1536]{1,0:T(8,128)(2,1)}, f32[1,4,8,128]{3,2,1,0:T(8,128)}) custom-call(s32[1]{0:T(128)} %bitcast.4.me_ref, s32[1]{0:T(128)S(6)} %copy.80.len_ref, bf16[1024,1536]{1,0:T(8,128)(2,1)} %add_convert_fusion.2.refs_0_, bf16[1024,1536]{1,0:T(8,128)(2,1)} %add_convert_fusion.1.refs_1_, ...), custom_call_target="tpu_custom_call" | custom-call | tf_op jit(solution)/shard_map/attend_backward/pallas_call | solution.py:262
  507.9 6.5 convolution_convert_fusion
  515.6 6.9 fusion.49
  522.6 7.2 fusion.50
  529.8 7.3 %fusion.48 = f32[1024,1536]{1,0:T(8,128)} fusion(bf16[1024,1024]{1,0:T(8,128)(2,1)} %get-tuple-element.74, bf16[1024,1536]{1,0:T(8,128)(2,1)S(1)} %copy-done.36), kind=kOutput, calls=%fused_computation.102 | convolution fusion | flops 3221225472 | bytes 11534336 | tf_op jit(solution)/shard_map/dot_general | solution.py:25
  537.1 9.3 %add_convert_fusion = bf16[1024,1536]{1,0:T(8,128)(2,1)} fusion(f32[1024,1536]{1,0:T(8,128)} %fusion.50, f32[1024,1536]{1,0:T(8,128)} %fusion.48, f32[1024,1536]{1,0:T(8,128)S(1)} %fusion.49, bf16[1024,1024]{1,0:T(8,128)(2,1)} %collective-permute-done.1, bf16[1024,1536]{1,0:T(8,128)(2,1)S(1)} %copy-done.15), kind=kOutput, calls=%fused_computation | convolution fusion | flops 3227516928 | bytes 27262976 | tf_op jit(solution)/shard_map/dot_general | solution.py:25
  550.0 7.7 %collective-permute-done.9 = bf16[1024,1024]{1,0:T(8,128)(2,1)} collective-permute-done((bf16[1024,1024]{1,0:T(8,128)(2,1)}, bf16[1024,1024]{1,0:T(8,128)(2,1)}, u32[]{:S(2)}, u32[]{:S(2)}) %collective-permute-start.9) | collective-permute-done | bytes 2097184 | tf_op jit(solution)/shard_map/ppermute | solution.py:497
  564.1 7.4 %fusion.28 = (f32[1024]{0:T(1024)S(1)}, f32[1024]{0:T(1024)S(1)}, f32[1024]{0:T(1024)S(1)}, f32[1024]{0:T(1024)S(1)}, bf16[1,1024,1024]{2,1,0:T(8,128)(2,1)}) fusion(bf16[1024,1024]{1,0:T(8,128)(2,1)} %collective-permute-done.8, bf16[1024,1024]{1,0:T(8,128)(2,1)S(1)} %convolution_convert_fusion.3, f32[1024]{0:T(1024)S(1)} %get-tuple-element.163, ...), kind=kLoop, calls=%fused_computation.37 | loop fusion | flops 30404608 | bytes 18919424 | tf_op jit(solution)/shard_map/reduce_sum | solution.py:42
  611.2 9.4 %collective-permute-done.16 = bf16[128,2048]{1,0:T(8,128)(2,1)S(1)} collective-permute-done((bf16[128,2048]{1,0:T(8,128)(2,1)S(1)}, bf16[128,2048]{1,0:T(8,128)(2,1)S(1)}, u32[]{:S(2)}, u32[]{:S(2)}) %collective-permute-start.16) | collective-permute-done | bytes 524320 | tf_op jit(solution)/shard_map/ppermute | solution.py:497
  621.9 84.6 %all-reduce.3.cloned.1.call-done = (bf16[3,1024,512]{1,2,0:T(8,128)(2,1)}, bf16[512,1024]{1,0:T(8,128)(2,1)}) async-done(((bf16[3,1024,512]{1,2,0:T(8,128)(2,1)}, bf16[512,1024]{1,0:T(8,128)(2,1)}), (bf16[3,1024,512]{1,2,0:T(8,128)(2,1)}, bf16[512,1024]{1,0:T(8,128)(2,1)})) %all-reduce.3.cloned.1.call-update) | async-done | bytes 4194320 | tf_op jit(solution)/shard_map/psum | solution.py:628
  (204 shorter events, 119.0 us)
Async XLA Ops:
  7.2 171.5 %all-gather.2.cloned.1.call-start = ((), (), s32[]{:S(2)}) async-start(), calls=%async_computation.1 | async-start | bytes 17825792 | tf_op jit(solution)/shard_map/all_gather | solution.py:533
  7.2 18.2 %copy-start.2 = (bf16[1,512,1024]{2,1,0:T(8,128)(2,1)S(1)}, bf16[1,512,1024]{2,1,0:T(8,128)(2,1)}, u32[]{:S(2)}) copy-start(bf16[1,512,1024]{2,1,0:T(8,128)(2,1)} %param.22) | copy-start | bytes 3145732
  8.4 15.0 %collective-permute-start.4 = (bf16[2,128,1024]{2,1,0:T(8,128)(2,1)S(1)}, bf16[2,128,1024]{2,1,0:T(8,128)(2,1)S(1)}, u32[]{:S(2)}, u32[]{:S(2)}) collective-permute-start(bf16[2,128,1024]{2,1,0:T(8,128)(2,1)S(1)} %get-tuple-element.150), channel_id=1, source_target_pairs={{16,0},{0,16},{17,1},{1,17},{18,2},{2,18},{19,3},{3,19},{20,4},{4,... | collective-permute-start | bytes 1572872 | tf_op jit(solution)/shard_map/ppermute | solution.py:494
  24.6 559.4 %reduce-scatter.2.cloned.1.call-start = ((), (), s32[]{:S(2)}) async-start(), calls=%async_computation.2 | async-start | bytes 17825792 | tf_op jit(solution)/shard_map/reduce_scatter | solution.py:596
  32.5 47.0 %collective-permute-start = (bf16[1024,1024]{1,0:T(8,128)(2,1)}, bf16[1024,1024]{1,0:T(8,128)(2,1)S(1)}, u32[]{:S(2)}, u32[]{:S(2)}) collective-permute-start(bf16[1024,1024]{1,0:T(8,128)(2,1)} %get-tuple-element.74), channel_id=1, source_target_pairs={{16,0},{0,16},{17,1},{1,17},{18,2},{2,18},{19,3},{3,19},{20,4},{4,... | collective-permute-start | bytes 6291464 | tf_op jit(solution)/shard_map/ppermute | solution.py:494
  79.6 57.6 %collective-permute-start.1 = (bf16[1024,1024]{1,0:T(8,128)(2,1)}, bf16[1024,1024]{1,0:T(8,128)(2,1)}, u32[]{:S(2)}, u32[]{:S(2)}) collective-permute-start(bf16[1024,1024]{1,0:T(8,128)(2,1)} %get-tuple-element.67), channel_id=1, source_target_pairs={{16,0},{0,16},{17,1},{1,17},{18,2},{2,18},{19,3},{3,19},{20,4},{4,... | collective-permute-start | bytes 6291464 | tf_op jit(solution)/shard_map/ppermute | solution.py:494
  129.8 47.5 %collective-permute-start.5 = (bf16[1024,512]{1,0:T(8,128)(2,1)}, bf16[1024,512]{1,0:T(8,128)(2,1)}, u32[]{:S(2)}, u32[]{:S(2)}) collective-permute-start(bf16[1024,512]{1,0:T(8,128)(2,1)} %get-tuple-element.77.refs_3_), channel_id=1, source_target_pairs={{0,16},{16,0},{1,17},{17,1},{2,18},{18,2},{3,19},{19,3},{4,20},{20... | collective-permute-start | bytes 3145736 | tf_op jit(solution)/shard_map/ppermute | solution.py:497
  137.1 41.6 %collective-permute-start.3 = (bf16[512,1024]{1,0:T(8,128)(2,1)S(1)}, bf16[512,1024]{1,0:T(8,128)(2,1)}, u32[]{:S(2)}, u32[]{:S(2)}) collective-permute-start(bf16[512,1024]{1,0:T(8,128)(2,1)S(1)} %copy-done.12), channel_id=1, source_target_pairs={{0,16},{16,0},{1,17},{17,1},{2,18},{18,2},{3,19},{19,3},{4,20},{20... | collective-permute-start | bytes 3145736 | tf_op jit(solution)/shard_map/ppermute | solution.py:497
  157.2 14.9 %copy-start.30 = (f32[2,4096]{1,0:T(2,128)S(1)}, f32[2,4096]{1,0:T(2,128)}, u32[]{:S(2)}) copy-start(f32[2,4096]{1,0:T(2,128)} %param.38) | copy-start | bytes 98308
  157.2 16.3 %copy-start.4 = (bf16[2,256,1024]{2,1,0:T(8,128)(2,1)S(1)}, bf16[2,256,1024]{2,1,0:T(8,128)(2,1)}, u32[]{:S(2)}) copy-start(bf16[2,256,1024]{2,1,0:T(8,128)(2,1)} %param.21) | copy-start | bytes 3145732
  171.1 89.1 %collective-permute-start.2 = (bf16[1024,512]{1,0:T(8,128)(2,1)}, bf16[1024,512]{1,0:T(8,128)(2,1)}, u32[]{:S(2)}, u32[]{:S(2)}) collective-permute-start(bf16[1024,512]{1,0:T(8,128)(2,1)} %get-tuple-element.71.refs_3_), channel_id=1, source_target_pairs={{0,16},{16,0},{1,17},{17,1},{2,18},{18,2},{3,19},{19,3},{4,20},{20... | collective-permute-start | bytes 3145736 | tf_op jit(solution)/shard_map/ppermute | solution.py:497
  259.2 116.3 %collective-permute-start.6 = (bf16[1024,512]{1,0:T(8,128)(2,1)}, bf16[1024,512]{1,0:T(8,128)(2,1)}, u32[]{:S(2)}, u32[]{:S(2)}) collective-permute-start(bf16[1024,512]{1,0:T(8,128)(2,1)} %get-tuple-element.81), channel_id=1, source_target_pairs={{16,0},{0,16},{17,1},{1,17},{18,2},{2,18},{19,3},{3,19},{20,4},{4,... | collective-permute-start | bytes 3145736 | tf_op jit(solution)/shard_map/ppermute | solution.py:494
  330.7 44.8 %collective-permute-start.7 = (bf16[1024,512]{1,0:T(8,128)(2,1)}, bf16[1024,512]{1,0:T(8,128)(2,1)S(1)}, u32[]{:S(2)}, u32[]{:S(2)}) collective-permute-start(bf16[1024,512]{1,0:T(8,128)(2,1)} %get-tuple-element.83), channel_id=1, source_target_pairs={{16,0},{0,16},{17,1},{1,17},{18,2},{2,18},{19,3},{3,19},{20,4},{4,... | collective-permute-start | bytes 3145736 | tf_op jit(solution)/shard_map/ppermute | solution.py:494
  376.5 330.0 %all-reduce.3.cloned.1.call-start = ((), (), s32[]{:S(2)}) async-start(), calls=%async_computation.3 | async-start | bytes 8388608 | tf_op jit(solution)/shard_map/psum | solution.py:628
  384.0 188.3 %collective-permute-start.15 = (bf16[512,1024]{1,0:T(8,128)(2,1)}, bf16[512,1024]{1,0:T(8,128)(2,1)S(1)}, u32[]{:S(2)}, u32[]{:S(2)}) collective-permute-start(bf16[512,1024]{1,0:T(8,128)(2,1)} %add_convert_fusion.6), channel_id=1, source_target_pairs={{16,0},{0,16},{17,1},{1,17},{18,2},{2,18},{19,3},{3,19},{20,4},{4,... | collective-permute-start | bytes 3145736 | tf_op jit(solution)/shard_map/ppermute | solution.py:494
  409.9 23.5 %copy-start.17 = (bf16[1024,4,3,128]{0,3,2,1:T(8,128)(2,1)S(1)}, bf16[1024,4,3,128]{0,3,2,1:T(8,128)(2,1)}, u32[]{:S(2)}) copy-start(bf16[1024,4,3,128]{0,3,2,1:T(8,128)(2,1)} %copy.50) | copy-start | bytes 9437188
  440.0 124.1 %collective-permute-start.8 = (bf16[1024,1024]{1,0:T(8,128)(2,1)}, bf16[1024,1024]{1,0:T(8,128)(2,1)}, u32[]{:S(2)}, u32[]{:S(2)}) collective-permute-start(bf16[1024,1024]{1,0:T(8,128)(2,1)} %convolution_convert_fusion.2), channel_id=1, source_target_pairs={{0,16},{16,0},{1,17},{17,1},{2,18},{18,2},{3,19},{19,3},{4,20},{20... | collective-permute-start | bytes 6291464 | tf_op jit(solution)/shard_map/ppermute | solution.py:497
  514.4 43.4 %collective-permute-start.9 = (bf16[1024,1024]{1,0:T(8,128)(2,1)}, bf16[1024,1024]{1,0:T(8,128)(2,1)}, u32[]{:S(2)}, u32[]{:S(2)}) collective-permute-start(bf16[1024,1024]{1,0:T(8,128)(2,1)} %convolution_convert_fusion), channel_id=1, source_target_pairs={{0,16},{16,0},{1,17},{17,1},{2,18},{18,2},{3,19},{19,3},{4,20},{20... | collective-permute-start | bytes 6291464 | tf_op jit(solution)/shard_map/ppermute | solution.py:497
  571.5 4.6 collective-permute-start.10
  576.2 1.4 collective-permute-start.11
  577.5 4.8 collective-permute-start.12
  582.4 15.2 %collective-permute-start.13 = (f32[23552]{0:T(1024)S(1)}, f32[23552]{0:T(1024)S(1)}, u32[]{:S(2)}, u32[]{:S(2)}) collective-permute-start(f32[23552]{0:T(1024)S(1)} %add.182), channel_id=1, source_target_pairs={{0,4},{1,5},{2,6},{3,7},{4,0},{5,1},{6,2},{7,3},{8,12},{9,13},{10,... | collective-permute-start | bytes 282632 | tf_op jit(solution)/shard_map/ppermute | solution.py:194
  597.6 9.1 %collective-permute-start.14 = (f32[23552]{0:T(1024)S(1)}, f32[23552]{0:T(1024)S(1)}, u32[]{:S(2)}, u32[]{:S(2)}) collective-permute-start(f32[23552]{0:T(1024)S(1)} %add.183), channel_id=1, source_target_pairs={{0,8},{1,9},{2,10},{3,11},{4,12},{5,13},{6,14},{7,15},{8,0},{9,1},... | collective-permute-start | bytes 282632 | tf_op jit(solution)/shard_map/ppermute | solution.py:194
  607.4 13.3 %collective-permute-start.16 = (bf16[128,2048]{1,0:T(8,128)(2,1)S(1)}, bf16[128,2048]{1,0:T(8,128)(2,1)S(1)}, u32[]{:S(2)}, u32[]{:S(2)}) collective-permute-start(bf16[128,2048]{1,0:T(8,128)(2,1)S(1)} %slice.162), channel_id=1, source_target_pairs={{0,16},{16,0},{1,17},{17,1},{2,18},{18,2},{3,19},{19,3},{4,20},{20... | collective-permute-start | bytes 1572872 | tf_op jit(solution)/shard_map/ppermute | solution.py:497
  (35 other events, 211.9 us)
Sparse Core Ops, SparseCore 0:
  24.7 128.3 all-gather.1
  375.7 179.0 reduce-scatter.1
  592.8 113.6 all-reduce.2

commit v2 on v1

--- a/solution.py
+++ b/solution.py
@@ -19,6 +19,7 @@
 GELU_CUBE = 0.044715
 BF = jnp.bfloat16
 F32 = jnp.float32
+MESH = pl.DeviceIdType.MESH
 
 
 def dot(a, b, dims=(((1,), (0,)), ((), ()))):
@@ -183,19 +184,6 @@
     sums_ref[0, 0, 3:, :] = jnp.zeros((5, LANES), F32)
 
 
-def sum_everywhere(value, axes):
-    for name, size in axes:
-        if size & (size - 1):
-            value = lax.psum(value, name)
-            continue
-        step = 1
-        while step < size:
-            pairs = [(d, d ^ step) for d in range(size)]
-            value = value + lax.ppermute(value, name, pairs)
-            step *= 2
-    return value
-
-
 def attention_specs(slots, span, first_block, width):
     part = span // slots
     return pl.BlockSpec((part, width), lambda r, p, *_: (first_block + r, p))
@@ -462,6 +450,312 @@
     )(*middles, *hidden_grads, *cots, *denses)
 
 
+def head_grads_kernel(count, *refs):
+    rows, grads = refs[:count], refs[count : 2 * count]
+    out_grad, result, total = refs[2 * count :]
+
+    @pl.when(pl.program_id(0) == 0)
+    def _():
+        total[...] = jnp.zeros_like(total)
+
+    wide = 2 * LANES
+    for at in range(0, total.shape[1], wide):
+        cols = slice(at, at + wide)
+        total[:, cols] += functools.reduce(
+            jnp.add,
+            [dot(left[...], right[:, cols], ROW_PAIRS) for left, right in zip(rows, grads)],
+        )
+
+    @pl.when(pl.program_id(0) == pl.num_programs(0) - 1)
+    def _():
+        for at in range(0, total.shape[1], LANES):
+            pair, kind = divmod(at // LANES, 3)
+            result[kind, :, pair * LANES : (pair + 1) * LANES] = total[:, at : at + LANES].astype(BF)
+        part, width = out_grad.shape
+        for at in range(0, width, part):
+            result[3, at : at + part, :] = out_grad[:, at : at + part].astype(BF)
+
+
+def head_grads(rows, grads, out_grad):
+    tokens, width = rows[0].shape
+    columns = grads[0].shape[1]
+    block = min(512, tokens)
+    return pl.pallas_call(
+        functools.partial(head_grads_kernel, len(rows)),
+        grid=(tokens // block,),
+        in_specs=[pl.BlockSpec((block, width), lambda i: (i, 0))] * len(rows)
+        + [pl.BlockSpec((block, columns), lambda i: (i, 0))] * len(grads)
+        + [pl.BlockSpec(out_grad.shape, lambda i: (0, 0))],
+        out_specs=pl.BlockSpec((4, width, columns // 3), lambda i: (0, 0, 0)),
+        out_shape=jax.ShapeDtypeStruct((4, width, columns // 3), BF),
+        scratch_shapes=[pltpu.VMEM((width, columns), F32)],
+        compiler_params=pltpu.CompilerParams(vmem_limit_bytes=56 * 2**20),
+        name="head_grads",
+    )(*rows, *grads, out_grad)
+
+
+def partner(name, bit):
+    me = lax.axis_index(name)
+    mine = lax.rem(me // (1 << bit), 2)
+    return mine, {name: me + (1 - 2 * mine) * (1 << bit)}
+
+
+def greet(places):
+    barrier = pltpu.get_barrier_semaphore()
+    for place_of in places:
+        pl.semaphore_signal(barrier, inc=1, device_id=place_of, device_id_type=MESH)
+    pl.semaphore_wait(barrier, len(places))
+
+
+def batch_sum_kernel(bits, chunks, steps, source, extra, result, extra_result, *refs):
+    levels, arrivals = refs[:bits], refs[bits : 2 * bits]
+    extra_totals, extra_arrivals = refs[2 * bits : 2 * bits + 2]
+    send_sems, recv_sems, extra_send_sems, extra_recv_sems = refs[2 * bits + 2 :]
+    rows = source.shape[0] // chunks
+    partners = [partner("batch", bit) for bit in range(bits)]
+    extra_partners = [partner(name, bit)[1] for name, bit in steps]
+    greet(extra_partners)
+    offsets, offset = [], 0
+    for bit in range(bits):
+        offset = offset + partners[bit][0] * (rows >> (bit + 1))
+        offsets.append(offset)
+
+    def aligned(value, size):
+        return pl.ds(pl.multiple_of(value, size), size)
+
+    def piece(chunk, bit, mine):
+        size = rows >> (bit + 1)
+        if bit == 0:
+            return source.at[aligned(chunk * rows + mine * size, size), :]
+        return levels[bit - 1].at[chunk, aligned(mine * size, size), :]
+
+    def final(chunk, bit):
+        return result.at[aligned(chunk * rows + offsets[bit], rows >> (bit + 1)), :]
+
+    copies = {}
+
+    def start(chunk, stage):
+        if stage < bits:
+            mine, other = partners[stage]
+            here, there = piece(chunk, stage, 1 - mine), arrivals[stage].at[chunk]
+        else:
+            bit = 2 * bits - 1 - stage
+            other = partners[bit][1]
+            here = there = final(chunk, bit)
+        copies[chunk, stage] = pltpu.make_async_remote_copy(
+            src_ref=here,
+            dst_ref=there,
+            send_sem=send_sems.at[chunk, stage],
+            recv_sem=recv_sems.at[chunk, stage],
+            device_id=other,
+            device_id_type=MESH,
+        )
+        copies[chunk, stage].start()
+
+    def finish(chunk, stage):
+        copies[chunk, stage].wait_recv()
+        if stage < bits:
+            kept = piece(chunk, stage, partners[stage][0])[...].astype(F32)
+            total = (kept + arrivals[stage][chunk].astype(F32)).astype(BF)
+            if stage == bits - 1:
+                final(chunk, stage)[...] = total
+            else:
+                levels[stage][chunk] = total
+
+    def extra_total(step):
+        if step == 0:
+            return extra
+        return extra_result if step == len(steps) else extra_totals.at[step - 1]
+
+    def extra_copy(step):
+        return pltpu.make_async_remote_copy(
+            src_ref=extra_total(step),
+            dst_ref=extra_arrivals.at[step],
+            send_sem=extra_send_sems.at[step],
+            recv_sem=extra_recv_sems.at[step],
+            device_id=extra_partners[step],
+            device_id_type=MESH,
+        )
+
+    extra_copies = []
+    for tick in range(max(chunks + 2 * bits, len(steps) + 1)):
+        if 0 < tick <= len(steps):
+            extra_copies[tick - 1].wait_recv()
+            extra_total(tick)[...] = extra_total(tick - 1)[...] + extra_arrivals[tick - 1]
+        if tick < len(steps):
+            extra_copies.append(extra_copy(tick))
+            extra_copies[tick].start()
+        for chunk in range(chunks):
+            stage = tick - chunk
+            if 0 < stage <= 2 * bits:
+                finish(chunk, stage - 1)
+            if 0 <= stage < 2 * bits:
+                start(chunk, stage)
+    for copy in (*copies.values(), *extra_copies):
+        copy.wait_send()
+
+
+def halving_steps(axes):
+    return [(name, bit) for name, size in axes for bit in range(size.bit_length() - 1)]
+
+
+def batch_sum(value, extra, axes):
+    bits = axes[0][1].bit_length() - 1
+    if bits == 0 or any(size & (size - 1) for _, size in axes):
+        return lax.psum(value, "batch"), lax.psum(extra, tuple(name for name, _ in axes))
+    steps = halving_steps(axes)
+    rows, columns = value.shape
+    chunks = 4
+    halves = [
+        pltpu.VMEM((chunks, rows // chunks >> (bit + 1), columns), BF) for bit in range(bits)
+    ]
+    return pl.pallas_call(
+        functools.partial(batch_sum_kernel, bits, chunks, steps),
+        in_specs=[pl.BlockSpec(memory_space=pltpu.VMEM)] * 2,
+        out_specs=[pl.BlockSpec(memory_space=pltpu.VMEM)] * 2,
+        out_shape=[
+            jax.ShapeDtypeStruct(value.shape, BF),
+            jax.ShapeDtypeStruct(extra.shape, F32),
+        ],
+        scratch_shapes=halves * 2
+        + [pltpu.VMEM((len(steps), *extra.shape), F32)] * 2
+        + [pltpu.SemaphoreType.DMA((chunks, 2 * bits))] * 2
+        + [pltpu.SemaphoreType.DMA((len(steps),))] * 2,
+        compiler_params=pltpu.CompilerParams(
+            collective_id=0, has_side_effects=True, vmem_limit_bytes=40 * 2**20
+        ),
+        name="batch_sum",
+    )(value, extra)
+
+
+def small_sum_kernel(steps, source, result, *refs):
+    totals, arrivals = refs[:-2][: len(steps) - 1], refs[:-2][len(steps) - 1 :]
+    send_sems, recv_sems = refs[-2:]
+    partners = [partner(name, bit)[1] for name, bit in steps]
+    greet(partners)
+    here = source
+    copies = []
+    for step, other in enumerate(partners):
+        copy = pltpu.make_async_remote_copy(
+            src_ref=here,
+            dst_ref=arrivals[step],
+            send_sem=send_sems.at[step],
+            recv_sem=recv_sems.at[step],
+            device_id=other,
+            device_id_type=MESH,
+        )
+        copy.start()
+        copies.append(copy)
+        copy.wait_recv()
+        there = result if step == len(partners) - 1 else totals[step]
+        there[...] = here[...] + arrivals[step][...]
+        here = there
+    for copy in copies:
+        copy.wait_send()
+
+
+def small_sum(value, axes):
+    steps = halving_steps(axes)
+    if not steps or any(size & (size - 1) for _, size in axes):
+        return lax.psum(value, tuple(name for name, _ in axes))
+    return pl.pallas_call(
+        functools.partial(small_sum_kernel, steps),
+        in_specs=[pl.BlockSpec(memory_space=pltpu.VMEM)],
+        out_specs=pl.BlockSpec(memory_space=pltpu.VMEM),
+        out_shape=jax.ShapeDtypeStruct(value.shape, F32),
+        scratch_shapes=[pltpu.VMEM(value.shape, F32)] * (2 * len(steps) - 1)
+        + [pltpu.SemaphoreType.DMA((len(steps),))] * 2,
+        compiler_params=pltpu.CompilerParams(
+            collective_id=1, has_side_effects=True, vmem_limit_bytes=40 * 2**20
+        ),
+        name="small_sum",
+    )(value)
+
+
+def first_back_kernel(count, rows_ref, grad_ref, weights, gains, shifts, residual_ref, *refs):
+    arrived = refs[:count]
+    result, sums_ref = refs[count:]
+
+    @pl.when(pl.program_id(0) == 0)
+    def _():
+        sums_ref[...] = jnp.zeros_like(sums_ref)
+
+    grad = dot(grad_ref[...], weights[...], COLUMN_PAIRS).astype(BF).astype(F32)
+    for term in arrived:
+        grad = grad + term[...].astype(F32)
+    gain = gains[0:1, :]
+    _, unit, inverse = normalize(rows_ref[...].astype(F32), gain, shifts[0:1, :])
+    scaled = grad * gain
+    inner = (
+        scaled
+        - jnp.mean(scaled, axis=-1, keepdims=True)
+        - unit * jnp.mean(scaled * unit, axis=-1, keepdims=True)
+    )
+    sums_ref[0:1, :] += column_sum(grad * unit)
+    sums_ref[1:2, :] += column_sum(grad)
+    result[...] = (residual_ref[...] + inner * inverse).astype(BF)
+
+
+def first_back(rows, qkv_grad, weights, gains, shifts, residual_grad, arrived):
+    tokens, width = rows.shape
+    block = min(256, tokens)
+
+    def tiles(columns):
+        return pl.BlockSpec((block, columns), lambda i: (i, 0))
+
+    def whole(array):
+        return pl.BlockSpec(array.shape, lambda i: (0, 0), pipeline_mode=pl.Buffered(1))
+
+    return pl.pallas_call(
+        functools.partial(first_back_kernel, len(arrived)),
+        grid=(tokens // block,),
+        in_specs=[
+            tiles(width),
+            tiles(qkv_grad.shape[1]),
+            whole(weights),
+            whole(gains),
+            whole(shifts),
+            tiles(width),
+        ]
+        + [tiles(width)] * len(arrived),
+        out_specs=[tiles(width), pl.BlockSpec((8, width), lambda i: (0, 0))],
+        out_shape=[
+            jax.ShapeDtypeStruct((tokens, width), BF),
+            jax.ShapeDtypeStruct((8, width), F32),
+        ],
+        compiler_params=pltpu.CompilerParams(vmem_limit_bytes=40 * 2**20),
+        name="first_back",
+    )(rows, qkv_grad, weights, gains, shifts, residual_grad, *arrived)
+
+
+def project_kernel(rows_ref, weights, biases, result):
+    rows = rows_ref[...]
+    for kind in range(3):
+        value = (dot(rows, weights[kind]) + biases[kind : kind + 1, :]).astype(BF)
+        for pair in range(value.shape[1] // LANES):
+            at = (3 * pair + kind) * LANES
+            result[:, at : at + LANES] = value[:, pair * LANES : (pair + 1) * LANES]
+
+
+def project(rows, weights, biases):
+    tokens, width = rows.shape
+    columns = 3 * weights.shape[2]
+    block = min(256, tokens)
+    return pl.pallas_call(
+        project_kernel,
+        grid=(tokens // block,),
+        in_specs=[
+            pl.BlockSpec((block, width), lambda i: (i, 0)),
+            pl.BlockSpec(weights.shape, lambda i: (0, 0, 0), pipeline_mode=pl.Buffered(1)),
+            pl.BlockSpec(biases.shape, lambda i: (0, 0), pipeline_mode=pl.Buffered(1)),
+        ],
+        out_specs=pl.BlockSpec((block, columns), lambda i: (i, 0)),
+        out_shape=jax.ShapeDtypeStruct((tokens, columns), BF),
+        compiler_params=pltpu.CompilerParams(vmem_limit_bytes=40 * 2**20),
+        name="project",
+    )(rows, weights, biases)
+
+
 def shards(
     slots,
     short_rows,
@@ -518,21 +812,14 @@
     weights = (
         head_weights.reshape(3, width, pairs, LANES).transpose(1, 2, 0, 3).reshape(width, 3 * part)
     )
-    biases = (
-        jnp.stack([head_biases[0], jnp.zeros_like(head_biases[0]), head_biases[1]])
-        .reshape(3, pairs, LANES)
-        .transpose(1, 0, 2)
-        .reshape(3 * part)
-    )
+    biases = jnp.stack([head_biases[0], jnp.zeros_like(head_biases[0]), head_biases[1]])
     scale_lanes = jnp.repeat(head_scale, HEAD).reshape(1, part)
 
     share = up_weight.shape[0]
     batches = mid_gain.shape[0] // (slots * share)
     own_feed = jnp.stack([up_weight, down_weight])
     feed_slots = [own_feed] + [fetch(own_feed, slot) for slot in range(1, slots)]
-    feed = lax.all_gather(
-        jnp.stack(feed_slots, 1).reshape(2 * slots * share, width), "batch", axis=0, tiled=True
-    )
+    feed = jnp.stack(feed_slots, 1).reshape(2 * slots * share, width)
 
     def turn(values, places):
         return jnp.roll(values, places, axis=1)
@@ -540,21 +827,28 @@
     mid_rows = jnp.concatenate([mid_gain[None], mid_shifts], 0).reshape(3, slots, batches, share)
     mid_rows = turn(mid_rows, -me[0]).transpose(0, 2, 1, 3).reshape(3, -1)
 
-    units, inverses, normed_slots = [], [], []
+    lows = []
     for rows in inputs:
-        value, unit, inverse = normalize(rows.astype(F32), norm_gains[0], norm_shifts[0])
-        low = value.astype(BF)
-        if normed_slots:
-            low, normed_slots[-1] = lax.optimization_barrier((low, normed_slots[-1]))
-        normed_slots.append([low] + [fetch(low, slot) for slot in range(1, slots)])
-        units.append(unit)
-        inverses.append(inverse)
-    out_weights, _ = lax.optimization_barrier((out_weight, normed_slots[-1]))
+        value, _, _ = normalize(rows.astype(F32), norm_gains[0], norm_shifts[0])
+        lows.append(value.astype(BF))
+    lows[0], feed = lax.optimization_barrier((lows[0], feed))
+    feed = lax.all_gather(feed, "batch", axis=0, tiled=True)
+    own_qkv = [project(rows, head_weights, biases) for rows in lows]
+    arrived = [fetch(lows[0], slot) for slot in range(1, slots)]
+    own_qkv, arrived, lows[1], weights = lax.optimization_barrier(
+        (own_qkv, arrived, lows[1], weights)
+    )
+    normed_slots = [
+        [lows[0], *arrived],
+        [lows[1]] + [fetch(lows[1], slot) for slot in range(1, slots)],
+    ]
+    out_weights, _ = lax.optimization_barrier((out_weight, normed_slots[-1][1:]))
     out_weights = [out_weight] + [deliver(out_weights, slot) for slot in range(1, slots)]
 
     qkv, saved, scaled = [], [], []
     for group in range(2):
-        projected = [(dot(rows, weights) + biases).astype(BF) for rows in normed_slots[group]]
+        projected = [own_qkv[group]]
+        projected += [project(rows, head_weights, biases) for rows in normed_slots[group][1:]]
         qkv.append(projected)
         outs, totals = [], []
         for job in jobs[group]:
@@ -595,10 +889,31 @@
     grad_slots, both = lax.optimization_barrier((grad_slots, both))
     both = lax.psum_scatter(both, "batch", scatter_dimension=0, tiled=True)
 
-    weight_grad = jnp.zeros((width, 3 * part), F32)
     bias_sums = jnp.zeros((8, part), F32)
-    normed_grads = []
+    grads, first_sums, qkv_grads = [], [], []
+
+    def send_back(qkv_grad):
+        return [
+            deliver(dot(qkv_grad[slot], weights, COLUMN_PAIRS).astype(BF), slot)
+            for slot in range(1, slots)
+        ]
+
+    def finish_back(group, arrived):
+        grad, group_sums = first_back(
+            inputs[group],
+            qkv_grads[group][0],
+            weights,
+            norm_gains,
+            norm_shifts,
+            residual_grads[group],
+            arrived,
+        )
+        grads.append(grad)
+        first_sums.append(group_sums)
+
     for group in range(2):
+        if group == 1:
+            grad_slots[1], qkv_grads[0] = lax.optimization_barrier((grad_slots[1], qkv_grads[0]))
         qkv_grad = []
         outs, totals = saved[group]
         for job, log_total in zip(jobs[group], totals):
@@ -614,61 +929,49 @@
                 *job[1:],
             )
             bias_sums = bias_sums + jnp.sum(back_sums, axis=0).transpose(1, 0, 2).reshape(8, part)
-        terms = [dot(piece, weights, COLUMN_PAIRS).astype(BF) for piece in qkv_grad]
-        terms = spread(terms, deliver)
-        normed_grad = terms[0].astype(F32)
-        for term in terms[1:]:
-            normed_grad = normed_grad + term.astype(F32)
-        normed_grads.append(normed_grad)
-        for rows, piece in zip(normed_slots[group], qkv_grad):
-            weight_grad = weight_grad + dot(rows, piece, ROW_PAIRS)
-
-    weight_grad, out_grad = weight_grad.astype(BF), out_grad.astype(BF)
-    weight_grad, out_grad, both = lax.optimization_barrier((weight_grad, out_grad, both))
-    summed_weight, summed_out = lax.psum((weight_grad, out_grad), "batch")
+        qkv_grads.append(qkv_grad)
+        if group == 0:
+            arrived = send_back(qkv_grad)
+    weight_grad = head_grads(
+        [rows for group in normed_slots for rows in group],
+        [piece for group in qkv_grads for piece in group],
+        out_grad,
+    )
+    qkv_grads[1], weight_grad = lax.optimization_barrier((qkv_grads[1], weight_grad))
+    arrived_last = send_back(qkv_grads[1])
+    finish_back(0, arrived)
+    mid_terms = (mid_sums[0] + mid_sums[1])[:3].reshape(3, batches, slots, share)
+    mid_terms = turn(mid_terms.transpose(0, 2, 1, 3), me[0])
+    norm_sums = sums[0] + sums[1]
+    own_sums = lax.dynamic_update_slice(
+        jnp.zeros((slots, 3 * part), F32), bias_sums[:3].reshape(1, -1), (me[0], jnp.int32(0))
+    )
+    shared = jnp.concatenate(
+        [norm_sums[1:7].reshape(-1), mid_terms.reshape(-1), own_sums.reshape(-1)]
+    ).reshape(-1, LANES)
+    axes = (("batch", batches), ("head", slots))
+    weight_grad, shared, grads[0] = lax.optimization_barrier((weight_grad, shared, grads[0]))
+    summed_weight, summed = batch_sum(weight_grad.reshape(4 * width, part), shared, axes)
+    arrived_last, summed_weight, both = lax.optimization_barrier(
+        (arrived_last, summed_weight, both)
+    )
+    summed_weight = summed_weight.reshape(4, width, part)
     both = both.reshape(slots, share, 2 * width)
     both_grads = both[0].astype(F32)
     for slot in range(1, slots):
         both_grads = both_grads + deliver(both[slot], slot).astype(F32)
-    grad_head_weights = (
-        summed_weight.reshape(width, pairs, 3, LANES)
-        .transpose(2, 0, 1, 3)
-        .reshape(3, width, part)
-        .astype(F32)
-    )
-
-    grads = []
-    first_gain = first_shift = jnp.zeros((1, width), F32)
-    for group in range(2):
-        inner, gain_term, shift_term = normalize_back(
-            normed_grads[group], units[group], inverses[group], norm_gains[0]
-        )
-        first_gain = first_gain + gain_term
-        first_shift = first_shift + shift_term
-        grads.append((residual_grads[group] + inner).astype(BF))
-    sums = sums[0] + sums[1]
-    mid_terms = (mid_sums[0] + mid_sums[1])[:3].reshape(3, batches, slots, share)
-    mid_terms = turn(mid_terms.transpose(0, 2, 1, 3), me[0])
-    shared = jnp.concatenate(
-        [
-            first_gain.reshape(-1),
-            sums[1:3].reshape(-1),
-            first_shift.reshape(-1),
-            sums[3:7].reshape(-1),
-            mid_terms.reshape(-1),
-        ]
-    )
-    shared_size = shared.shape[0]
-    own_sums = lax.dynamic_update_slice(
-        jnp.zeros((slots, 3 * part), F32), bias_sums[:3].reshape(1, -1), (me[0], jnp.int32(0))
-    )
-    summed = sum_everywhere(
-        jnp.concatenate([shared, own_sums.reshape(-1)]), (("head", slots), ("batch", batches))
-    )
-    norm_sums = summed[: 8 * width].reshape(8, width)
-    mid_terms = summed[8 * width : shared_size].reshape(3, -1)
+    finish_back(1, arrived_last)
+    late = first_sums[0] + first_sums[1]
+    late, both_grads = lax.optimization_barrier((late, both_grads))
+    late = small_sum(late[:2].reshape(-1, LANES), axes).reshape(2, width)
+    summed = summed.reshape(-1)
+    norm_sums, mid_terms, own_sums = jnp.split(
+        summed, [6 * width, 6 * width + 3 * mid_gain.shape[0]]
+    )
+    norm_sums = norm_sums.reshape(6, width)
+    mid_terms = mid_terms.reshape(3, -1)
     own_sums = lax.dynamic_slice(
-        summed[shared_size:].reshape(slots, 3 * part), (me[0], jnp.int32(0)), (1, 3 * part)
+        own_sums.reshape(slots, 3 * part), (me[0], jnp.int32(0)), (1, 3 * part)
     ).reshape(3, part)
     return (
         outputs[1][:short_tokens].reshape(shapes[0]),
@@ -677,12 +980,14 @@
         grads[1][:short_tokens].reshape(shapes[0]),
         grads[1][short_tokens:].reshape(shapes[1]),
         grads[0].reshape(shapes[2]),
-        norm_sums[:3],
-        norm_sums[3:],
-        grad_head_weights,
+        jnp.concatenate([late[:1], norm_sums[:2]], 0),
+        jnp.concatenate([late[1:], norm_sums[2:]], 0),
+        summed_weight[:3].astype(F32),
         own_sums[:2],
         jnp.sum(own_sums[2].reshape(-1, HEAD), axis=1),
-        summed_out.astype(F32),
+        jnp.concatenate(
+            [summed_weight[3, at : at + part] for at in range(0, width, part)], 1
+        ).astype(F32),
         both_grads[:, width:],
         mid_terms[0],
         jnp.stack([mid_terms[2], mid_terms[1]]),

time: 722 us -> 662 us (0.917)
  Pallas kernels: 365 us -> 498 us
  waiting for transfers between devices: 162 us -> 35.5 us
  matrix products: 91.5 us -> 22.9 us
  local copies, waits for them, and re-layouts: 36.1 us -> 45 us
    pallas_call x0 -> x9, Pallas kernels: none -> 144 us  [the longest x1 70.9 us: batch_sum(): pl.pallas_call(functools.partial(batch_sum_kernel, bits, chunks, steps),...]
    psum x1 -> x0, waiting for transfers between devices: 84.6 us -> none  [shards(): summed_weight, summed_out = lax.psum((weight_grad, out_grad), 'batch')]
    dot_general x16 -> x6, matrix products: 91.5 us -> 22.9 us  [dot(): return lax.dot_general(a, b, dims, preferred_element_type=F32)]
    ppermute x6, waiting for transfers between devices: 46.5 us -> 28.8 us  [fetch(): lax.ppermute(value, 'head', [((d + slot) % slots, d) for d in range(slots)])]
    ppermute x5 -> x0, waiting for transfers between devices: 12.3 us -> none  [sum_everywhere(): value = value + lax.ppermute(value, name, pairs)]
    ppermute x6, waiting for transfers between devices: 18.6 us -> 6.6 us  [deliver(): lax.ppermute(value, 'head', [(d, (d + slot) % slots) for d in range(slots)])]
    unnamed x84 -> x92, local copies, waits for them, and re-layouts: 12.7 us -> 23.3 us
    pallas_call x2, Pallas kernels: 151 us -> 140 us  [middle_pass(): call(rows, cotangent, *scaled, *out_weights, feed, gains, shifts, mid_gai...]
  transfers between devices with their start and end apart: 20 -> 14, of which waited for: 10 -> 3; matrix products, arithmetic and copies ran while one was open for 20% -> 10% of each run, Pallas kernels for 51% -> 74%
where the time goes in v2:
time: 662 us; the launch traced here: 657 us
  Pallas kernels  498 us (75%)
  local copies, waits for them, and re-layouts  45 us (7%)
  waiting for transfers between devices  35.5 us (5%)
  other arithmetic  24.9 us (4%)
  matrix products  22.9 us (3%)
  between operations  16.3 us (2%)
  starting transfers between devices  14.7 us (2%)
    pallas_call x2, Pallas kernels, middle_pass(): call(rows, cotangent, *scaled, *out_weights, feed, gains, shifts, mid_gai...  140 us
    pallas_call x3, Pallas kernels, attend_backward(): call(me, lengths, *qkv, *outs, *grads, scale_lanes, log_total, *kept)  108 us
    pallas_call x1, Pallas kernels, batch_sum(): pl.pallas_call(functools.partial(batch_sum_kernel, bits, chunks, steps),...  70.9 us
    pallas_call x3, Pallas kernels, attend_forward(): *outs, log_total = call(me, lengths, *qkv, scale_lanes, *kept)  62.3 us
    pallas_call x1, Pallas kernels, feed_grads(): pl.pallas_call(functools.partial(feed_grads_kernel, groups), grid=(hidden...  43.6 us
    ppermute x6, waiting for transfers between devices, fetch(): lax.ppermute(value, 'head', [((d + slot) % slots, d) for d in range(slots)])  28.8 us
    pallas_call x1, Pallas kernels, head_grads(): pl.pallas_call(functools.partial(head_grads_kernel, len(rows)), grid=(tok...  23.6 us
    unnamed x92, local copies, waits for them, and re-layouts  23.3 us
  transfers between devices with their start and end apart: 14, of which 3 were waited for; matrix products, arithmetic and copies ran while one was open for 10% of the time, Pallas kernels for 74%

profile of v2, /device:TPU:0, one launch (start us, length us, event | category | flops | bytes accessed | tf_op | source)
XLA Modules:
  0.0 657.3 jit_solution(3282538540224965091)
XLA Ops:
  33.7 5.4 project.5.refs_0_
  40.7 4.0 project.4.refs_0_
  46.4 25.7 %collective-permute-done.1.rows_ref.refs_1_ = bf16[1024,1024]{1,0:T(8,128)(2,1)} collective-permute-done((bf16[1024,1024]{1,0:T(8,128)(2,1)}, bf16[1024,1024]{1,0:T(8,128)(2,1)}, u32[]{:S(2)}, u32[]{:S(2)}) %collective-permute-start.1) | collective-permute-done | bytes 2097184 | tf_op jit(solution)/shard_map/ppermute | solution.py:788
  74.9 5.3 project.7.refs_1_
  81.8 35.9 %attend_forward.5 = (bf16[1024,512]{1,0:T(8,128)(2,1)}, bf16[1024,512]{1,0:T(8,128)(2,1)}, f32[4,1,2,2048]{3,2,1,0:T(2,128)}) custom-call(s32[1]{0:T(128)} %bitcast.4.me_ref, s32[1]{0:T(128)S(6)} %copy.67.len_ref, bf16[1024,1536]{1,0:T(8,128)(2,1)} %copy-done.5, bf16[1024,1536]{1,0:T(8,128)(2,1)} %copy-done.6, f32[1,512]{1,0:T(1,128)} %reshape_reshape.3.refs_2_.refs_6_), custom_call_target="tpu_custom_call" | custom-call | tf_op jit(solution)/shard_map/attend_forward/pallas_call | solution.py:215
  120.3 5.5 project.6.refs_1_
  127.5 12.5 %attend_forward.3 = (bf16[1024,512]{1,0:T(8,128)(2,1)}, bf16[1024,512]{1,0:T(8,128)(2,1)}, f32[4,2,2,512]{3,2,1,0:T(2,128)}) custom-call(s32[1]{0:T(128)} %bitcast.4.me_ref, s32[2]{0:T(128)} %len_ref.7, bf16[1024,1536]{1,0:T(8,128)(2,1)} %copy-done.1, bf16[1024,1536]{1,0:T(8,128)(2,1)} %copy-done.2, f32[1,512]{1,0:T(1,128)} %reshape_reshape.3.refs_2_.refs_6_), custom_call_target="tpu_custom_call" | custom-call | tf_op jit(solution)/shard_map/attend_forward/pallas_call | solution.py:215
  140.1 13.9 %attend_forward.4 = (bf16[1024,512]{1,0:T(8,128)(2,1)}, bf16[1024,512]{1,0:T(8,128)(2,1)}, f32[4,1,2,1024]{3,2,1,0:T(2,128)}) custom-call(s32[1]{0:T(128)} %bitcast.4.me_ref, s32[1]{0:T(128)S(6)} %copy.66.len_ref, bf16[1024,1536]{1,0:T(8,128)(2,1)} %copy-done.1, bf16[1024,1536]{1,0:T(8,128)(2,1)} %copy-done.2, ...), custom_call_target="tpu_custom_call", output_to_operand_aliasing={{0}: (5, {}), {1}: (6, {})} | custom-call | tf_op jit(solution)/shard_map/attend_forward/pallas_call | solution.py:215
  160.0 6.6 %collective-permute-done.4.refs_5_ = bf16[512,1024]{1,0:T(8,128)(2,1)} collective-permute-done((bf16[512,1024]{1,0:T(8,128)(2,1)}, bf16[512,1024]{1,0:T(8,128)(2,1)}, u32[]{:S(2)}, u32[]{:S(2)}) %collective-permute-start.4) | collective-permute-done | bytes 1048608 | tf_op jit(solution)/shard_map/ppermute | solution.py:791
  166.6 69.9 %middle_pass.3 = (bf16[1024,1024]{1,0:T(8,128)(2,1)}, f32[1024,1024]{1,0:T(8,128)}, bf16[1024,1024]{1,0:T(8,128)(2,1)}, bf16[1024,1024]{1,0:T(8,128)(2,1)}, bf16...) custom-call(bf16[1024,1024]{1,0:T(8,128)(2,1)} %bitcast.81, ...), custom_call_target="tpu_custom_call" | custom-call | tf_op jit(solution)/shard_map/middle_pass/pallas_call | solution.py:415
  238.3 70.5 %middle_pass.2 = (bf16[1024,1024]{1,0:T(8,128)(2,1)}, f32[1024,1024]{1,0:T(8,128)}, bf16[1024,1024]{1,0:T(8,128)(2,1)}, bf16[1024,1024]{1,0:T(8,128)(2,1)}, bf16...) custom-call(bf16[1024,1024]{1,0:T(8,128)(2,1)} %pad_maximum_fusion.r, ...), custom_call_target="tpu_custom_call" | custom-call | tf_op jit(solution)/shard_map/middle_pass/pallas_call | solution.py:415
  310.2 43.6 %feed_grads.1 = bf16[4096,2048]{1,0:T(8,128)(2,1)} custom-call(bf16[1024,4096]{1,0:T(8,128)(2,1)} %get-tuple-element.108.refs_0_, bf16[1024,4096]{1,0:T(8,128)(2,1)} %get-tuple-element.109.refs_1_, bf16[1024,4096]{1,0:T(8,128)(2,1)} %get-tuple-element.110.refs_2_, bf16[1024,4096]{1,0:T(8,128)(2,1)} %get-tuple-element.111.refs_3_, ...), custom_call_target="tpu_custom_call" | custom-call | tf_op jit(solution)/shard_map/feed_grads/pallas_call | solution.py:441
  360.0 4.0 fusion.25
  373.0 66.8 %attend_backward.3 = (bf16[1024,1536]{1,0:T(8,128)(2,1)}, bf16[1024,1536]{1,0:T(8,128)(2,1)}, f32[1,4,8,128]{3,2,1,0:T(8,128)}) custom-call(s32[1]{0:T(128)} %bitcast.4.me_ref, s32[1]{0:T(128)S(6)} %copy.67.len_ref, bf16[1024,1536]{1,0:T(8,128)(2,1)} %copy-done.5, bf16[1024,1536]{1,0:T(8,128)(2,1)} %copy-done.6, ...), custom_call_target="tpu_custom_call" | custom-call | tf_op jit(solution)/shard_map/attend_backward/pallas_call | solution.py:250
  439.8 6.5 convolution_convert_fusion
  447.4 17.6 %attend_backward.4 = (bf16[1024,1536]{1,0:T(8,128)(2,1)}, bf16[1024,1536]{1,0:T(8,128)(2,1)}, f32[2,4,8,128]{3,2,1,0:T(8,128)}) custom-call(s32[1]{0:T(128)} %bitcast.4.me_ref, s32[2]{0:T(128)} %len_ref.7, bf16[1024,1536]{1,0:T(8,128)(2,1)} %copy-done.1, bf16[1024,1536]{1,0:T(8,128)(2,1)} %copy-done.2, bf16[1024,512]{1,0:T(8,128)(2,1)} %get-tuple-element.94.refs_2_, ...), custom_call_target="tpu_custom_call" | custom-call | tf_op jit(solution)/shard_map/attend_backward/pallas_call | solution.py:250
  465.0 23.5 %attend_backward.5 = (bf16[1024,1536]{1,0:T(8,128)(2,1)}, bf16[1024,1536]{1,0:T(8,128)(2,1)}, f32[1,4,8,128]{3,2,1,0:T(8,128)}) custom-call(s32[1]{0:T(128)} %bitcast.4.me_ref, s32[1]{0:T(128)S(6)} %copy.66.len_ref, bf16[1024,1536]{1,0:T(8,128)(2,1)} %copy-done.1, bf16[1024,1536]{1,0:T(8,128)(2,1)} %copy-done.2, ...), custom_call_target="tpu_custom_call", output_to_operand_aliasing={{0}: (10, {}), {1}: (11, {})} | custom-call | tf_op jit(solution)/shard_map/attend_backward/pallas_call | solution.py:250
  491.8 23.6 %head_grads.1 = bf16[4,1024,512]{2,1,0:T(8,128)(2,1)} custom-call(bf16[1024,1024]{1,0:T(8,128)(2,1)} %get-tuple-element.89.rows_ref.refs_0_, bf16[1024,1024]{1,0:T(8,128)(2,1)} %collective-permute-done.1.rows_ref.refs_1_, bf16[1024,1024]{1,0:T(8,128)(2,1)} %get-tuple-element.91.rows_ref.refs_2_, bf16[1024,1024]{1,0:T(8,128)(2,1)} %collective-permute-done.2.rows_ref.refs_3_, ...), custom_call_target="tpu_custom_call" | custom-call | tf_op jit(solution)/shard_map/head_grads/pallas_call | solution.py:483
  515.5 4.7 convolution_convert_fusion.1
  528.5 8.6 %first_back.2 = (bf16[1024,1024]{1,0:T(8,128)(2,1)}, f32[8,1024]{1,0:T(8,128)S(1)}) custom-call(bf16[1024,1024]{1,0:T(8,128)(2,1)S(1)} %bitcast.82, bf16[1024,1536]{1,0:T(8,128)(2,1)S(1)} %copy-done.13, bf16[1024,1536]{1,0:T(8,128)(2,1)S(1)} %copy-done.7, f32[3,1024]{1,0:T(4,128)S(1)} %copy-done.16, f32[5,1024]{1,0:T(8,128)S(1)} %copy-done.15, ...), custom_call_target="tpu_custom_call" | custom-call | tf_op jit(solution)/shard_map/first_back/pallas_call | solution.py:709
  537.1 70.9 %batch_sum.1 = (bf16[4096,512]{1,0:T(8,128)(2,1)S(1)}, f32[168,128]{1,0:T(8,128)S(1)}) custom-call(bf16[4096,512]{1,0:T(8,128)(2,1)S(1)} %bitcast.83, f32[168,128]{1,0:T(8,128)S(1)} %maximum_bitcast_fusion.extra), custom_call_target="tpu_custom_call" | custom-call | tf_op jit(solution)/shard_map/batch_sum/pallas_call | solution.py:612
  618.3 4.1 convert.1
  624.0 7.3 %first_back.3 = (bf16[1024,1024]{1,0:T(8,128)(2,1)S(1)}, f32[8,1024]{1,0:T(8,128)S(1)}) custom-call(bf16[1024,1024]{1,0:T(8,128)(2,1)S(1)} %copy-done.10, bf16[1024,1536]{1,0:T(8,128)(2,1)S(1)} %copy-done.9, bf16[1024,1536]{1,0:T(8,128)(2,1)S(1)} %copy-done.8, f32[3,1024]{1,0:T(4,128)S(1)} %copy-done.16, f32[5,1024]{1,0:T(8,128)S(1)} %copy-done.15, ...), custom_call_target="tpu_custom_call" | custom-call | tf_op jit(solution)/shard_map/first_back/pallas_call | solution.py:709
  635.7 13.2 %small_sum.1 = f32[16,128]{1,0:T(8,128)S(1)} custom-call(f32[16,128]{1,0:T(8,128)S(1)} %reshape.203.source), custom_call_target="tpu_custom_call" | custom-call | tf_op jit(solution)/shard_map/small_sum/pallas_call | solution.py:661
  (194 shorter events, 91.5 us)
Async XLA Ops:
  7.2 8.3 %copy-start.3 = (bf16[1,1024,1024]{2,1,0:T(8,128)(2,1)S(1)}, bf16[1,1024,1024]{2,1,0:T(8,128)(2,1)}, u32[]{:S(2)}) copy-start(bf16[1,1024,1024]{2,1,0:T(8,128)(2,1)} %param.23) | copy-start | bytes 6291460
  7.2 159.3 %all-gather.2.cloned.1.call-start = ((), (), s32[]{:S(2)}) async-start(), calls=%async_computation.1 | async-start | bytes 17825792 | tf_op jit(solution)/shard_map/all_gather | solution.py:835
  8.5 15.0 %collective-permute-start = (bf16[2,128,1024]{2,1,0:T(8,128)(2,1)S(1)}, bf16[2,128,1024]{2,1,0:T(8,128)(2,1)S(1)}, u32[]{:S(2)}, u32[]{:S(2)}) collective-permute-start(bf16[2,128,1024]{2,1,0:T(8,128)(2,1)S(1)} %get-tuple-element.170), channel_id=1, source_target_pairs={{16,0},{0,16},{17,1},{1,17},{18,2},{2,18},{19,3},{3,19},{20,4},{4,... | collective-permute-start | bytes 1572872 | tf_op jit(solution)/shard_map/ppermute | solution.py:788
  24.6 588.2 %reduce-scatter.2.cloned.1.call-start = ((), (), s32[]{:S(2)}) async-start(), calls=%async_computation.2 | async-start | bytes 17825792 | tf_op jit(solution)/shard_map/reduce_scatter | solution.py:890
  24.9 47.2 %collective-permute-start.1 = (bf16[1024,1024]{1,0:T(8,128)(2,1)}, bf16[1024,1024]{1,0:T(8,128)(2,1)}, u32[]{:S(2)}, u32[]{:S(2)}) collective-permute-start(bf16[1024,1024]{1,0:T(8,128)(2,1)} %get-tuple-element.89.rows_ref.refs_0_), channel_id=1, source_target_pairs={{16,0},{0,16},{17,1},{1,17},{18,2},{2,18},{19,3},{3,19},{20,4},{4,... | collective-permute-start | bytes 6291464 | tf_op jit(solution)/shard_map/ppermute | solution.py:788
  33.7 7.0 %copy-start.11 = (bf16[1024,1024]{1,0:T(8,128)(2,1)S(1)}, bf16[1024,1024]{1,0:T(8,128)(2,1)}, u32[]{:S(2)}) copy-start(bf16[1024,1024]{1,0:T(8,128)(2,1)} %get-tuple-element.89.rows_ref.refs_0_) | copy-start | bytes 6291460
  40.7 32.8 %copy-start.44 = (f32[8]{0:T(128)S(1)}, f32[8]{0:T(128)}, u32[]{:S(2)}) copy-start(f32[8]{0:T(128)} %param.34) | copy-start | bytes 100
  72.0 46.3 %collective-permute-start.2 = (bf16[1024,1024]{1,0:T(8,128)(2,1)}, bf16[1024,1024]{1,0:T(8,128)(2,1)}, u32[]{:S(2)}, u32[]{:S(2)}) collective-permute-start(bf16[1024,1024]{1,0:T(8,128)(2,1)} %get-tuple-element.91.rows_ref.refs_2_), channel_id=1, source_target_pairs={{16,0},{0,16},{17,1},{1,17},{18,2},{2,18},{19,3},{3,19},{20,4},{4,... | collective-permute-start | bytes 6291464 | tf_op jit(solution)/shard_map/ppermute | solution.py:788
  117.7 42.3 %collective-permute-start.5 = (bf16[1024,512]{1,0:T(8,128)(2,1)}, bf16[1024,512]{1,0:T(8,128)(2,1)}, u32[]{:S(2)}, u32[]{:S(2)}) collective-permute-start(bf16[1024,512]{1,0:T(8,128)(2,1)} %get-tuple-element.102.refs_3_), channel_id=1, source_target_pairs={{0,16},{16,0},{1,17},{17,1},{2,18},{18,2},{3,19},{19,3},{4,20},{20... | collective-permute-start | bytes 3145736 | tf_op jit(solution)/shard_map/ppermute | solution.py:791
  118.4 48.2 %collective-permute-start.4 = (bf16[512,1024]{1,0:T(8,128)(2,1)}, bf16[512,1024]{1,0:T(8,128)(2,1)}, u32[]{:S(2)}, u32[]{:S(2)}) collective-permute-start(bf16[512,1024]{1,0:T(8,128)(2,1)} %refs_4_.3), channel_id=1, source_target_pairs={{0,16},{16,0},{1,17},{17,1},{2,18},{18,2},{3,19},{19,3},{4,20},{20... | collective-permute-start | bytes 3145736 | tf_op jit(solution)/shard_map/ppermute | solution.py:791
  140.0 14.7 %copy-start.39 = (f32[2,4096]{1,0:T(2,128)S(1)}, f32[2,4096]{1,0:T(2,128)}, u32[]{:S(2)}) copy-start(f32[2,4096]{1,0:T(2,128)} %param.38) | copy-start | bytes 98308
  140.0 14.7 %copy-start.40 = (f32[4096]{0:T(1024)S(1)}, f32[4096]{0:T(1024)}, u32[]{:S(2)}) copy-start(f32[4096]{0:T(1024)} %param.37) | copy-start | bytes 49156
  140.0 16.1 %copy-start.19 = (bf16[1,512,1024]{2,1,0:T(8,128)(2,1)S(1)}, bf16[1,512,1024]{2,1,0:T(8,128)(2,1)}, u32[]{:S(2)}) copy-start(bf16[1,512,1024]{2,1,0:T(8,128)(2,1)} %param.22) | copy-start | bytes 3145732
  140.1 16.1 %copy-start.21 = (bf16[2,256,1024]{2,1,0:T(8,128)(2,1)S(1)}, bf16[2,256,1024]{2,1,0:T(8,128)(2,1)}, u32[]{:S(2)}) copy-start(bf16[2,256,1024]{2,1,0:T(8,128)(2,1)} %param.21) | copy-start | bytes 3145732
  154.0 83.3 %collective-permute-start.3 = (bf16[1024,512]{1,0:T(8,128)(2,1)}, bf16[1024,512]{1,0:T(8,128)(2,1)S(1)}, u32[]{:S(2)}, u32[]{:S(2)}) collective-permute-start(bf16[1024,512]{1,0:T(8,128)(2,1)} %get-tuple-element.95.refs_3_), channel_id=1, source_target_pairs={{0,16},{16,0},{1,17},{17,1},{2,18},{18,2},{3,19},{19,3},{4,20},{20... | collective-permute-start | bytes 3145736 | tf_op jit(solution)/shard_map/ppermute | solution.py:791
  236.5 117.3 %collective-permute-start.6 = (bf16[1024,512]{1,0:T(8,128)(2,1)}, bf16[1024,512]{1,0:T(8,128)(2,1)S(1)}, u32[]{:S(2)}, u32[]{:S(2)}) collective-permute-start(bf16[1024,512]{1,0:T(8,128)(2,1)} %get-tuple-element.105), channel_id=1, source_target_pairs={{16,0},{0,16},{17,1},{1,17},{18,2},{2,18},{19,3},{3,19},{20,4},{4,... | collective-permute-start | bytes 3145736 | tf_op jit(solution)/shard_map/ppermute | solution.py:788
  308.8 45.0 %collective-permute-start.7 = (bf16[1024,512]{1,0:T(8,128)(2,1)}, bf16[1024,512]{1,0:T(8,128)(2,1)S(1)}, u32[]{:S(2)}, u32[]{:S(2)}) collective-permute-start(bf16[1024,512]{1,0:T(8,128)(2,1)} %get-tuple-element.107), channel_id=1, source_target_pairs={{16,0},{0,16},{17,1},{1,17},{18,2},{2,18},{19,3},{3,19},{20,4},{4,... | collective-permute-start | bytes 3145736 | tf_op jit(solution)/shard_map/ppermute | solution.py:788
  367.9 120.6 %collective-permute-start.8 = (bf16[512,1024]{1,0:T(8,128)(2,1)}, bf16[512,1024]{1,0:T(8,128)(2,1)}, u32[]{:S(2)}, u32[]{:S(2)}) collective-permute-start(bf16[512,1024]{1,0:T(8,128)(2,1)} %add_convert_fusion), channel_id=1, source_target_pairs={{16,0},{0,16},{17,1},{1,17},{18,2},{2,18},{19,3},{3,19},{20,4},{4,... | collective-permute-start | bytes 3145736 | tf_op jit(solution)/shard_map/ppermute | solution.py:788
  446.3 78.4 %collective-permute-start.10 = (bf16[1024,1024]{1,0:T(8,128)(2,1)}, bf16[1024,1024]{1,0:T(8,128)(2,1)}, u32[]{:S(2)}, u32[]{:S(2)}) collective-permute-start(bf16[1024,1024]{1,0:T(8,128)(2,1)} %convolution_convert_fusion), channel_id=1, source_target_pairs={{0,16},{16,0},{1,17},{17,1},{2,18},{18,2},{3,19},{19,3},{4,20},{20... | collective-permute-start | bytes 6291464 | tf_op jit(solution)/shard_map/ppermute | solution.py:791
  465.0 23.5 %copy-start.25 = (f32[512,1024]{1,0:T(8,128)S(1)}, f32[512,1024]{1,0:T(8,128)}, u32[]{:S(2)}) copy-start(f32[512,1024]{1,0:T(8,128)} %fusion.24) | copy-start | bytes 6291460
  491.8 23.6 %copy-start.23 = (bf16[1024,1536]{1,0:T(8,128)(2,1)S(1)}, bf16[1024,1536]{1,0:T(8,128)(2,1)}, u32[]{:S(2)}) copy-start(bf16[1024,1536]{1,0:T(8,128)(2,1)} %get-tuple-element.136.refs_7_) | copy-start | bytes 9437188
  520.2 92.6 %collective-permute-start.9 = (bf16[1024,1024]{1,0:T(8,128)(2,1)}, bf16[1024,1024]{1,0:T(8,128)(2,1)}, u32[]{:S(2)}, u32[]{:S(2)}) collective-permute-start(bf16[1024,1024]{1,0:T(8,128)(2,1)} %convolution_convert_fusion.1), channel_id=1, source_target_pairs={{0,16},{16,0},{1,17},{17,1},{2,18},{18,2},{3,19},{19,3},{4,20},{20... | collective-permute-start | bytes 6291464 | tf_op jit(solution)/shard_map/ppermute | solution.py:791
  528.5 8.6 %copy-start.12 = (bf16[4,1024,512]{2,1,0:T(8,128)(2,1)S(1)}, bf16[4,1024,512]{2,1,0:T(8,128)(2,1)}, u32[]{:S(2)}) copy-start(bf16[4,1024,512]{2,1,0:T(8,128)(2,1)} %head_grads.1) | copy-start | bytes 12582916
  613.9 20.6 %collective-permute-start.11 = (bf16[128,2048]{1,0:T(8,128)(2,1)S(1)}, bf16[128,2048]{1,0:T(8,128)(2,1)S(1)}, u32[]{:S(2)}, u32[]{:S(2)}) collective-permute-start(bf16[128,2048]{1,0:T(8,128)(2,1)S(1)} %slice.151), channel_id=1, source_target_pairs={{0,16},{16,0},{1,17},{17,1},{2,18},{18,2},{3,19},{19,3},{4,20},{20... | collective-permute-start | bytes 1572872 | tf_op jit(solution)/shard_map/ppermute | solution.py:791
  (37 other events, 121.6 us)
Sparse Core Ops, SparseCore 0:
  24.7 128.3 all-gather.1
  355.3 179.0 reduce-scatter.1

commit v3 on v2

--- a/solution.py
+++ b/solution.py
@@ -130,49 +130,77 @@
     inner_sum = dot(picks, inner_high, COLUMN_PAIRS) + dot(picks, inner_low, COLUMN_PAIRS)
     scale_sum = jnp.sum(inner, axis=0, keepdims=True) / scale_ref[...]
     count = span // block
+
+    def tile(head, keys_from, keys_to, start, stop, key_head, value_head, key_turned):
+        rows = slice(start, stop)
+        query_block, grad_block = query[rows, :], mixed_grad[rows, :]
+        score = dot(key_head, query_block, COLUMN_PAIRS)
+        shares = jnp.exp2(score * EXPONENT_SCALE - total_ref[0, 0, head : head + 1, rows])
+        key_place = keys_from + lax.broadcasted_iota(jnp.int32, score.shape, 0)
+        allowed = None
+        if start < keys_to:
+            allowed = key_place <= start + lax.broadcasted_iota(jnp.int32, score.shape, 1)
+        if keys_to > span // 2:
+            short = key_place < length
+            allowed = short if allowed is None else allowed & short
+        if allowed is not None:
+            shares = jnp.where(allowed, shares, 0.0)
+        share_grad = dot(value_head, grad_block, COLUMN_PAIRS)
+        score_grad = shares * (share_grad - inner_sum[head : head + 1, rows])
+        score_grad = score_grad.astype(BF)
+        value_term = dot(shares.astype(BF), grad_block)
+        key_term = dot(score_grad, query_block)
+        return value_term, key_term, dot(key_turned, score_grad)
+
+    query_grad[...] = jnp.zeros_like(query_grad)
     for j in range(count):
-        cols = slice(j * block, (j + 1) * block)
+        at = j * block
+        cols = slice(at, at + block)
         key_block, value_block = keys[cols, :], values[cols, :]
-        key_parts, value_parts = [], []
+        heads = []
         for head in range(2):
             mine = first if head == 0 else jnp.logical_not(first)
             key_head = jnp.where(mine, key_block, jnp.zeros_like(key_block))
             value_head = jnp.where(mine, value_block, jnp.zeros_like(value_block))
-            key_sum = value_sum = None
+            key_turned = jnp.transpose(key_head.astype(F32)).astype(BF)
+            heads.append((key_head, value_head, key_turned))
+        sums = [None, None]
+        half = block // 2
+
+        def one(head, i):
+            key_head, value_head, key_turned = heads[head]
+            if i == j and True:
+                parts = []
+                for low, high in ((0, half), (half, block)):
+                    value_term, key_term, query_term = tile(
+                        head, at + low, at + high, at + low, at + block,
+                        key_head[low:high], value_head[low:high], key_turned[:, low:high],
+                    )
+                    query_grad[:, at + low : at + block] += query_term
+                    parts.append((value_term, key_term))
+                terms = [jnp.concatenate(pair, 0) for pair in zip(*parts)]
+            else:
+                start = i * block
+                value_term, key_term, query_term = tile(
+                    head, at, at + block, start, start + block, key_head, value_head, key_turned
+                )
+                query_grad[:, start : start + block] += query_term
+                terms = [value_term, key_term]
+            if sums[head] is None:
+                sums[head] = terms
+            else:
+                sums[head] = [x + y for x, y in zip(sums[head], terms)]
+
+        for head in range(2):
             for i in range(j, count):
-                rows = slice(i * block, (i + 1) * block)
-                query_block, grad_block = query[rows, :], mixed_grad[rows, :]
-                score = dot(key_head, query_block, COLUMN_PAIRS)
-                shares = jnp.exp2(score * EXPONENT_SCALE - total_ref[0, 0, head : head + 1, rows])
-                key_place = lax.broadcasted_iota(jnp.int32, (block, block), 0)
-                allowed = None
-                if i == j:
-                    allowed = key_place <= lax.broadcasted_iota(jnp.int32, (block, block), 1)
-                if (j + 1) * block > span // 2:
-                    short = key_place < length - j * block
-                    allowed = short if allowed is None else allowed & short
-                if allowed is not None:
-                    shares = jnp.where(allowed, shares, 0.0)
-                share_grad = dot(value_head, grad_block, COLUMN_PAIRS)
-                score_grad = shares * (share_grad - inner_sum[head : head + 1, rows])
-                score_grad = score_grad.astype(BF)
-                term = dot(shares.astype(BF), grad_block)
-                value_sum = term if value_sum is None else value_sum + term
-                term = dot(score_grad, query_block)
-                key_sum = term if key_sum is None else key_sum + term
-                term = dot(score_grad, key_head, ROW_PAIRS)
-                if j == 0 and head == 0:
-                    query_grad[rows, :] = term
-                else:
-                    query_grad[rows, :] += term
-            key_parts.append(key_sum)
-            value_parts.append(value_sum)
-        key_grad[cols, :] = (jnp.where(first, *key_parts) * HEAD ** (-0.5)).astype(BF)
-        value_grad[cols, :] = jnp.where(first, *value_parts).astype(BF)
+                one(head, i)
+        value_grad[cols, :] = jnp.where(first, sums[0][0], sums[1][0]).astype(BF)
+        key_grad[cols, :] = (jnp.where(first, sums[0][1], sums[1][1]) * HEAD ** (-0.5)).astype(BF)
+    product[...] = jnp.transpose(query_grad[...])
     query_sum = value_sum = jnp.zeros((1, LANES), F32)
     for slot in range(slots):
         at = pl.ds(place(me, slot, slots, part), part)
-        piece = (query_grad[at, :] * HEAD ** (-0.5)).astype(BF)
+        piece = (product[at, :] * HEAD ** (-0.5)).astype(BF)
         results[slot][:, :LANES] = piece
         results[slot][:, LANES : 2 * LANES] = key_grad[at, :]
         results[slot][:, 2 * LANES :] = value_grad[at, :]
@@ -238,7 +266,7 @@
             out_specs=[attention_specs(slots, span, first_block, 3 * LANES)] * slots
             + [pl.BlockSpec((1, 1, 8, LANES), lambda r, p, *_: (r, p, 0, 0))],
             scratch_shapes=[pltpu.VMEM((span, LANES), BF)] * 4
-            + [pltpu.VMEM((span, LANES), F32)] * 2
+            + [pltpu.VMEM((span, LANES), F32), pltpu.VMEM((LANES, span), F32)]
             + [pltpu.VMEM((span, LANES), BF)] * 2,
         ),
         out_shape=[jax.ShapeDtypeStruct((tokens, pairs * 3 * LANES), BF)] * slots
@@ -452,7 +480,7 @@
 
 def head_grads_kernel(count, *refs):
     rows, grads = refs[:count], refs[count : 2 * count]
-    out_grad, result, total = refs[2 * count :]
+    *out_grads, result, total = refs[2 * count :]
 
     @pl.when(pl.program_id(0) == 0)
     def _():
@@ -471,12 +499,13 @@
         for at in range(0, total.shape[1], LANES):
             pair, kind = divmod(at // LANES, 3)
             result[kind, :, pair * LANES : (pair + 1) * LANES] = total[:, at : at + LANES].astype(BF)
-        part, width = out_grad.shape
+        part, width = out_grads[0].shape
+        out_grad = functools.reduce(jnp.add, [item[...].astype(F32) for item in out_grads])
         for at in range(0, width, part):
             result[3, at : at + part, :] = out_grad[:, at : at + part].astype(BF)
 
 
-def head_grads(rows, grads, out_grad):
+def head_grads(rows, grads, out_grads):
     tokens, width = rows[0].shape
     columns = grads[0].shape[1]
     block = min(512, tokens)
@@ -485,13 +514,13 @@
         grid=(tokens // block,),
         in_specs=[pl.BlockSpec((block, width), lambda i: (i, 0))] * len(rows)
         + [pl.BlockSpec((block, columns), lambda i: (i, 0))] * len(grads)
-        + [pl.BlockSpec(out_grad.shape, lambda i: (0, 0))],
+        + [pl.BlockSpec(item.shape, lambda i: (0, 0)) for item in out_grads],
         out_specs=pl.BlockSpec((4, width, columns // 3), lambda i: (0, 0, 0)),
         out_shape=jax.ShapeDtypeStruct((4, width, columns // 3), BF),
         scratch_shapes=[pltpu.VMEM((width, columns), F32)],
         compiler_params=pltpu.CompilerParams(vmem_limit_bytes=56 * 2**20),
         name="head_grads",
-    )(*rows, *grads, out_grad)
+    )(*rows, *grads, *out_grads)
 
 
 def partner(name, bit):
@@ -672,6 +701,67 @@
     )(value)
 
 
+def unproject(grads, weights):
+    total = None
+    for kind in range(3):
+        pieces = [
+            grads[:, at : at + LANES] for at in range(kind * LANES, grads.shape[1], 3 * LANES)
+        ]
+        piece = pieces[0] if len(pieces) == 1 else jnp.concatenate(pieces, 1)
+        term = dot(piece, weights[kind], COLUMN_PAIRS)
+        total = term if total is None else total + term
+    return total.astype(BF)
+
+
+def unproject_kernel(grads, weights, result):
+    result[...] = unproject(grads, weights)
+
+
+def unproject_pass(grads, weights):
+    tokens, columns = grads.shape
+    width = weights.shape[1]
+    block = min(256, tokens)
+    return pl.pallas_call(
+        unproject_kernel,
+        grid=(tokens // block,),
+        in_specs=[
+            pl.BlockSpec((block, columns), lambda i: (i, 0)),
+            pl.BlockSpec(weights.shape, lambda i: (0, 0, 0), pipeline_mode=pl.Buffered(1)),
+        ],
+        out_specs=pl.BlockSpec((block, width), lambda i: (i, 0)),
+        out_shape=jax.ShapeDtypeStruct((tokens, width), BF),
+        compiler_params=pltpu.CompilerParams(vmem_limit_bytes=40 * 2**20),
+        name="unproject",
+    )(grads, weights)
+
+
+def out_grads_kernel(groups, slots, *refs):
+    grads, scaled, results = refs[:groups], refs[groups:-slots], refs[-slots:]
+    for slot, result in enumerate(results):
+        total = functools.reduce(
+            jnp.add,
+            [
+                dot(scaled[group * slots + slot][...], grads[group][...], ROW_PAIRS)
+                for group in range(groups)
+            ],
+        )
+        result[...] = total.astype(BF)
+
+
+def out_grads_pass(grads, scaled):
+    slots = len(scaled[0])
+    part, width = scaled[0][0].shape[1], grads[0].shape[1]
+    items = [*grads, *[item for group in scaled for item in group]]
+    return pl.pallas_call(
+        functools.partial(out_grads_kernel, len(grads), slots),
+        in_specs=[pl.BlockSpec(memory_space=pltpu.VMEM)] * len(items),
+        out_specs=[pl.BlockSpec(memory_space=pltpu.VMEM)] * slots,
+        out_shape=[jax.ShapeDtypeStruct((part, width), BF)] * slots,
+        compiler_params=pltpu.CompilerParams(vmem_limit_bytes=40 * 2**20),
+        name="out_grads",
+    )(*items)
+
+
 def first_back_kernel(count, rows_ref, grad_ref, weights, gains, shifts, residual_ref, *refs):
     arrived = refs[:count]
     result, sums_ref = refs[count:]
@@ -680,7 +770,7 @@
     def _():
         sums_ref[...] = jnp.zeros_like(sums_ref)
 
-    grad = dot(grad_ref[...], weights[...], COLUMN_PAIRS).astype(BF).astype(F32)
+    grad = unproject(grad_ref, weights).astype(F32)
     for term in arrived:
         grad = grad + term[...].astype(F32)
     gain = gains[0:1, :]
@@ -704,7 +794,8 @@
         return pl.BlockSpec((block, columns), lambda i: (i, 0))
 
     def whole(array):
-        return pl.BlockSpec(array.shape, lambda i: (0, 0), pipeline_mode=pl.Buffered(1))
+        zeros = (0,) * array.ndim
+        return pl.BlockSpec(array.shape, lambda i: zeros, pipeline_mode=pl.Buffered(1))
 
     return pl.pallas_call(
         functools.partial(first_back_kernel, len(arrived)),
@@ -781,7 +872,6 @@
     shapes = tuple((item.shape for item in (short_rows, medium_rows, long_rows)))
     width = short_rows.shape[2]
     part = head_weights.shape[2]
-    pairs = part // LANES
     me = lax.axis_index("head").astype(jnp.int32).reshape(1)
 
     def fetch(value, slot):
@@ -809,9 +899,6 @@
     medium_job = (medium_len, counts[1], spans[1], short_tokens // shapes[1][1])
     jobs = ([long_job], [short_job, medium_job])
 
-    weights = (
-        head_weights.reshape(3, width, pairs, LANES).transpose(1, 2, 0, 3).reshape(width, 3 * part)
-    )
     biases = jnp.stack([head_biases[0], jnp.zeros_like(head_biases[0]), head_biases[1]])
     scale_lanes = jnp.repeat(head_scale, HEAD).reshape(1, part)
 
@@ -835,9 +922,7 @@
     feed = lax.all_gather(feed, "batch", axis=0, tiled=True)
     own_qkv = [project(rows, head_weights, biases) for rows in lows]
     arrived = [fetch(lows[0], slot) for slot in range(1, slots)]
-    own_qkv, arrived, lows[1], weights = lax.optimization_barrier(
-        (own_qkv, arrived, lows[1], weights)
-    )
+    own_qkv, arrived, lows[1] = lax.optimization_barrier((own_qkv, arrived, lows[1]))
     normed_slots = [
         [lows[0], *arrived],
         [lows[1]] + [fetch(lows[1], slot) for slot in range(1, slots)],
@@ -857,7 +942,7 @@
         saved.append((outs, totals))
         scaled.append(spread(outs, deliver))
 
-    outputs, residual_grads, grad_slots, sums, mid_sums, out_grads = [], [], [], [], [], []
+    outputs, residual_grads, grad_slots, sums, mid_sums, attended_grads = [], [], [], [], [], []
     middles, hidden_grads, denses = [], [], []
     for group in range(2):
         results = middle_pass(
@@ -880,12 +965,9 @@
         sums.append(results[6])
         mid_sums.append(results[7])
         grad_slots.append(spread(results[8:], fetch))
-        terms = [dot(rows, results[3], ROW_PAIRS) for rows in scaled[group]]
-        out_grads = terms if not out_grads else [a + b for a, b in zip(out_grads, terms)]
+        attended_grads.append(results[3])
     both = feed_grads(middles, hidden_grads, cots, denses)
-    out_grad = out_grads[0]
-    for slot in range(1, slots):
-        out_grad = out_grad + fetch(out_grads[slot].astype(BF), slot).astype(F32)
+    out_grads = spread(out_grads_pass(attended_grads, scaled), fetch)
     grad_slots, both = lax.optimization_barrier((grad_slots, both))
     both = lax.psum_scatter(both, "batch", scatter_dimension=0, tiled=True)
 
@@ -894,7 +976,7 @@
 
     def send_back(qkv_grad):
         return [
-            deliver(dot(qkv_grad[slot], weights, COLUMN_PAIRS).astype(BF), slot)
+            deliver(unproject_pass(qkv_grad[slot], head_weights), slot)
             for slot in range(1, slots)
         ]
 
@@ -902,7 +984,7 @@
         grad, group_sums = first_back(
             inputs[group],
             qkv_grads[group][0],
-            weights,
+            head_weights,
             norm_gains,
             norm_shifts,
             residual_grads[group],
@@ -935,7 +1017,7 @@
     weight_grad = head_grads(
         [rows for group in normed_slots for rows in group],
         [piece for group in qkv_grads for piece in group],
-        out_grad,
+        out_grads,
     )
     qkv_grads[1], weight_grad = lax.optimization_barrier((qkv_grads[1], weight_grad))
     arrived_last = send_back(qkv_grads[1])

time: 662 us -> 638 us (0.964)
  matrix products: 22.9 us -> 0 us
    dot_general x6 -> x0, matrix products: 22.9 us -> none  [dot(): return lax.dot_general(a, b, dims, preferred_element_type=F32)]
    pallas_call x0 -> x3, Pallas kernels: none -> 16.9 us  [the longest x2 9.75 us: unproject_pass(): pl.pallas_call(unproject_kernel, grid=(tokens // block,), in_specs=[pl.Bl...]
    pallas_call x3, Pallas kernels: 108 us -> 93.2 us  [attend_backward(): call(me, lengths, *qkv, *outs, *grads, scale_lanes, log_total, *kept)]
    ppermute x6, waiting for transfers between devices: 28.8 us -> 35.8 us  [fetch(): lax.ppermute(value, 'head', [((d + slot) % slots, d) for d in range(slots)])]
    unnamed x92 -> x81, local copies, waits for them, and re-layouts: 23.3 us -> 24.3 us
  transfers between devices with their start and end apart: 14 -> 14, of which waited for: 3 -> 3; matrix products, arithmetic and copies ran while one was open for 10% -> 5% of each run, Pallas kernels for 74% -> 76%
where the time goes in v3:
time: 638 us; the launch traced here: 634 us
  Pallas kernels  497 us (78%)
  waiting for transfers between devices  41.5 us (7%)
  local copies, waits for them, and re-layouts  39.2 us (6%)
  other arithmetic  22.9 us (4%)
  starting transfers between devices  17.1 us (3%)
  between operations  16.2 us (3%)
    pallas_call x2, Pallas kernels, middle_pass(): call(rows, cotangent, *scaled, *out_weights, feed, gains, shifts, mid_gai...  140 us
    pallas_call x3, Pallas kernels, attend_backward(): call(me, lengths, *qkv, *outs, *grads, scale_lanes, log_total, *kept)  93.2 us
    pallas_call x1, Pallas kernels, batch_sum(): pl.pallas_call(functools.partial(batch_sum_kernel, bits, chunks, steps),...  70.7 us
    pallas_call x3, Pallas kernels, attend_forward(): *outs, log_total = call(me, lengths, *qkv, scale_lanes, *kept)  62.5 us
    pallas_call x1, Pallas kernels, feed_grads(): pl.pallas_call(functools.partial(feed_grads_kernel, groups), grid=(hidden...  43.6 us
    ppermute x6, waiting for transfers between devices, fetch(): lax.ppermute(value, 'head', [((d + slot) % slots, d) for d in range(slots)])  35.8 us
    unnamed x81, local copies, waits for them, and re-layouts  24.3 us
    pallas_call x1, Pallas kernels, head_grads(): pl.pallas_call(functools.partial(head_grads_kernel, len(rows)), grid=(tok...  23.4 us
  transfers between devices with their start and end apart: 14, of which 3 were waited for; matrix products, arithmetic and copies ran while one was open for 5% of the time, Pallas kernels for 76%

profile of v3, /device:TPU:0, one launch (start us, length us, event | category | flops | bytes accessed | tf_op | source)
XLA Modules:
  0.0 634.0 jit_solution(5972694491350030453)
XLA Ops:
  26.8 5.2 project.5.refs_0_
  33.7 4.0 project.4.refs_0_
  39.4 32.6 %collective-permute-done.1.rows_ref.refs_1_ = bf16[1024,1024]{1,0:T(8,128)(2,1)S(1)} collective-permute-done((bf16[1024,1024]{1,0:T(8,128)(2,1)}, bf16[1024,1024]{1,0:T(8,128)(2,1)S(1)}, u32[]{:S(2)}, u32[]{:S(2)}) %collective-permute-start.1) | collective-permute-done | bytes 2097184 | tf_op jit(solution)/shard_map/ppermute | solution.py:878
  77.8 4.0 project.7.refs_1_
  83.4 35.8 %attend_forward.5 = (bf16[1024,512]{1,0:T(8,128)(2,1)}, bf16[1024,512]{1,0:T(8,128)(2,1)}, f32[4,1,2,2048]{3,2,1,0:T(2,128)}) custom-call(s32[1]{0:T(128)} %bitcast.4.me_ref, s32[1]{0:T(128)S(6)} %copy.55.len_ref, bf16[1024,1536]{1,0:T(8,128)(2,1)} %copy-done.5, bf16[1024,1536]{1,0:T(8,128)(2,1)} %copy-done.6, f32[1,512]{1,0:T(1,128)} %reshape_reshape.3.refs_2_.refs_6_), custom_call_target="tpu_custom_call" | custom-call | tf_op jit(solution)/shard_map/attend_forward/pallas_call | solution.py:243
  121.9 5.2 project.6.refs_1_
  128.8 12.9 %attend_forward.3 = (bf16[1024,512]{1,0:T(8,128)(2,1)}, bf16[1024,512]{1,0:T(8,128)(2,1)}, f32[4,2,2,512]{3,2,1,0:T(2,128)}) custom-call(s32[1]{0:T(128)} %bitcast.4.me_ref, s32[2]{0:T(128)} %len_ref.7, bf16[1024,1536]{1,0:T(8,128)(2,1)} %copy-done.1, bf16[1024,1536]{1,0:T(8,128)(2,1)} %copy-done.2, f32[1,512]{1,0:T(1,128)} %reshape_reshape.3.refs_2_.refs_6_), custom_call_target="tpu_custom_call" | custom-call | tf_op jit(solution)/shard_map/attend_forward/pallas_call | solution.py:243
  141.7 13.8 %attend_forward.4 = (bf16[1024,512]{1,0:T(8,128)(2,1)}, bf16[1024,512]{1,0:T(8,128)(2,1)}, f32[4,1,2,1024]{3,2,1,0:T(2,128)}) custom-call(s32[1]{0:T(128)} %bitcast.4.me_ref, s32[1]{0:T(128)S(6)} %copy.54.len_ref, bf16[1024,1536]{1,0:T(8,128)(2,1)} %copy-done.1, bf16[1024,1536]{1,0:T(8,128)(2,1)} %copy-done.2, ...), custom_call_target="tpu_custom_call", output_to_operand_aliasing={{0}: (5, {}), {1}: (6, {})} | custom-call | tf_op jit(solution)/shard_map/attend_forward/pallas_call | solution.py:243
  162.4 5.7 collective-permute-done.4.refs_5_
  168.1 69.9 %middle_pass.3 = (bf16[1024,1024]{1,0:T(8,128)(2,1)}, f32[1024,1024]{1,0:T(8,128)}, bf16[1024,1024]{1,0:T(8,128)(2,1)}, bf16[1024,1024]{1,0:T(8,128)(2,1)}, bf16...) custom-call(bf16[1024,1024]{1,0:T(8,128)(2,1)} %bitcast.65, ...), custom_call_target="tpu_custom_call" | custom-call | tf_op jit(solution)/shard_map/middle_pass/pallas_call | solution.py:443
  238.9 70.5 %middle_pass.2 = (bf16[1024,1024]{1,0:T(8,128)(2,1)}, f32[1024,1024]{1,0:T(8,128)}, bf16[1024,1024]{1,0:T(8,128)(2,1)}, bf16[1024,1024]{1,0:T(8,128)(2,1)}, bf16...) custom-call(bf16[1024,1024]{1,0:T(8,128)(2,1)} %pad_maximum_fusion.r, ...), custom_call_target="tpu_custom_call" | custom-call | tf_op jit(solution)/shard_map/middle_pass/pallas_call | solution.py:443
  310.7 43.6 %feed_grads.1 = bf16[4096,2048]{1,0:T(8,128)(2,1)} custom-call(bf16[1024,4096]{1,0:T(8,128)(2,1)} %get-tuple-element.109.refs_0_, bf16[1024,4096]{1,0:T(8,128)(2,1)} %get-tuple-element.110.refs_1_, bf16[1024,4096]{1,0:T(8,128)(2,1)} %get-tuple-element.111.refs_2_, bf16[1024,4096]{1,0:T(8,128)(2,1)} %get-tuple-element.112.refs_3_, ...), custom_call_target="tpu_custom_call" | custom-call | tf_op jit(solution)/shard_map/feed_grads/pallas_call | solution.py:469
  360.0 7.1 %out_grads.1 = (bf16[512,1024]{1,0:T(8,128)(2,1)S(1)}, bf16[512,1024]{1,0:T(8,128)(2,1)}) custom-call(bf16[1024,1024]{1,0:T(8,128)(2,1)S(1)} %copy-done.19, bf16[1024,1024]{1,0:T(8,128)(2,1)S(1)} %copy-done.20, bf16[1024,512]{1,0:T(8,128)(2,1)S(1)} %copy-done.15, bf16[1024,512]{1,0:T(8,128)(2,1)} %collective-permute-done.5.refs_3_, ...), custom_call_target="tpu_custom_call" | custom-call | tf_op jit(solution)/shard_map/out_grads/pallas_call | solution.py:755
  368.9 57.7 %attend_backward.3 = (bf16[1024,1536]{1,0:T(8,128)(2,1)}, bf16[1024,1536]{1,0:T(8,128)(2,1)}, f32[1,4,8,128]{3,2,1,0:T(8,128)}) custom-call(s32[1]{0:T(128)} %bitcast.4.me_ref, s32[1]{0:T(128)S(6)} %copy.55.len_ref, bf16[1024,1536]{1,0:T(8,128)(2,1)} %copy-done.5, bf16[1024,1536]{1,0:T(8,128)(2,1)} %copy-done.6, ...), custom_call_target="tpu_custom_call" | custom-call | tf_op jit(solution)/shard_map/attend_backward/pallas_call | solution.py:278
  428.7 4.9 unproject.3
  435.0 16.3 %attend_backward.4 = (bf16[1024,1536]{1,0:T(8,128)(2,1)}, bf16[1024,1536]{1,0:T(8,128)(2,1)}, f32[2,4,8,128]{3,2,1,0:T(8,128)}) custom-call(s32[1]{0:T(128)} %bitcast.4.me_ref, s32[2]{0:T(128)} %len_ref.7, bf16[1024,1536]{1,0:T(8,128)(2,1)} %copy-done.1, bf16[1024,1536]{1,0:T(8,128)(2,1)} %copy-done.2, bf16[1024,512]{1,0:T(8,128)(2,1)} %get-tuple-element.95.refs_2_.refs_4_, ...), custom_call_target="tpu_custom_call" | custom-call | tf_op jit(solution)/shard_map/attend_backward/pallas_call | solution.py:278
  451.3 19.3 %attend_backward.5 = (bf16[1024,1536]{1,0:T(8,128)(2,1)}, bf16[1024,1536]{1,0:T(8,128)(2,1)}, f32[1,4,8,128]{3,2,1,0:T(8,128)}) custom-call(s32[1]{0:T(128)} %bitcast.4.me_ref, s32[1]{0:T(128)S(6)} %copy.54.len_ref, bf16[1024,1536]{1,0:T(8,128)(2,1)} %copy-done.1, bf16[1024,1536]{1,0:T(8,128)(2,1)} %copy-done.2, ...), custom_call_target="tpu_custom_call", output_to_operand_aliasing={{0}: (10, {}), {1}: (11, {})} | custom-call | tf_op jit(solution)/shard_map/attend_backward/pallas_call | solution.py:278
  470.6 23.4 %head_grads.1 = bf16[4,1024,512]{2,1,0:T(8,128)(2,1)} custom-call(bf16[1024,1024]{1,0:T(8,128)(2,1)} %get-tuple-element.90.rows_ref.refs_0_, bf16[1024,1024]{1,0:T(8,128)(2,1)} %copy-done.16, bf16[1024,1024]{1,0:T(8,128)(2,1)} %get-tuple-element.92.rows_ref.refs_2_, bf16[1024,1024]{1,0:T(8,128)(2,1)} %collective-permute-done.2.rows_ref.refs_3_, ...), custom_call_target="tpu_custom_call" | custom-call | tf_op jit(solution)/shard_map/head_grads/pallas_call | solution.py:512
  494.0 4.9 unproject.2
  506.6 8.5 %first_back.2 = (bf16[1024,1024]{1,0:T(8,128)(2,1)}, f32[8,1024]{1,0:T(8,128)S(1)}) custom-call(bf16[1024,1024]{1,0:T(8,128)(2,1)S(1)} %bitcast.66, bf16[1024,1536]{1,0:T(8,128)(2,1)S(1)} %copy-done.13, bf16[3,1024,512]{2,1,0:T(8,128)(2,1)S(1)} %copy-done, f32[3,1024]{1,0:T(4,128)S(1)} %copy-done.23, f32[5,1024]{1,0:T(8,128)S(1)} %copy-done.22, ...), custom_call_target="tpu_custom_call" | custom-call | tf_op jit(solution)/shard_map/first_back/pallas_call | solution.py:800
  515.1 70.7 %batch_sum.1 = (bf16[4096,512]{1,0:T(8,128)(2,1)S(1)}, f32[168,128]{1,0:T(8,128)S(1)}) custom-call(bf16[4096,512]{1,0:T(8,128)(2,1)S(1)} %bitcast.67, f32[168,128]{1,0:T(8,128)S(1)} %maximum_bitcast_fusion.extra), custom_call_target="tpu_custom_call" | custom-call | tf_op jit(solution)/shard_map/batch_sum/pallas_call | solution.py:641
  597.5 3.8 convert.1
  601.6 7.3 %first_back.3 = (bf16[1024,1024]{1,0:T(8,128)(2,1)S(1)}, f32[8,1024]{1,0:T(8,128)S(1)}) custom-call(bf16[1024,1024]{1,0:T(8,128)(2,1)S(1)} %copy-done.10, bf16[1024,1536]{1,0:T(8,128)(2,1)S(1)} %copy-done.7, bf16[3,1024,512]{2,1,0:T(8,128)(2,1)S(1)} %copy-done, f32[3,1024]{1,0:T(4,128)S(1)} %copy-done.23, f32[5,1024]{1,0:T(8,128)S(1)} %copy-done.22, ...), custom_call_target="tpu_custom_call" | custom-call | tf_op jit(solution)/shard_map/first_back/pallas_call | solution.py:800
  613.2 12.5 %small_sum.1 = f32[16,128]{1,0:T(8,128)S(1)} custom-call(f32[16,128]{1,0:T(8,128)S(1)} %reshape.195.source), custom_call_target="tpu_custom_call" | custom-call | tf_op jit(solution)/shard_map/small_sum/pallas_call | solution.py:690
  (177 shorter events, 78.6 us)
Async XLA Ops:
  7.2 6.2 copy-start.24
  7.2 8.3 %copy-start.3 = (bf16[1,1024,1024]{2,1,0:T(8,128)(2,1)S(1)}, bf16[1,1024,1024]{2,1,0:T(8,128)(2,1)}, u32[]{:S(2)}) copy-start(bf16[1,1024,1024]{2,1,0:T(8,128)(2,1)} %param.23) | copy-start | bytes 6291460
  7.2 160.9 %all-gather.2.cloned.1.call-start = ((), (), s32[]{:S(2)}) async-start(), calls=%async_computation.1 | async-start | bytes 17825792 | tf_op jit(solution)/shard_map/all_gather | solution.py:922
  8.5 15.0 %collective-permute-start = (bf16[2,128,1024]{2,1,0:T(8,128)(2,1)S(1)}, bf16[2,128,1024]{2,1,0:T(8,128)(2,1)S(1)}, u32[]{:S(2)}, u32[]{:S(2)}) collective-permute-start(bf16[2,128,1024]{2,1,0:T(8,128)(2,1)S(1)} %get-tuple-element.172), channel_id=1, source_target_pairs={{16,0},{0,16},{17,1},{1,17},{18,2},{2,18},{19,3},{3,19},{20,4},{4,... | collective-permute-start | bytes 1572872 | tf_op jit(solution)/shard_map/ppermute | solution.py:878
  20.3 6.5 %copy-start.38 = (f32[2,512]{1,0:T(2,128)S(1)}, f32[2,512]{1,0:T(2,128)}, u32[]{:S(2)}) copy-start(f32[2,512]{1,0:T(2,128)} %param.33) | copy-start | bytes 12292
  20.3 6.6 %copy-start = (bf16[3,1024,512]{2,1,0:T(8,128)(2,1)S(1)}, bf16[3,1024,512]{2,1,0:T(8,128)(2,1)}, u32[]{:S(2)}) copy-start(bf16[3,1024,512]{2,1,0:T(8,128)(2,1)} %weights.15) | copy-start | bytes 9437188
  24.6 565.9 %reduce-scatter.2.cloned.1.call-start = ((), (), s32[]{:S(2)}) async-start(), calls=%async_computation.2 | async-start | bytes 17825792 | tf_op jit(solution)/shard_map/reduce_scatter | solution.py:972
  24.9 47.1 %collective-permute-start.1 = (bf16[1024,1024]{1,0:T(8,128)(2,1)}, bf16[1024,1024]{1,0:T(8,128)(2,1)S(1)}, u32[]{:S(2)}, u32[]{:S(2)}) collective-permute-start(bf16[1024,1024]{1,0:T(8,128)(2,1)} %get-tuple-element.90.rows_ref.refs_0_), channel_id=1, source_target_pairs={{16,0},{0,16},{17,1},{1,17},{18,2},{2,18},{19,3},{3,19},{20,4},{4,... | collective-permute-start | bytes 6291464 | tf_op jit(solution)/shard_map/ppermute | solution.py:878
  26.8 6.9 %copy-start.11 = (bf16[1024,1024]{1,0:T(8,128)(2,1)S(1)}, bf16[1024,1024]{1,0:T(8,128)(2,1)}, u32[]{:S(2)}) copy-start(bf16[1024,1024]{1,0:T(8,128)(2,1)} %get-tuple-element.90.rows_ref.refs_0_) | copy-start | bytes 6291460
  33.7 41.1 %copy-start.39 = (f32[8]{0:T(128)S(1)}, f32[8]{0:T(128)}, u32[]{:S(2)}) copy-start(f32[8]{0:T(128)} %param.34) | copy-start | bytes 100
  73.3 46.6 %collective-permute-start.2 = (bf16[1024,1024]{1,0:T(8,128)(2,1)}, bf16[1024,1024]{1,0:T(8,128)(2,1)}, u32[]{:S(2)}, u32[]{:S(2)}) collective-permute-start(bf16[1024,1024]{1,0:T(8,128)(2,1)} %get-tuple-element.92.rows_ref.refs_2_), channel_id=1, source_target_pairs={{16,0},{0,16},{17,1},{1,17},{18,2},{2,18},{19,3},{3,19},{20,4},{4,... | collective-permute-start | bytes 6291464 | tf_op jit(solution)/shard_map/ppermute | solution.py:878
  119.2 43.2 %collective-permute-start.5 = (bf16[1024,512]{1,0:T(8,128)(2,1)}, bf16[1024,512]{1,0:T(8,128)(2,1)}, u32[]{:S(2)}, u32[]{:S(2)}) collective-permute-start(bf16[1024,512]{1,0:T(8,128)(2,1)} %get-tuple-element.103.refs_3_), channel_id=1, source_target_pairs={{0,16},{16,0},{1,17},{17,1},{2,18},{18,2},{3,19},{19,3},{4,20},{20... | collective-permute-start | bytes 3145736 | tf_op jit(solution)/shard_map/ppermute | solution.py:881
  119.9 48.2 %collective-permute-start.4 = (bf16[512,1024]{1,0:T(8,128)(2,1)}, bf16[512,1024]{1,0:T(8,128)(2,1)}, u32[]{:S(2)}, u32[]{:S(2)}) collective-permute-start(bf16[512,1024]{1,0:T(8,128)(2,1)} %refs_4_.3), channel_id=1, source_target_pairs={{0,16},{16,0},{1,17},{17,1},{2,18},{18,2},{3,19},{19,3},{4,20},{20... | collective-permute-start | bytes 3145736 | tf_op jit(solution)/shard_map/ppermute | solution.py:881
  141.7 14.6 %copy-start.34 = (f32[2,4096]{1,0:T(2,128)S(1)}, f32[2,4096]{1,0:T(2,128)}, u32[]{:S(2)}) copy-start(f32[2,4096]{1,0:T(2,128)} %param.38) | copy-start | bytes 98308
  141.7 14.7 %copy-start.35 = (f32[4096]{0:T(1024)S(1)}, f32[4096]{0:T(1024)}, u32[]{:S(2)}) copy-start(f32[4096]{0:T(1024)} %param.37) | copy-start | bytes 49156
  155.5 83.4 %collective-permute-start.3 = (bf16[1024,512]{1,0:T(8,128)(2,1)}, bf16[1024,512]{1,0:T(8,128)(2,1)}, u32[]{:S(2)}, u32[]{:S(2)}) collective-permute-start(bf16[1024,512]{1,0:T(8,128)(2,1)} %get-tuple-element.96.refs_3_), channel_id=1, source_target_pairs={{0,16},{16,0},{1,17},{17,1},{2,18},{18,2},{3,19},{19,3},{4,20},{20... | collective-permute-start | bytes 3145736 | tf_op jit(solution)/shard_map/ppermute | solution.py:881
  238.1 116.3 %collective-permute-start.6 = (bf16[1024,512]{1,0:T(8,128)(2,1)}, bf16[1024,512]{1,0:T(8,128)(2,1)}, u32[]{:S(2)}, u32[]{:S(2)}) collective-permute-start(bf16[1024,512]{1,0:T(8,128)(2,1)} %get-tuple-element.106), channel_id=1, source_target_pairs={{16,0},{0,16},{17,1},{1,17},{18,2},{2,18},{19,3},{3,19},{20,4},{4,... | collective-permute-start | bytes 3145736 | tf_op jit(solution)/shard_map/ppermute | solution.py:878
  309.4 45.0 %collective-permute-start.7 = (bf16[1024,512]{1,0:T(8,128)(2,1)}, bf16[1024,512]{1,0:T(8,128)(2,1)}, u32[]{:S(2)}, u32[]{:S(2)}) collective-permute-start(bf16[1024,512]{1,0:T(8,128)(2,1)} %get-tuple-element.108), channel_id=1, source_target_pairs={{16,0},{0,16},{17,1},{1,17},{18,2},{2,18},{19,3},{3,19},{20,4},{4,... | collective-permute-start | bytes 3145736 | tf_op jit(solution)/shard_map/ppermute | solution.py:878
  368.1 102.4 %collective-permute-start.8 = (bf16[512,1024]{1,0:T(8,128)(2,1)}, bf16[512,1024]{1,0:T(8,128)(2,1)}, u32[]{:S(2)}, u32[]{:S(2)}) collective-permute-start(bf16[512,1024]{1,0:T(8,128)(2,1)} %get-tuple-element.135), channel_id=1, source_target_pairs={{16,0},{0,16},{17,1},{1,17},{18,2},{2,18},{19,3},{3,19},{20,4},{4,... | collective-permute-start | bytes 3145736 | tf_op jit(solution)/shard_map/ppermute | solution.py:878
  433.6 69.4 %collective-permute-start.10 = (bf16[1024,1024]{1,0:T(8,128)(2,1)}, bf16[1024,1024]{1,0:T(8,128)(2,1)}, u32[]{:S(2)}, u32[]{:S(2)}) collective-permute-start(bf16[1024,1024]{1,0:T(8,128)(2,1)} %unproject.3), channel_id=1, source_target_pairs={{0,16},{16,0},{1,17},{17,1},{2,18},{18,2},{3,19},{19,3},{4,20},{20... | collective-permute-start | bytes 6291464 | tf_op jit(solution)/shard_map/ppermute | solution.py:881
  470.6 23.4 %copy-start.8 = (bf16[1024,1536]{1,0:T(8,128)(2,1)S(1)}, bf16[1024,1536]{1,0:T(8,128)(2,1)}, u32[]{:S(2)}) copy-start(bf16[1024,1536]{1,0:T(8,128)(2,1)} %get-tuple-element.138.refs_7_.grads) | copy-start | bytes 9437188
  498.9 91.6 %collective-permute-start.9 = (bf16[1024,1024]{1,0:T(8,128)(2,1)}, bf16[1024,1024]{1,0:T(8,128)(2,1)}, u32[]{:S(2)}, u32[]{:S(2)}) collective-permute-start(bf16[1024,1024]{1,0:T(8,128)(2,1)} %unproject.2), channel_id=1, source_target_pairs={{0,16},{16,0},{1,17},{17,1},{2,18},{18,2},{3,19},{19,3},{4,20},{20... | collective-permute-start | bytes 6291464 | tf_op jit(solution)/shard_map/ppermute | solution.py:881
  506.6 8.5 %copy-start.12 = (bf16[4,1024,512]{2,1,0:T(8,128)(2,1)S(1)}, bf16[4,1024,512]{2,1,0:T(8,128)(2,1)}, u32[]{:S(2)}) copy-start(bf16[4,1024,512]{2,1,0:T(8,128)(2,1)} %head_grads.1) | copy-start | bytes 12582916
  591.6 20.4 %collective-permute-start.11 = (bf16[128,2048]{1,0:T(8,128)(2,1)S(1)}, bf16[128,2048]{1,0:T(8,128)(2,1)S(1)}, u32[]{:S(2)}, u32[]{:S(2)}) collective-permute-start(bf16[128,2048]{1,0:T(8,128)(2,1)S(1)} %slice.151), channel_id=1, source_target_pairs={{0,16},{16,0},{1,17},{17,1},{2,18},{18,2},{3,19},{19,3},{4,20},{20... | collective-permute-start | bytes 1572872 | tf_op jit(solution)/shard_map/ppermute | solution.py:881
  (32 other events, 95.0 us)
Sparse Core Ops, SparseCore 0:
  24.7 128.3 all-gather.1
  354.5 182.2 reduce-scatter.1

commit v4 on v3

--- a/solution.py
+++ b/solution.py
@@ -880,6 +880,18 @@
     def deliver(value, slot):
         return lax.ppermute(value, "head", [(d, (d + slot) % slots) for d in range(slots)])
 
+    def deliver_shared(value, slot):
+        size = lax.axis_size("batch")
+        half = value.shape[0] // 2
+        if size % 2 or half % 16:
+            return deliver(value, slot)
+        odd = lax.rem(lax.axis_index("batch"), 2).astype(jnp.int32)
+        mine = deliver(lax.dynamic_slice_in_dim(value, odd * half, half, 0), slot)
+        other = lax.ppermute(mine, "batch", [(d, d ^ 1) for d in range(size)])
+        return jnp.where(
+            odd == 0, jnp.concatenate([mine, other], 0), jnp.concatenate([other, mine], 0)
+        )
+
     def spread(own, move):
         return [own[slot] if slot == 0 else move(own[slot], slot) for slot in range(slots)]
 
@@ -922,14 +934,13 @@
     feed = lax.all_gather(feed, "batch", axis=0, tiled=True)
     own_qkv = [project(rows, head_weights, biases) for rows in lows]
     arrived = [fetch(lows[0], slot) for slot in range(1, slots)]
-    own_qkv, arrived, lows[1] = lax.optimization_barrier((own_qkv, arrived, lows[1]))
+    own_qkv, arrived, lows[1], inputs[1], cots[1] = lax.optimization_barrier(
+        (own_qkv, arrived, lows[1], inputs[1], cots[1])
+    )
     normed_slots = [
         [lows[0], *arrived],
         [lows[1]] + [fetch(lows[1], slot) for slot in range(1, slots)],
     ]
-    out_weights, _ = lax.optimization_barrier((out_weight, normed_slots[-1][1:]))
-    out_weights = [out_weight] + [deliver(out_weights, slot) for slot in range(1, slots)]
-
     qkv, saved, scaled = [], [], []
     for group in range(2):
         projected = [own_qkv[group]]
@@ -940,6 +951,11 @@
             outs, log_total = attend_forward(me, job[0], projected, scale_lanes, outs, *job[1:])
             totals.append(log_total)
         saved.append((outs, totals))
+        if group == 0:
+            outs, other_weight = lax.optimization_barrier((outs, out_weight))
+            out_weights = [out_weight] + [
+                deliver_shared(other_weight, slot) for slot in range(1, slots)
+            ]
         scaled.append(spread(outs, deliver))
 
     outputs, residual_grads, grad_slots, sums, mid_sums, attended_grads = [], [], [], [], [], []

time: 638 us -> 635 us (level)
  waiting for transfers between devices: 41.5 us -> 33.8 us
    unnamed x81 -> x87, local copies, waits for them, and re-layouts: 24.3 us -> 24.4 us
  transfers between devices with their start and end apart: 14 -> 15, of which waited for: 3 -> 3; matrix products, arithmetic and copies ran while one was open for 5% -> 5% of each run, Pallas kernels for 76% -> 77%
where the time goes in v4:
time: 635 us; the launch traced here: 630 us
  Pallas kernels  501 us (79%)
  local copies, waits for them, and re-layouts  39.2 us (6%)
  waiting for transfers between devices  33.8 us (5%)
  other arithmetic  23.7 us (4%)
  starting transfers between devices  16.4 us (3%)
  between operations  16.3 us (3%)
    pallas_call x2, Pallas kernels, middle_pass(): call(rows, cotangent, *scaled, *out_weights, feed, gains, shifts, mid_gai...  140 us
    pallas_call x3, Pallas kernels, attend_backward(): call(me, lengths, *qkv, *outs, *grads, scale_lanes, log_total, *kept)  93 us
    pallas_call x1, Pallas kernels, batch_sum(): pl.pallas_call(functools.partial(batch_sum_kernel, bits, chunks, steps),...  70.5 us
    pallas_call x3, Pallas kernels, attend_forward(): *outs, log_total = call(me, lengths, *qkv, scale_lanes, *kept)  62.6 us
    pallas_call x1, Pallas kernels, feed_grads(): pl.pallas_call(functools.partial(feed_grads_kernel, groups), grid=(hidden...  43.6 us
    ppermute x6, waiting for transfers between devices, fetch(): lax.ppermute(value, 'head', [((d + slot) % slots, d) for d in range(slots)])  32.9 us
    unnamed x87, local copies, waits for them, and re-layouts  24.4 us
    pallas_call x1, Pallas kernels, head_grads(): pl.pallas_call(functools.partial(head_grads_kernel, len(rows)), grid=(tok...  23.4 us
  transfers between devices with their start and end apart: 15, of which 3 were waited for; matrix products, arithmetic and copies ran while one was open for 5% of the time, Pallas kernels for 77%

profile of v4, /device:TPU:0, one launch (start us, length us, event | category | flops | bytes accessed | tf_op | source)
XLA Modules:
  0.0 630.1 jit_solution(978987753532160641)
XLA Ops:
  16.6 3.7 fusion.7
  26.7 5.4 project.5.refs_0_
  36.4 4.0 project.4.refs_0_
  42.0 29.7 %collective-permute-done.1.rows_ref.refs_1_ = bf16[1024,1024]{1,0:T(8,128)(2,1)S(1)} collective-permute-done((bf16[1024,1024]{1,0:T(8,128)(2,1)}, bf16[1024,1024]{1,0:T(8,128)(2,1)S(1)}, u32[]{:S(2)}, u32[]{:S(2)}) %collective-permute-start.1) | collective-permute-done | bytes 2097184 | tf_op jit(solution)/shard_map/ppermute | solution.py:878
  77.6 4.0 project.7.refs_1_
  83.2 35.9 %attend_forward.5 = (bf16[1024,512]{1,0:T(8,128)(2,1)}, bf16[1024,512]{1,0:T(8,128)(2,1)}, f32[4,1,2,2048]{3,2,1,0:T(2,128)}) custom-call(s32[1]{0:T(128)} %bitcast.12.me_ref, s32[1]{0:T(128)S(6)} %copy.55.len_ref, bf16[1024,1536]{1,0:T(8,128)(2,1)} %copy-done.5, bf16[1024,1536]{1,0:T(8,128)(2,1)} %copy-done.6, f32[1,512]{1,0:T(1,128)} %reshape_reshape.3.refs_2_.refs_6_), custom_call_target="tpu_custom_call" | custom-call | tf_op jit(solution)/shard_map/attend_forward/pallas_call | solution.py:243
  121.9 5.2 project.6.refs_1_
  128.8 12.9 %attend_forward.3 = (bf16[1024,512]{1,0:T(8,128)(2,1)}, bf16[1024,512]{1,0:T(8,128)(2,1)}, f32[4,2,2,512]{3,2,1,0:T(2,128)}) custom-call(s32[1]{0:T(128)} %bitcast.12.me_ref, s32[2]{0:T(128)} %len_ref.7, bf16[1024,1536]{1,0:T(8,128)(2,1)} %copy-done.1, bf16[1024,1536]{1,0:T(8,128)(2,1)} %copy-done.2, f32[1,512]{1,0:T(1,128)} %reshape_reshape.3.refs_2_.refs_6_), custom_call_target="tpu_custom_call" | custom-call | tf_op jit(solution)/shard_map/attend_forward/pallas_call | solution.py:243
  141.8 13.8 %attend_forward.4 = (bf16[1024,512]{1,0:T(8,128)(2,1)}, bf16[1024,512]{1,0:T(8,128)(2,1)}, f32[4,1,2,1024]{3,2,1,0:T(2,128)}) custom-call(s32[1]{0:T(128)} %bitcast.12.me_ref, s32[1]{0:T(128)S(6)} %copy.54.len_ref, bf16[1024,1536]{1,0:T(8,128)(2,1)} %copy-done.1, bf16[1024,1536]{1,0:T(8,128)(2,1)} %copy-done.2, ...), custom_call_target="tpu_custom_call", output_to_operand_aliasing={{0}: (5, {}), {1}: (6, {})} | custom-call | tf_op jit(solution)/shard_map/attend_forward/pallas_call | solution.py:243
  161.6 69.9 %middle_pass.3 = (bf16[1024,1024]{1,0:T(8,128)(2,1)}, f32[1024,1024]{1,0:T(8,128)}, bf16[1024,1024]{1,0:T(8,128)(2,1)}, bf16[1024,1024]{1,0:T(8,128)(2,1)}, bf16...) custom-call(bf16[1024,1024]{1,0:T(8,128)(2,1)} %bitcast.65, ...), custom_call_target="tpu_custom_call" | custom-call | tf_op jit(solution)/shard_map/middle_pass/pallas_call | solution.py:443
  232.8 70.5 %middle_pass.2 = (bf16[1024,1024]{1,0:T(8,128)(2,1)}, f32[1024,1024]{1,0:T(8,128)}, bf16[1024,1024]{1,0:T(8,128)(2,1)}, bf16[1024,1024]{1,0:T(8,128)(2,1)}, bf16...) custom-call(bf16[1024,1024]{1,0:T(8,128)(2,1)} %get-tuple-element.95, ...), custom_call_target="tpu_custom_call" | custom-call | tf_op jit(solution)/shard_map/middle_pass/pallas_call | solution.py:443
  304.2 43.6 %feed_grads.1 = bf16[4096,2048]{1,0:T(8,128)(2,1)} custom-call(bf16[1024,4096]{1,0:T(8,128)(2,1)} %get-tuple-element.117.refs_0_, bf16[1024,4096]{1,0:T(8,128)(2,1)} %get-tuple-element.118.refs_1_, bf16[1024,4096]{1,0:T(8,128)(2,1)} %get-tuple-element.119.refs_2_, bf16[1024,4096]{1,0:T(8,128)(2,1)} %get-tuple-element.120.refs_3_, ...), custom_call_target="tpu_custom_call" | custom-call | tf_op jit(solution)/shard_map/feed_grads/pallas_call | solution.py:469
  353.5 7.6 %out_grads.1 = (bf16[512,1024]{1,0:T(8,128)(2,1)S(1)}, bf16[512,1024]{1,0:T(8,128)(2,1)}) custom-call(bf16[1024,1024]{1,0:T(8,128)(2,1)S(1)} %copy-done.19, bf16[1024,1024]{1,0:T(8,128)(2,1)S(1)} %copy-done.20, bf16[1024,512]{1,0:T(8,128)(2,1)S(1)} %copy-done.15, bf16[1024,512]{1,0:T(8,128)(2,1)} %collective-permute-done.6.refs_3_, ...), custom_call_target="tpu_custom_call" | custom-call | tf_op jit(solution)/shard_map/out_grads/pallas_call | solution.py:755
  362.8 57.5 %attend_backward.3 = (bf16[1024,1536]{1,0:T(8,128)(2,1)}, bf16[1024,1536]{1,0:T(8,128)(2,1)}, f32[1,4,8,128]{3,2,1,0:T(8,128)}) custom-call(s32[1]{0:T(128)} %bitcast.12.me_ref, s32[1]{0:T(128)S(6)} %copy.55.len_ref, bf16[1024,1536]{1,0:T(8,128)(2,1)} %copy-done.5, bf16[1024,1536]{1,0:T(8,128)(2,1)} %copy-done.6, ...), custom_call_target="tpu_custom_call" | custom-call | tf_op jit(solution)/shard_map/attend_backward/pallas_call | solution.py:278
  422.4 4.9 unproject.3
  428.9 16.3 %attend_backward.4 = (bf16[1024,1536]{1,0:T(8,128)(2,1)}, bf16[1024,1536]{1,0:T(8,128)(2,1)}, f32[2,4,8,128]{3,2,1,0:T(8,128)}) custom-call(s32[1]{0:T(128)} %bitcast.12.me_ref, s32[2]{0:T(128)} %len_ref.7, bf16[1024,1536]{1,0:T(8,128)(2,1)} %copy-done.1, bf16[1024,1536]{1,0:T(8,128)(2,1)} %copy-done.2, ...), custom_call_target="tpu_custom_call" | custom-call | tf_op jit(solution)/shard_map/attend_backward/pallas_call | solution.py:278
  445.2 19.2 %attend_backward.5 = (bf16[1024,1536]{1,0:T(8,128)(2,1)}, bf16[1024,1536]{1,0:T(8,128)(2,1)}, f32[1,4,8,128]{3,2,1,0:T(8,128)}) custom-call(s32[1]{0:T(128)} %bitcast.12.me_ref, s32[1]{0:T(128)S(6)} %copy.54.len_ref, bf16[1024,1536]{1,0:T(8,128)(2,1)} %copy-done.1, bf16[1024,1536]{1,0:T(8,128)(2,1)} %copy-done.2, ...), custom_call_target="tpu_custom_call", output_to_operand_aliasing={{0}: (10, {}), {1}: (11, {})} | custom-call | tf_op jit(solution)/shard_map/attend_backward/pallas_call | solution.py:278
  464.4 23.4 %head_grads.1 = bf16[4,1024,512]{2,1,0:T(8,128)(2,1)} custom-call(bf16[1024,1024]{1,0:T(8,128)(2,1)} %get-tuple-element.94.rows_ref.refs_0_, bf16[1024,1024]{1,0:T(8,128)(2,1)} %copy-done.16, bf16[1024,1024]{1,0:T(8,128)(2,1)} %get-tuple-element.98.rows_ref.refs_2_, bf16[1024,1024]{1,0:T(8,128)(2,1)} %collective-permute-done.2.rows_ref.refs_3_, ...), custom_call_target="tpu_custom_call" | custom-call | tf_op jit(solution)/shard_map/head_grads/pallas_call | solution.py:512
  487.8 4.9 unproject.2
  500.2 8.5 %first_back.2 = (bf16[1024,1024]{1,0:T(8,128)(2,1)}, f32[8,1024]{1,0:T(8,128)S(1)}) custom-call(bf16[1024,1024]{1,0:T(8,128)(2,1)S(1)} %bitcast.66, bf16[1024,1536]{1,0:T(8,128)(2,1)S(1)} %copy-done.13, bf16[3,1024,512]{2,1,0:T(8,128)(2,1)S(1)} %copy-done, f32[3,1024]{1,0:T(4,128)S(1)} %copy-done.23, f32[5,1024]{1,0:T(8,128)S(1)} %copy-done.22, ...), custom_call_target="tpu_custom_call" | custom-call | tf_op jit(solution)/shard_map/first_back/pallas_call | solution.py:800
  508.7 70.5 %batch_sum.1 = (bf16[4096,512]{1,0:T(8,128)(2,1)S(1)}, f32[168,128]{1,0:T(8,128)S(1)}) custom-call(bf16[4096,512]{1,0:T(8,128)(2,1)S(1)} %bitcast.67, f32[168,128]{1,0:T(8,128)S(1)} %maximum_bitcast_fusion.extra), custom_call_target="tpu_custom_call" | custom-call | tf_op jit(solution)/shard_map/batch_sum/pallas_call | solution.py:641
  590.5 3.8 convert.1
  594.7 7.3 %first_back.3 = (bf16[1024,1024]{1,0:T(8,128)(2,1)S(1)}, f32[8,1024]{1,0:T(8,128)S(1)}) custom-call(bf16[1024,1024]{1,0:T(8,128)(2,1)S(1)} %copy-done.10, bf16[1024,1536]{1,0:T(8,128)(2,1)S(1)} %copy-done.7, bf16[3,1024,512]{2,1,0:T(8,128)(2,1)S(1)} %copy-done, f32[3,1024]{1,0:T(4,128)S(1)} %copy-done.23, f32[5,1024]{1,0:T(8,128)S(1)} %copy-done.22, ...), custom_call_target="tpu_custom_call" | custom-call | tf_op jit(solution)/shard_map/first_back/pallas_call | solution.py:800
  606.3 15.5 %small_sum.1 = f32[16,128]{1,0:T(8,128)S(1)} custom-call(f32[16,128]{1,0:T(8,128)S(1)} %reshape.195.source), custom_call_target="tpu_custom_call" | custom-call | tf_op jit(solution)/shard_map/small_sum/pallas_call | solution.py:690
  (186 shorter events, 76.0 us)
Async XLA Ops:
  7.2 8.3 %copy-start.3 = (bf16[1,1024,1024]{2,1,0:T(8,128)(2,1)S(1)}, bf16[1,1024,1024]{2,1,0:T(8,128)(2,1)}, u32[]{:S(2)}) copy-start(bf16[1,1024,1024]{2,1,0:T(8,128)(2,1)} %param.23) | copy-start | bytes 6291460
  7.2 154.4 %all-gather.2.cloned.1.call-start = ((), (), s32[]{:S(2)}) async-start(), calls=%async_computation.1 | async-start | bytes 17825792 | tf_op jit(solution)/shard_map/all_gather | solution.py:934
  8.5 15.0 %collective-permute-start = (bf16[2,128,1024]{2,1,0:T(8,128)(2,1)S(1)}, bf16[2,128,1024]{2,1,0:T(8,128)(2,1)S(1)}, u32[]{:S(2)}, u32[]{:S(2)}) collective-permute-start(bf16[2,128,1024]{2,1,0:T(8,128)(2,1)S(1)} %get-tuple-element.180), channel_id=1, source_target_pairs={{16,0},{0,16},{17,1},{1,17},{18,2},{2,18},{19,3},{3,19},{20,4},{4,... | collective-permute-start | bytes 1572872 | tf_op jit(solution)/shard_map/ppermute | solution.py:878
  24.6 559.3 %reduce-scatter.2.cloned.1.call-start = ((), (), s32[]{:S(2)}) async-start(), calls=%async_computation.2 | async-start | bytes 17825792 | tf_op jit(solution)/shard_map/reduce_scatter | solution.py:988
  24.7 47.1 %collective-permute-start.1 = (bf16[1024,1024]{1,0:T(8,128)(2,1)}, bf16[1024,1024]{1,0:T(8,128)(2,1)S(1)}, u32[]{:S(2)}, u32[]{:S(2)}) collective-permute-start(bf16[1024,1024]{1,0:T(8,128)(2,1)} %get-tuple-element.94.rows_ref.refs_0_), channel_id=1, source_target_pairs={{16,0},{0,16},{17,1},{1,17},{18,2},{2,18},{19,3},{3,19},{20,4},{4,... | collective-permute-start | bytes 6291464 | tf_op jit(solution)/shard_map/ppermute | solution.py:878
  26.6 7.1 %copy-start.27 = (bf16[2,256,1024]{2,1,0:T(8,128)(2,1)S(1)}, bf16[2,256,1024]{2,1,0:T(8,128)(2,1)}, u32[]{:S(2)}) copy-start(bf16[2,256,1024]{2,1,0:T(8,128)(2,1)} %param.21) | copy-start | bytes 3145732
  26.6 7.1 %copy-start.30 = (bf16[1,512,1024]{2,1,0:T(8,128)(2,1)S(1)}, bf16[1,512,1024]{2,1,0:T(8,128)(2,1)}, u32[]{:S(2)}) copy-start(bf16[1,512,1024]{2,1,0:T(8,128)(2,1)} %param.28) | copy-start | bytes 3145732
  36.3 38.2 %copy-start.42 = (f32[8]{0:T(128)S(1)}, f32[8]{0:T(128)}, u32[]{:S(2)}) copy-start(f32[8]{0:T(128)} %param.34) | copy-start | bytes 100
  73.1 48.8 %collective-permute-start.2 = (bf16[1024,1024]{1,0:T(8,128)(2,1)}, bf16[1024,1024]{1,0:T(8,128)(2,1)}, u32[]{:S(2)}, u32[]{:S(2)}) collective-permute-start(bf16[1024,1024]{1,0:T(8,128)(2,1)} %get-tuple-element.98.rows_ref.refs_2_), channel_id=1, source_target_pairs={{16,0},{0,16},{17,1},{1,17},{18,2},{2,18},{19,3},{3,19},{20,4},{4,... | collective-permute-start | bytes 6291464 | tf_op jit(solution)/shard_map/ppermute | solution.py:878
  83.2 35.9 %copy-start.28 = (bf16[512,1024]{1,0:T(8,128)(2,1)S(1)}, bf16[512,1024]{1,0:T(8,128)(2,1)}, u32[]{:S(2)}) copy-start(bf16[512,1024]{1,0:T(8,128)(2,1)} %refs_4_.3) | copy-start | bytes 3145732
  119.1 37.3 %collective-permute-start.4 = (bf16[256,1024]{1,0:T(8,128)(2,1)S(1)}, bf16[256,1024]{1,0:T(8,128)(2,1)}, u32[]{:S(2)}, u32[]{:S(2)}) collective-permute-start(bf16[256,1024]{1,0:T(8,128)(2,1)S(1)} %constant_dynamic-slice_fusion), channel_id=1, source_target_pairs={{0,16},{16,0},{1,17},{17,1},{2,18},{18,2},{3,19},{19,3},{4,20},{20... | collective-permute-start | bytes 1572872 | tf_op jit(solution)/shard_map/ppermute | solution.py:881
  120.6 41.0 %collective-permute-start.6 = (bf16[1024,512]{1,0:T(8,128)(2,1)}, bf16[1024,512]{1,0:T(8,128)(2,1)}, u32[]{:S(2)}, u32[]{:S(2)}) collective-permute-start(bf16[1024,512]{1,0:T(8,128)(2,1)} %get-tuple-element.111.refs_3_), channel_id=1, source_target_pairs={{0,16},{16,0},{1,17},{17,1},{2,18},{18,2},{3,19},{19,3},{4,20},{20... | collective-permute-start | bytes 3145736 | tf_op jit(solution)/shard_map/ppermute | solution.py:881
  141.8 14.6 %copy-start.37 = (f32[2,4096]{1,0:T(2,128)S(1)}, f32[2,4096]{1,0:T(2,128)}, u32[]{:S(2)}) copy-start(f32[2,4096]{1,0:T(2,128)} %param.38) | copy-start | bytes 98308
  141.8 14.7 %copy-start.38 = (f32[4096]{0:T(1024)S(1)}, f32[4096]{0:T(1024)}, u32[]{:S(2)}) copy-start(f32[4096]{0:T(1024)} %param.37) | copy-start | bytes 49156
  155.5 77.2 %collective-permute-start.3 = (bf16[1024,512]{1,0:T(8,128)(2,1)}, bf16[1024,512]{1,0:T(8,128)(2,1)}, u32[]{:S(2)}, u32[]{:S(2)}) collective-permute-start(bf16[1024,512]{1,0:T(8,128)(2,1)} %get-tuple-element.102.refs_3_), channel_id=1, source_target_pairs={{0,16},{16,0},{1,17},{17,1},{2,18},{18,2},{3,19},{19,3},{4,20},{20... | collective-permute-start | bytes 3145736 | tf_op jit(solution)/shard_map/ppermute | solution.py:881
  156.4 2.3 collective-permute-start.5
  231.5 116.3 %collective-permute-start.7 = (bf16[1024,512]{1,0:T(8,128)(2,1)}, bf16[1024,512]{1,0:T(8,128)(2,1)}, u32[]{:S(2)}, u32[]{:S(2)}) collective-permute-start(bf16[1024,512]{1,0:T(8,128)(2,1)} %get-tuple-element.114), channel_id=1, source_target_pairs={{16,0},{0,16},{17,1},{1,17},{18,2},{2,18},{19,3},{3,19},{20,4},{4,... | collective-permute-start | bytes 3145736 | tf_op jit(solution)/shard_map/ppermute | solution.py:878
  303.3 44.6 %collective-permute-start.8 = (bf16[1024,512]{1,0:T(8,128)(2,1)}, bf16[1024,512]{1,0:T(8,128)(2,1)}, u32[]{:S(2)}, u32[]{:S(2)}) collective-permute-start(bf16[1024,512]{1,0:T(8,128)(2,1)} %get-tuple-element.116), channel_id=1, source_target_pairs={{16,0},{0,16},{17,1},{1,17},{18,2},{2,18},{19,3},{3,19},{20,4},{4,... | collective-permute-start | bytes 3145736 | tf_op jit(solution)/shard_map/ppermute | solution.py:878
  362.1 102.2 %collective-permute-start.9 = (bf16[512,1024]{1,0:T(8,128)(2,1)}, bf16[512,1024]{1,0:T(8,128)(2,1)}, u32[]{:S(2)}, u32[]{:S(2)}) collective-permute-start(bf16[512,1024]{1,0:T(8,128)(2,1)} %get-tuple-element.143), channel_id=1, source_target_pairs={{16,0},{0,16},{17,1},{1,17},{18,2},{2,18},{19,3},{3,19},{20,4},{4,... | collective-permute-start | bytes 3145736 | tf_op jit(solution)/shard_map/ppermute | solution.py:878
  427.3 69.3 %collective-permute-start.11 = (bf16[1024,1024]{1,0:T(8,128)(2,1)}, bf16[1024,1024]{1,0:T(8,128)(2,1)}, u32[]{:S(2)}, u32[]{:S(2)}) collective-permute-start(bf16[1024,1024]{1,0:T(8,128)(2,1)} %unproject.3), channel_id=1, source_target_pairs={{0,16},{16,0},{1,17},{17,1},{2,18},{18,2},{3,19},{19,3},{4,20},{20... | collective-permute-start | bytes 6291464 | tf_op jit(solution)/shard_map/ppermute | solution.py:881
  464.4 23.4 %copy-start.8 = (bf16[1024,1536]{1,0:T(8,128)(2,1)S(1)}, bf16[1024,1536]{1,0:T(8,128)(2,1)}, u32[]{:S(2)}) copy-start(bf16[1024,1536]{1,0:T(8,128)(2,1)} %get-tuple-element.146.refs_7_.grads) | copy-start | bytes 9437188
  492.7 91.3 %collective-permute-start.10 = (bf16[1024,1024]{1,0:T(8,128)(2,1)}, bf16[1024,1024]{1,0:T(8,128)(2,1)}, u32[]{:S(2)}, u32[]{:S(2)}) collective-permute-start(bf16[1024,1024]{1,0:T(8,128)(2,1)} %unproject.2), channel_id=1, source_target_pairs={{0,16},{16,0},{1,17},{17,1},{2,18},{18,2},{3,19},{19,3},{4,20},{20... | collective-permute-start | bytes 6291464 | tf_op jit(solution)/shard_map/ppermute | solution.py:881
  500.2 8.5 %copy-start.12 = (bf16[4,1024,512]{2,1,0:T(8,128)(2,1)S(1)}, bf16[4,1024,512]{2,1,0:T(8,128)(2,1)}, u32[]{:S(2)}) copy-start(bf16[4,1024,512]{2,1,0:T(8,128)(2,1)} %head_grads.1) | copy-start | bytes 12582916
  585.1 20.0 %collective-permute-start.12 = (bf16[128,2048]{1,0:T(8,128)(2,1)S(1)}, bf16[128,2048]{1,0:T(8,128)(2,1)S(1)}, u32[]{:S(2)}, u32[]{:S(2)}) collective-permute-start(bf16[128,2048]{1,0:T(8,128)(2,1)S(1)} %slice.151), channel_id=1, source_target_pairs={{0,16},{16,0},{1,17},{17,1},{2,18},{18,2},{3,19},{19,3},{4,20},{20... | collective-permute-start | bytes 1572872 | tf_op jit(solution)/shard_map/ppermute | solution.py:881
  (36 other events, 123.0 us)
Sparse Core Ops, SparseCore 0:
  24.7 128.3 all-gather.1
  348.0 182.7 reduce-scatter.1

commit v5 on v4

--- a/solution.py
+++ b/solution.py
@@ -390,7 +390,7 @@
         return inner * inverse
 
     residual_grad = cot_wide + back(dense_grad, dense_unit, dense_inverse, 2)
-    residual_grad_ref[...] = residual_grad
+    residual_grad_ref[...] = residual_grad.astype(BF)
     attended_grad = back(residual_grad, post_unit, post_inverse, 1)
     sums_ref[5:6, :] += column_sum(attended_grad)
     sums_ref[6:7, :] += column_sum(cot_wide)
@@ -427,7 +427,7 @@
         + [tiles(part)] * slots,
         out_shape=[
             jax.ShapeDtypeStruct((tokens, width), BF),
-            jax.ShapeDtypeStruct((tokens, width), F32),
+            jax.ShapeDtypeStruct((tokens, width), BF),
             jax.ShapeDtypeStruct((tokens, width), BF),
             jax.ShapeDtypeStruct((tokens, width), BF),
             jax.ShapeDtypeStruct((tokens, hidden), BF),
@@ -783,7 +783,7 @@
     )
     sums_ref[0:1, :] += column_sum(grad * unit)
     sums_ref[1:2, :] += column_sum(grad)
-    result[...] = (residual_ref[...] + inner * inverse).astype(BF)
+    result[...] = (residual_ref[...].astype(F32) + inner * inverse).astype(BF)
 
 
 def first_back(rows, qkv_grad, weights, gains, shifts, residual_grad, arrived):

time: 635 us -> 637 us (level)
    unnamed x87 -> x91, local copies, waits for them, and re-layouts: 24.4 us -> 27 us
where the time goes in v5:
time: 637 us; the launch traced here: 633 us
  Pallas kernels  502 us (79%)
  local copies, waits for them, and re-layouts  41.8 us (7%)
  waiting for transfers between devices  33.8 us (5%)
  other arithmetic  24.1 us (4%)
  between operations  16.3 us (3%)
  starting transfers between devices  15 us (2%)
    pallas_call x2, Pallas kernels, middle_pass(): call(rows, cotangent, *scaled, *out_weights, feed, gains, shifts, mid_gai...  140 us
    pallas_call x3, Pallas kernels, attend_backward(): call(me, lengths, *qkv, *outs, *grads, scale_lanes, log_total, *kept)  93 us
    pallas_call x1, Pallas kernels, batch_sum(): pl.pallas_call(functools.partial(batch_sum_kernel, bits, chunks, steps),...  71.1 us
    pallas_call x3, Pallas kernels, attend_forward(): *outs, log_total = call(me, lengths, *qkv, scale_lanes, *kept)  62.7 us
    pallas_call x1, Pallas kernels, feed_grads(): pl.pallas_call(functools.partial(feed_grads_kernel, groups), grid=(hidden...  43.6 us
    ppermute x6, waiting for transfers between devices, fetch(): lax.ppermute(value, 'head', [((d + slot) % slots, d) for d in range(slots)])  32.9 us
    unnamed x91, local copies, waits for them, and re-layouts  27 us
    pallas_call x1, Pallas kernels, head_grads(): pl.pallas_call(functools.partial(head_grads_kernel, len(rows)), grid=(tok...  23.8 us
  transfers between devices with their start and end apart: 15, of which 3 were waited for; matrix products, arithmetic and copies ran while one was open for 5% of the time, Pallas kernels for 77%

profile of v5, /device:TPU:0, one launch (start us, length us, event | category | flops | bytes accessed | tf_op | source)
XLA Modules:
  0.0 633.1 jit_solution(2377462667940654331)
XLA Ops:
  16.6 3.7 fusion.7
  26.7 5.4 project.5.refs_0_
  36.4 4.0 project.4.refs_0_
  42.0 29.8 %collective-permute-done.1.rows_ref.refs_1_ = bf16[1024,1024]{1,0:T(8,128)(2,1)S(1)} collective-permute-done((bf16[1024,1024]{1,0:T(8,128)(2,1)}, bf16[1024,1024]{1,0:T(8,128)(2,1)S(1)}, u32[]{:S(2)}, u32[]{:S(2)}) %collective-permute-start.1) | collective-permute-done | bytes 2097184 | tf_op jit(solution)/shard_map/ppermute | solution.py:878
  77.5 4.0 project.7.refs_1_
  83.1 36.0 %attend_forward.5 = (bf16[1024,512]{1,0:T(8,128)(2,1)}, bf16[1024,512]{1,0:T(8,128)(2,1)}, f32[4,1,2,2048]{3,2,1,0:T(2,128)}) custom-call(s32[1]{0:T(128)} %bitcast.12.me_ref, s32[1]{0:T(128)S(6)} %copy.55.len_ref, bf16[1024,1536]{1,0:T(8,128)(2,1)} %copy-done.5, bf16[1024,1536]{1,0:T(8,128)(2,1)} %copy-done.6, f32[1,512]{1,0:T(1,128)} %reshape_reshape.3.refs_2_.refs_6_), custom_call_target="tpu_custom_call" | custom-call | tf_op jit(solution)/shard_map/attend_forward/pallas_call | solution.py:243
  122.0 5.2 project.6.refs_1_
  128.9 12.9 %attend_forward.3 = (bf16[1024,512]{1,0:T(8,128)(2,1)}, bf16[1024,512]{1,0:T(8,128)(2,1)}, f32[4,2,2,512]{3,2,1,0:T(2,128)}) custom-call(s32[1]{0:T(128)} %bitcast.12.me_ref, s32[2]{0:T(128)} %len_ref.7, bf16[1024,1536]{1,0:T(8,128)(2,1)} %copy-done.1, bf16[1024,1536]{1,0:T(8,128)(2,1)} %copy-done.2, f32[1,512]{1,0:T(1,128)} %reshape_reshape.3.refs_2_.refs_6_), custom_call_target="tpu_custom_call" | custom-call | tf_op jit(solution)/shard_map/attend_forward/pallas_call | solution.py:243
  141.9 13.8 %attend_forward.4 = (bf16[1024,512]{1,0:T(8,128)(2,1)}, bf16[1024,512]{1,0:T(8,128)(2,1)}, f32[4,1,2,1024]{3,2,1,0:T(2,128)}) custom-call(s32[1]{0:T(128)} %bitcast.12.me_ref, s32[1]{0:T(128)S(6)} %copy.54.len_ref, bf16[1024,1536]{1,0:T(8,128)(2,1)} %copy-done.1, bf16[1024,1536]{1,0:T(8,128)(2,1)} %copy-done.2, ...), custom_call_target="tpu_custom_call", output_to_operand_aliasing={{0}: (5, {}), {1}: (6, {})} | custom-call | tf_op jit(solution)/shard_map/attend_forward/pallas_call | solution.py:243
  161.6 70.0 %middle_pass.3 = (bf16[1024,1024]{1,0:T(8,128)(2,1)}, bf16[1024,1024]{1,0:T(8,128)(2,1)}, bf16[1024,1024]{1,0:T(8,128)(2,1)}, bf16[1024,1024]{1,0:T(8,128)(2,1)}...) custom-call(bf16[1024,1024]{1,0:T(8,128)(2,1)} %bitcast.65, ...), custom_call_target="tpu_custom_call" | custom-call | tf_op jit(solution)/shard_map/middle_pass/pallas_call | solution.py:443
  232.9 70.5 %middle_pass.2 = (bf16[1024,1024]{1,0:T(8,128)(2,1)}, bf16[1024,1024]{1,0:T(8,128)(2,1)}, bf16[1024,1024]{1,0:T(8,128)(2,1)}, bf16[1024,1024]{1,0:T(8,128)(2,1)}...) custom-call(bf16[1024,1024]{1,0:T(8,128)(2,1)} %get-tuple-element.95, ...), custom_call_target="tpu_custom_call" | custom-call | tf_op jit(solution)/shard_map/middle_pass/pallas_call | solution.py:443
  304.3 43.6 %feed_grads.1 = bf16[4096,2048]{1,0:T(8,128)(2,1)} custom-call(bf16[1024,4096]{1,0:T(8,128)(2,1)} %get-tuple-element.117.refs_0_, bf16[1024,4096]{1,0:T(8,128)(2,1)} %get-tuple-element.118.refs_1_, bf16[1024,4096]{1,0:T(8,128)(2,1)} %get-tuple-element.119.refs_2_, bf16[1024,4096]{1,0:T(8,128)(2,1)} %get-tuple-element.120.refs_3_, ...), custom_call_target="tpu_custom_call" | custom-call | tf_op jit(solution)/shard_map/feed_grads/pallas_call | solution.py:469
  353.5 7.6 %out_grads.1 = (bf16[512,1024]{1,0:T(8,128)(2,1)S(1)}, bf16[512,1024]{1,0:T(8,128)(2,1)}) custom-call(bf16[1024,1024]{1,0:T(8,128)(2,1)S(1)} %copy-done.21, bf16[1024,1024]{1,0:T(8,128)(2,1)S(1)} %copy-done.22, bf16[1024,512]{1,0:T(8,128)(2,1)S(1)} %copy-done.15, bf16[1024,512]{1,0:T(8,128)(2,1)} %collective-permute-done.6.refs_3_, ...), custom_call_target="tpu_custom_call" | custom-call | tf_op jit(solution)/shard_map/out_grads/pallas_call | solution.py:755
  362.9 57.5 %attend_backward.3 = (bf16[1024,1536]{1,0:T(8,128)(2,1)}, bf16[1024,1536]{1,0:T(8,128)(2,1)}, f32[1,4,8,128]{3,2,1,0:T(8,128)}) custom-call(s32[1]{0:T(128)} %bitcast.12.me_ref, s32[1]{0:T(128)S(6)} %copy.55.len_ref, bf16[1024,1536]{1,0:T(8,128)(2,1)} %copy-done.5, bf16[1024,1536]{1,0:T(8,128)(2,1)} %copy-done.6, ...), custom_call_target="tpu_custom_call" | custom-call | tf_op jit(solution)/shard_map/attend_backward/pallas_call | solution.py:278
  422.5 4.9 unproject.3
  429.0 16.2 %attend_backward.4 = (bf16[1024,1536]{1,0:T(8,128)(2,1)}, bf16[1024,1536]{1,0:T(8,128)(2,1)}, f32[2,4,8,128]{3,2,1,0:T(8,128)}) custom-call(s32[1]{0:T(128)} %bitcast.12.me_ref, s32[2]{0:T(128)} %len_ref.7, bf16[1024,1536]{1,0:T(8,128)(2,1)} %copy-done.1, bf16[1024,1536]{1,0:T(8,128)(2,1)} %copy-done.2, ...), custom_call_target="tpu_custom_call" | custom-call | tf_op jit(solution)/shard_map/attend_backward/pallas_call | solution.py:278
  445.2 19.2 %attend_backward.5 = (bf16[1024,1536]{1,0:T(8,128)(2,1)}, bf16[1024,1536]{1,0:T(8,128)(2,1)}, f32[1,4,8,128]{3,2,1,0:T(8,128)}) custom-call(s32[1]{0:T(128)} %bitcast.12.me_ref, s32[1]{0:T(128)S(6)} %copy.54.len_ref, bf16[1024,1536]{1,0:T(8,128)(2,1)} %copy-done.1, bf16[1024,1536]{1,0:T(8,128)(2,1)} %copy-done.2, ...), custom_call_target="tpu_custom_call", output_to_operand_aliasing={{0}: (10, {}), {1}: (11, {})} | custom-call | tf_op jit(solution)/shard_map/attend_backward/pallas_call | solution.py:278
  464.5 23.8 %head_grads.1 = bf16[4,1024,512]{2,1,0:T(8,128)(2,1)} custom-call(bf16[1024,1024]{1,0:T(8,128)(2,1)} %get-tuple-element.94.rows_ref.refs_0_, bf16[1024,1024]{1,0:T(8,128)(2,1)} %copy-done.16, bf16[1024,1024]{1,0:T(8,128)(2,1)} %get-tuple-element.98.rows_ref.refs_2_, bf16[1024,1024]{1,0:T(8,128)(2,1)} %collective-permute-done.2.rows_ref.refs_3_, ...), custom_call_target="tpu_custom_call" | custom-call | tf_op jit(solution)/shard_map/head_grads/pallas_call | solution.py:512
  488.3 4.9 unproject.2
  502.3 8.2 %first_back.2 = (bf16[1024,1024]{1,0:T(8,128)(2,1)}, f32[8,1024]{1,0:T(8,128)S(1)}) custom-call(bf16[1024,1024]{1,0:T(8,128)(2,1)S(1)} %bitcast.66, bf16[1024,1536]{1,0:T(8,128)(2,1)S(1)} %copy-done.13, bf16[3,1024,512]{2,1,0:T(8,128)(2,1)S(1)} %copy-done, f32[3,1024]{1,0:T(4,128)S(1)} %copy-done.25, f32[5,1024]{1,0:T(8,128)S(1)} %copy-done.24, ...), custom_call_target="tpu_custom_call" | custom-call | tf_op jit(solution)/shard_map/first_back/pallas_call | solution.py:800
  510.6 71.1 %batch_sum.1 = (bf16[4096,512]{1,0:T(8,128)(2,1)S(1)}, f32[168,128]{1,0:T(8,128)S(1)}) custom-call(bf16[4096,512]{1,0:T(8,128)(2,1)S(1)} %bitcast.67, f32[168,128]{1,0:T(8,128)S(1)} %maximum_bitcast_fusion.extra), custom_call_target="tpu_custom_call" | custom-call | tf_op jit(solution)/shard_map/batch_sum/pallas_call | solution.py:641
  591.7 4.1 convert.1
  597.1 8.1 %first_back.3 = (bf16[1024,1024]{1,0:T(8,128)(2,1)S(1)}, f32[8,1024]{1,0:T(8,128)S(1)}) custom-call(bf16[1024,1024]{1,0:T(8,128)(2,1)S(1)} %copy-done.10, bf16[1024,1536]{1,0:T(8,128)(2,1)S(1)} %copy-done.7, bf16[3,1024,512]{2,1,0:T(8,128)(2,1)} %weights.15, f32[3,1024]{1,0:T(4,128)S(1)} %copy-done.25, f32[5,1024]{1,0:T(8,128)S(1)} %copy-done.24, ...), custom_call_target="tpu_custom_call" | custom-call | tf_op jit(solution)/shard_map/first_back/pallas_call | solution.py:800
  609.5 15.3 %small_sum.1 = f32[16,128]{1,0:T(8,128)S(1)} custom-call(f32[16,128]{1,0:T(8,128)S(1)} %reshape.195.source), custom_call_target="tpu_custom_call" | custom-call | tf_op jit(solution)/shard_map/small_sum/pallas_call | solution.py:690
  (190 shorter events, 77.1 us)
Async XLA Ops:
  7.2 8.3 %copy-start.3 = (bf16[1,1024,1024]{2,1,0:T(8,128)(2,1)S(1)}, bf16[1,1024,1024]{2,1,0:T(8,128)(2,1)}, u32[]{:S(2)}) copy-start(bf16[1,1024,1024]{2,1,0:T(8,128)(2,1)} %param.23) | copy-start | bytes 6291460
  7.2 154.4 %all-gather.2.cloned.1.call-start = ((), (), s32[]{:S(2)}) async-start(), calls=%async_computation.1 | async-start | bytes 17825792 | tf_op jit(solution)/shard_map/all_gather | solution.py:934
  8.5 15.0 %collective-permute-start = (bf16[2,128,1024]{2,1,0:T(8,128)(2,1)S(1)}, bf16[2,128,1024]{2,1,0:T(8,128)(2,1)S(1)}, u32[]{:S(2)}, u32[]{:S(2)}) collective-permute-start(bf16[2,128,1024]{2,1,0:T(8,128)(2,1)S(1)} %get-tuple-element.180), channel_id=1, source_target_pairs={{16,0},{0,16},{17,1},{1,17},{18,2},{2,18},{19,3},{3,19},{20,4},{4,... | collective-permute-start | bytes 1572872 | tf_op jit(solution)/shard_map/ppermute | solution.py:878
  24.6 561.8 %reduce-scatter.2.cloned.1.call-start = ((), (), s32[]{:S(2)}) async-start(), calls=%async_computation.2 | async-start | bytes 17825792 | tf_op jit(solution)/shard_map/reduce_scatter | solution.py:988
  24.7 47.1 %collective-permute-start.1 = (bf16[1024,1024]{1,0:T(8,128)(2,1)}, bf16[1024,1024]{1,0:T(8,128)(2,1)S(1)}, u32[]{:S(2)}, u32[]{:S(2)}) collective-permute-start(bf16[1024,1024]{1,0:T(8,128)(2,1)} %get-tuple-element.94.rows_ref.refs_0_), channel_id=1, source_target_pairs={{16,0},{0,16},{17,1},{1,17},{18,2},{2,18},{19,3},{3,19},{20,4},{4,... | collective-permute-start | bytes 6291464 | tf_op jit(solution)/shard_map/ppermute | solution.py:878
  26.6 7.1 %copy-start.29 = (bf16[2,256,1024]{2,1,0:T(8,128)(2,1)S(1)}, bf16[2,256,1024]{2,1,0:T(8,128)(2,1)}, u32[]{:S(2)}) copy-start(bf16[2,256,1024]{2,1,0:T(8,128)(2,1)} %param.21) | copy-start | bytes 3145732
  26.6 7.1 %copy-start.32 = (bf16[1,512,1024]{2,1,0:T(8,128)(2,1)S(1)}, bf16[1,512,1024]{2,1,0:T(8,128)(2,1)}, u32[]{:S(2)}) copy-start(bf16[1,512,1024]{2,1,0:T(8,128)(2,1)} %param.28) | copy-start | bytes 3145732
  36.4 38.1 %copy-start.44 = (f32[8]{0:T(128)S(1)}, f32[8]{0:T(128)}, u32[]{:S(2)}) copy-start(f32[8]{0:T(128)} %param.34) | copy-start | bytes 100
  73.1 48.9 %collective-permute-start.2 = (bf16[1024,1024]{1,0:T(8,128)(2,1)}, bf16[1024,1024]{1,0:T(8,128)(2,1)}, u32[]{:S(2)}, u32[]{:S(2)}) collective-permute-start(bf16[1024,1024]{1,0:T(8,128)(2,1)} %get-tuple-element.98.rows_ref.refs_2_), channel_id=1, source_target_pairs={{16,0},{0,16},{17,1},{1,17},{18,2},{2,18},{19,3},{3,19},{20,4},{4,... | collective-permute-start | bytes 6291464 | tf_op jit(solution)/shard_map/ppermute | solution.py:878
  83.1 36.0 %copy-start.30 = (bf16[512,1024]{1,0:T(8,128)(2,1)S(1)}, bf16[512,1024]{1,0:T(8,128)(2,1)}, u32[]{:S(2)}) copy-start(bf16[512,1024]{1,0:T(8,128)(2,1)} %refs_4_.3) | copy-start | bytes 3145732
  119.2 37.3 %collective-permute-start.4 = (bf16[256,1024]{1,0:T(8,128)(2,1)S(1)}, bf16[256,1024]{1,0:T(8,128)(2,1)}, u32[]{:S(2)}, u32[]{:S(2)}) collective-permute-start(bf16[256,1024]{1,0:T(8,128)(2,1)S(1)} %constant_dynamic-slice_fusion), channel_id=1, source_target_pairs={{0,16},{16,0},{1,17},{17,1},{2,18},{18,2},{3,19},{19,3},{4,20},{20... | collective-permute-start | bytes 1572872 | tf_op jit(solution)/shard_map/ppermute | solution.py:881
  120.6 41.0 %collective-permute-start.6 = (bf16[1024,512]{1,0:T(8,128)(2,1)}, bf16[1024,512]{1,0:T(8,128)(2,1)}, u32[]{:S(2)}, u32[]{:S(2)}) collective-permute-start(bf16[1024,512]{1,0:T(8,128)(2,1)} %get-tuple-element.111.refs_3_), channel_id=1, source_target_pairs={{0,16},{16,0},{1,17},{17,1},{2,18},{18,2},{3,19},{19,3},{4,20},{20... | collective-permute-start | bytes 3145736 | tf_op jit(solution)/shard_map/ppermute | solution.py:881
  141.8 14.6 %copy-start.39 = (f32[2,4096]{1,0:T(2,128)S(1)}, f32[2,4096]{1,0:T(2,128)}, u32[]{:S(2)}) copy-start(f32[2,4096]{1,0:T(2,128)} %param.38) | copy-start | bytes 98308
  141.9 14.6 %copy-start.40 = (f32[4096]{0:T(1024)S(1)}, f32[4096]{0:T(1024)}, u32[]{:S(2)}) copy-start(f32[4096]{0:T(1024)} %param.37) | copy-start | bytes 49156
  155.6 77.3 %collective-permute-start.3 = (bf16[1024,512]{1,0:T(8,128)(2,1)}, bf16[1024,512]{1,0:T(8,128)(2,1)}, u32[]{:S(2)}, u32[]{:S(2)}) collective-permute-start(bf16[1024,512]{1,0:T(8,128)(2,1)} %get-tuple-element.102.refs_3_), channel_id=1, source_target_pairs={{0,16},{16,0},{1,17},{17,1},{2,18},{18,2},{3,19},{19,3},{4,20},{20... | collective-permute-start | bytes 3145736 | tf_op jit(solution)/shard_map/ppermute | solution.py:881
  156.4 2.3 collective-permute-start.5
  231.6 116.3 %collective-permute-start.7 = (bf16[1024,512]{1,0:T(8,128)(2,1)}, bf16[1024,512]{1,0:T(8,128)(2,1)}, u32[]{:S(2)}, u32[]{:S(2)}) collective-permute-start(bf16[1024,512]{1,0:T(8,128)(2,1)} %get-tuple-element.114), channel_id=1, source_target_pairs={{16,0},{0,16},{17,1},{1,17},{18,2},{2,18},{19,3},{3,19},{20,4},{4,... | collective-permute-start | bytes 3145736 | tf_op jit(solution)/shard_map/ppermute | solution.py:878
  303.4 44.5 %collective-permute-start.8 = (bf16[1024,512]{1,0:T(8,128)(2,1)}, bf16[1024,512]{1,0:T(8,128)(2,1)}, u32[]{:S(2)}, u32[]{:S(2)}) collective-permute-start(bf16[1024,512]{1,0:T(8,128)(2,1)} %get-tuple-element.116), channel_id=1, source_target_pairs={{16,0},{0,16},{17,1},{1,17},{18,2},{2,18},{19,3},{3,19},{20,4},{4,... | collective-permute-start | bytes 3145736 | tf_op jit(solution)/shard_map/ppermute | solution.py:878
  362.2 102.2 %collective-permute-start.9 = (bf16[512,1024]{1,0:T(8,128)(2,1)}, bf16[512,1024]{1,0:T(8,128)(2,1)}, u32[]{:S(2)}, u32[]{:S(2)}) collective-permute-start(bf16[512,1024]{1,0:T(8,128)(2,1)} %get-tuple-element.143), channel_id=1, source_target_pairs={{16,0},{0,16},{17,1},{1,17},{18,2},{2,18},{19,3},{3,19},{20,4},{4,... | collective-permute-start | bytes 3145736 | tf_op jit(solution)/shard_map/ppermute | solution.py:878
  427.4 69.8 %collective-permute-start.11 = (bf16[1024,1024]{1,0:T(8,128)(2,1)}, bf16[1024,1024]{1,0:T(8,128)(2,1)}, u32[]{:S(2)}, u32[]{:S(2)}) collective-permute-start(bf16[1024,1024]{1,0:T(8,128)(2,1)} %unproject.3), channel_id=1, source_target_pairs={{0,16},{16,0},{1,17},{17,1},{2,18},{18,2},{3,19},{19,3},{4,20},{20... | collective-permute-start | bytes 6291464 | tf_op jit(solution)/shard_map/ppermute | solution.py:881
  464.5 23.8 %copy-start.8 = (bf16[1024,1536]{1,0:T(8,128)(2,1)S(1)}, bf16[1024,1536]{1,0:T(8,128)(2,1)}, u32[]{:S(2)}) copy-start(bf16[1024,1536]{1,0:T(8,128)(2,1)} %get-tuple-element.146.refs_7_.grads) | copy-start | bytes 9437188
  493.2 93.3 %collective-permute-start.10 = (bf16[1024,1024]{1,0:T(8,128)(2,1)}, bf16[1024,1024]{1,0:T(8,128)(2,1)}, u32[]{:S(2)}, u32[]{:S(2)}) collective-permute-start(bf16[1024,1024]{1,0:T(8,128)(2,1)} %unproject.2), channel_id=1, source_target_pairs={{0,16},{16,0},{1,17},{17,1},{2,18},{18,2},{3,19},{19,3},{4,20},{20... | collective-permute-start | bytes 6291464 | tf_op jit(solution)/shard_map/ppermute | solution.py:881
  502.3 8.2 %copy-start.12 = (bf16[4,1024,512]{2,1,0:T(8,128)(2,1)S(1)}, bf16[4,1024,512]{2,1,0:T(8,128)(2,1)}, u32[]{:S(2)}) copy-start(bf16[4,1024,512]{2,1,0:T(8,128)(2,1)} %head_grads.1) | copy-start | bytes 12582916
  587.5 20.7 %collective-permute-start.12 = (bf16[128,2048]{1,0:T(8,128)(2,1)S(1)}, bf16[128,2048]{1,0:T(8,128)(2,1)S(1)}, u32[]{:S(2)}, u32[]{:S(2)}) collective-permute-start(bf16[128,2048]{1,0:T(8,128)(2,1)S(1)} %slice.151), channel_id=1, source_target_pairs={{0,16},{16,0},{1,17},{17,1},{2,18},{18,2},{3,19},{19,3},{4,20},{20... | collective-permute-start | bytes 1572872 | tf_op jit(solution)/shard_map/ppermute | solution.py:881
  (38 other events, 130.8 us)
Sparse Core Ops, SparseCore 0:
  24.7 128.3 all-gather.1
  348.0 180.0 reduce-scatter.1
